TPU v7x, 128 devices: a whole 4x4x4 slice. The times are simulated.
128 devices in a mesh: row: 8 (over y_lo, z), col: 16 (over x, y_hi, core).
Axes of the slice: x: 4, y: 4 (y_hi: 2, y_lo: 2; y = y_hi * 2 + y_lo), z: 4, core: 2. Of those that a mesh axis runs over, the one named last changes fastest.
Arguments:
- inputs: bfloat16 [1024, 8192], P('row', 'col'), may hold values from -6 to 6
- gate_matrix: bfloat16 [8192, 26624], P('col', 'row'), may hold values from -0.0625 to 0.0625
- lift_matrix: bfloat16 [8192, 26624], P('col', 'row'), may hold values from -0.0625 to 0.0625
- out_cotangent: bfloat16 [1024, 26624], P('col', 'row'), may hold values from -6 to 6
Outputs:
- gated_out: bfloat16 [1024, 26624], P('col', 'row')
- grad_inputs: bfloat16 [1024, 8192], P('row', 'col')
- grad_gate: bfloat16 [8192, 26624], P('col', 'row')
- grad_lift: bfloat16 [8192, 26624], P('col', 'row')
All inputs are finite; a program needn't handle non-finite values.
Results may differ from a plain program's by a relative error of at most 0.0049.
Values may be sent and summed in bfloat16 or wider, within the bound.
No kernel may reach another device: no remote copies, remote signals or barrier semaphores. Data moves between devices by JAX's collectives and lax.ppermute only.
A program may use at most 192 MiB of HBM per device.

v0:
```python
import jax
import jax.numpy as jnp
from jax import lax
from jax.sharding import PartitionSpec as P


def gate_terms(gate, lift, cotangent):
    sigma = jax.nn.sigmoid(gate)
    silu_val = gate * sigma
    cot = cotangent.astype(jnp.float32)
    gated = (silu_val * lift).astype(jnp.bfloat16)
    grad_gatepre = (cot * lift * sigma * (1.0 + gate * (1.0 - sigma))).astype(jnp.bfloat16)
    grad_liftpre = (cot * silu_val).astype(jnp.bfloat16)
    return (gated, grad_gatepre, grad_liftpre)


def token_contract(left, right):
    return lax.dot_general(
        left, right, (((0,), (0,)), ((), ())), preferred_element_type=jnp.float32
    )


def body(inputs, gate_matrix, lift_matrix, out_cotangent):
    all_tokens = lax.all_gather(inputs, "row", axis=0, tiled=True)
    own_rows = out_cotangent.shape[0]
    part_gate = jnp.dot(all_tokens, gate_matrix, preferred_element_type=jnp.float32)
    part_lift = jnp.dot(all_tokens, lift_matrix, preferred_element_type=jnp.float32)
    gate, lift = lax.psum((part_gate, part_lift), "col")
    full_cot = lax.all_gather(out_cotangent, "col", axis=0, tiled=True)
    gated_all, grad_gatepre, grad_liftpre = gate_terms(gate, lift, full_cot)
    start = lax.axis_index("col") * own_rows
    gated_out = lax.dynamic_slice_in_dim(gated_all, start, own_rows, 0)
    grad_gate = token_contract(all_tokens, grad_gatepre).astype(jnp.bfloat16)
    grad_lift = token_contract(all_tokens, grad_liftpre).astype(jnp.bfloat16)
    total = lax.dot_general(
        grad_gatepre, gate_matrix, (((1,), (1,)), ((), ())), preferred_element_type=jnp.float32
    )
    grad_inputs = lax.psum_scatter(
        total
        + lax.dot_general(
            grad_liftpre, lift_matrix, (((1,), (1,)), ((), ())), preferred_element_type=jnp.float32
        ),
        "row",
        scatter_dimension=0,
        tiled=True,
    ).astype(jnp.bfloat16)
    return (gated_out, grad_inputs, grad_gate, grad_lift)


def solution(mesh):
    return jax.shard_map(
        body,
        mesh=mesh,
        in_specs=(P("row", "col"), P("col", "row"), P("col", "row"), P("col", "row")),
        out_specs=(P("col", "row"), P("row", "col"), P("col", "row"), P("col", "row")),
        check_vma=False,
    )
```

profile of v0, /device:TPU:0, one launch (start us, length us, event | category | flops | bytes accessed | tf_op | source)
XLA Modules:
  0.0 788.2 jit_solution(18045195376431485690)
XLA Ops:
  7.2 0.0 copy-start
  7.2 0.0 all-gather.3.cloned.1.call-start
  7.2 0.7 all-gather.3.cloned.1.call-update
  7.9 0.0 all-gather.5.cloned.1.call-start
  8.0 0.7 all-gather.5.cloned.1.call-update
  8.7 0.0 all-reduce.3.cloned.1.call-start
  8.7 42.6 %all-gather.3.cloned.1.call-done = bf16[1024,512]{1,0:T(8,128)(2,1)} async-done(((bf16[128,512]{1,0:T(8,128)(2,1)}), bf16[1024,512]{1,0:T(8,128)(2,1)}) %all-gather.3.cloned.1.call-update) | async-done | bytes 1048592 | tf_op jit(solution)/shard_map/all_gather | solution.py:24
  51.3 0.0 copy-done
  51.3 8.5 %fusion.12 = f32[1024,3328]{1,0:T(8,128)} fusion(bf16[1024,512]{1,0:T(8,128)(2,1)} %all-gather.3.cloned.1.call-done, bf16[512,3328]{1,0:T(8,128)(2,1)S(1)} %copy-done), kind=kOutput, calls=%fused_computation.15 | convolution fusion | flops 3489660928 | bytes 18087936 | tf_op jit(solution)/shard_map/dot_general | solution.py:26
  59.8 0.0 copy-done.3
  59.8 0.0 copy-done.4
  59.8 6.7 fusion.13
  66.5 0.0 all-reduce.3.cloned.1.call-update
  66.6 0.0 reduce-scatter.2.cloned.1.call-start
  66.6 52.6 %all-gather.5.cloned.1.call-done = bf16[1024,3328]{1,0:T(8,128)(2,1)} async-done(((bf16[64,3328]{1,0:T(8,128)(2,1)}), bf16[1024,3328]{1,0:T(8,128)(2,1)}) %all-gather.5.cloned.1.call-update) | async-done | bytes 6815760 | tf_op jit(solution)/shard_map/all_gather | solution.py:29
  119.2 570.2 %all-reduce.3.cloned.1.call-done = (f32[1024,3328]{1,0:T(8,128)}, f32[1024,3328]{1,0:T(8,128)}) async-done(((f32[1024,3328]{1,0:T(8,128)}, f32[1024,3328]{1,0:T(8,128)}), (f32[1024,3328]{1,0:T(8,128)}, f32[1024,3328]{1,0:T(8,128)})) %all-reduce.3.cloned.1.call-update) | async-done | bytes 27262992 | tf_op jit(solution)/shard_map/psum | solution.py:28
  689.4 20.1 %fusion.2 = (bf16[1024,3328]{1,0:T(8,128)(2,1)S(1)}, f32[1024,3328]{1,0:T(8,128)}) fusion(f32[1024,3328]{1,0:T(8,128)} %get-tuple-element.8, bf16[1024,3328]{1,0:T(8,128)(2,1)} %all-gather.5.cloned.1.call-done, f32[1024,3328]{1,0:T(8,128)} %get-tuple-element.9), kind=kLoop, calls=%fused_computation.4 | loop fusion | flops 40894464 | bytes 54525952 | tf_op jit(solution)/shard_map/convert_element_type | solution.py:12
  709.5 2.9 copy-done.2
  712.4 5.0 fusion.14
  717.4 0.0 slice-done
  717.4 0.0 slice-done.1
  717.4 0.0 slice-done.2
  717.4 0.0 slice-done.3
  717.4 8.5 %convolution_add_fusion = f32[1024,512]{1,0:T(8,128)} fusion(f32[1024,512]{1,0:T(8,128)} %fusion.14, bf16[512,3328]{1,0:T(8,128)(2,1)} %param.6, bf16[1024,3328]{1,0:T(8,128)(2,1)} %all-gather.5.cloned.1.call-done, f32[1024,3328]{1,0:T(8,128)S(1)} %bitcast.15), kind=kOutput, calls=%fused_computation.12 | convolution fusion | flops 3514040320 | bytes 28049408 | tf_op jit(solution)/shard_map/dot_general | solution.py:40
  725.9 0.0 reduce-scatter.2.cloned.1.call-update
  726.0 6.9 fusion.5
  732.9 3.5 copy.8
  736.4 10.9 %fusion.6 = bf16[512,3328]{0,1:T(8,128)(2,1)} fusion(bf16[1024,512]{1,0:T(8,128)(2,1)} %all-gather.3.cloned.1.call-done, bf16[1024,3328]{1,0:T(8,128)(2,1)} %all-gather.5.cloned.1.call-done, f32[1024,3328]{1,0:T(8,128)} %get-tuple-element.9), kind=kOutput, calls=%fused_computation.11 | convolution fusion | flops 3515219968 | bytes 24903680 | tf_op jit(solution)/shard_map/dot_general | solution.py:18
  747.3 5.5 copy.9
  752.8 2.3 fusion.7
  755.1 24.9 %reduce-scatter.2.cloned.1.call-done = f32[128,512]{1,0:T(8,128)} async-done(((f32[1024,512]{1,0:T(8,128)}), f32[128,512]{1,0:T(8,128)}) %reduce-scatter.2.cloned.1.call-update) | async-done | bytes 262160 | tf_op jit(solution)/shard_map/reduce_scatter | solution.py:38
  780.0 1.6 convert_element_type.31
  (10 shorter events, 0.0 us)
Async XLA Ops:
  7.2 44.1 %copy-start = (bf16[512,3328]{1,0:T(8,128)(2,1)S(1)}, bf16[512,3328]{1,0:T(8,128)(2,1)}, u32[]{:S(2)}) copy-start(bf16[512,3328]{1,0:T(8,128)(2,1)} %param.5) | copy-start | bytes 10223620
  7.2 44.1 %all-gather.3.cloned.1.call-start = ((), (), s32[]{:S(2)}) async-start(), calls=%async_computation.1 | async-start | bytes 1179648 | tf_op jit(solution)/shard_map/all_gather | solution.py:24
  7.9 111.3 %all-gather.5.cloned.1.call-start = ((), (), s32[]{:S(2)}) async-start(), calls=%async_computation.2 | async-start | bytes 7241728 | tf_op jit(solution)/shard_map/all_gather | solution.py:29
  8.7 680.7 %all-reduce.3.cloned.1.call-start = ((), (), s32[]{:S(2)}) async-start(), calls=%async_computation.4 | async-start | bytes 54525952 | tf_op jit(solution)/shard_map/psum | solution.py:28
  51.3 8.5 %copy-start.3 = (bf16[512,3328]{1,0:T(8,128)(2,1)S(1)}, bf16[512,3328]{1,0:T(8,128)(2,1)}, u32[]{:S(2)}) copy-start(bf16[512,3328]{1,0:T(8,128)(2,1)} %param.6) | copy-start | bytes 10223620
  51.3 8.5 %copy-start.4 = (bf16[1024,512]{1,0:T(8,128)(2,1)S(1)}, bf16[1024,512]{1,0:T(8,128)(2,1)}, u32[]{:S(2)}) copy-start(bf16[1024,512]{1,0:T(8,128)(2,1)} %all-gather.3.cloned.1.call-done) | copy-start | bytes 3145732
  66.6 713.4 %reduce-scatter.2.cloned.1.call-start = ((), (), s32[]{:S(2)}) async-start(), calls=%async_computation.3 | async-start | bytes 2359296 | tf_op jit(solution)/shard_map/reduce_scatter | solution.py:38
  689.4 28.0 %slice-start = ((s8[13631488]{0:T(1024)(128)(4,1)}), s8[4194304]{0:T(1024)(128)(4,1)S(1)}, s32[]{:S(2)}) async-start(s8[13631488]{0:T(1024)(128)(4,1)} %bitcast.14), calls=%async_computation.5 | async-start | bytes 8388608
  689.4 28.0 %slice-start.1 = ((s8[13631488]{0:T(1024)(128)(4,1)}), s8[4194304]{0:T(1024)(128)(4,1)S(1)}, s32[]{:S(2)}) async-start(s8[13631488]{0:T(1024)(128)(4,1)} %bitcast.14), calls=%async_computation.6 | async-start | bytes 8388608
  689.4 28.0 %slice-start.2 = ((s8[13631488]{0:T(1024)(128)(4,1)}), s8[4194304]{0:T(1024)(128)(4,1)S(1)}, s32[]{:S(2)}) async-start(s8[13631488]{0:T(1024)(128)(4,1)} %bitcast.14), calls=%async_computation.7 | async-start | bytes 8388608
  709.5 2.9 copy-start.2
  712.4 5.0 slice-start.3
  736.4 45.3 %copy-start.1 = (bf16[512,3328]{1,0:T(8,128)(2,1)S(1)}, bf16[512,3328]{1,0:T(8,128)(2,1)}, u32[]{:S(2)}) copy-start(bf16[512,3328]{1,0:T(8,128)(2,1)} %param.5) | copy-start | bytes 10223620
Sparse Core Ops, SparseCore 0:
  9.7 41.6 all-gather.2
  53.7 65.4 all-gather.4
  121.7 567.5 all-reduce.2
  726.1 53.8 reduce-scatter.1
where the time goes:
time: 788 us
  waiting for transfers between devices  692 us (88%)
  matrix products  46.6 us (6%)
  other arithmetic  24 us (3%)
  between operations  13.8 us (2%)
  local copies, waits for them, and re-layouts  11.9 us (2%)
    psum x1, waiting for transfers between devices, body(): gate, lift = lax.psum((part_gate, part_lift), 'col')  570 us
    all_gather x1, waiting for transfers between devices, body(): full_cot = lax.all_gather(out_cotangent, 'col', axis=0, tiled=True)  52.6 us
    all_gather x1, waiting for transfers between devices, body(): all_tokens = lax.all_gather(inputs, 'row', axis=0, tiled=True)  42.6 us
    reduce_scatter x1, waiting for transfers between devices, body(): lax.psum_scatter(total + lax.dot_general(grad_liftpre, lift_matrix, (((1,...  24.9 us
    convert_element_type x1, other arithmetic, gate_terms(): (cot * lift * sigma * (1.0 + gate * (1.0 - sigma))).astype(jnp.bfloat16)  20.1 us
    dot_general x2, matrix products, token_contract(): lax.dot_general(left, right, (((0,), (0,)), ((), ())), preferred_element_...  17.8 us
  transfers between devices with their start and end apart: 4, of which 4 were waited for; matrix products, arithmetic and copies ran while one was open for 6% of the time, Pallas kernels for 0%

commit v1 on v0

v1 whole, which is shorter than its diff:
```python
import functools

import jax
import jax.numpy as jnp
from jax import lax
from jax.experimental import pallas as pl
from jax.experimental.pallas import tpu as pltpu
from jax.sharding import PartitionSpec as P

F32, BF16 = jnp.float32, jnp.bfloat16
TILE = 256
CHUNKS = (("a", 4), ("b", 3), ("a", 3), ("b", 3))
MIB = 1 << 20


def column(x, y, core):
    return (x % 4) * 4 + (y % 2) * 2 + core % 2


COLS = [(c, c // 4, (c // 2) % 2, c % 2) for c in range(16)]
CORE = [(c, column(x, y, k + 1)) for c, x, y, k in COLS]
ALONG_Y = [(c, column(x, y + 1, k)) for c, x, y, k in COLS]
ALONG_X = [(c, column(x + 1 - 2 * k, y, k)) for c, x, y, k in COLS]


def row_step(i):
    return [(r, ((r // 4 + i // 4) % 2) * 4 + (r % 4 + i % 4) % 4) for r in range(8)]


def over_x(v):
    return lax.ppermute(v, "col", ALONG_X)


def over_y(v):
    return lax.ppermute(v, "col", ALONG_Y)


def over_core(v):
    return lax.ppermute(v, "col", CORE)


def params(mib):
    return pltpu.CompilerParams(vmem_limit_bytes=mib * MIB)


def whole(shape):
    return pl.BlockSpec(shape, lambda *_: (0,) * len(shape))


SMEM = pl.BlockSpec(memory_space=pltpu.SMEM)
ANY = pl.BlockSpec(memory_space=pl.ANY)


def cost(flops, bytes_accessed):
    return pl.CostEstimate(flops=flops, bytes_accessed=bytes_accessed, transcendentals=0)


def arrange_kernel(at_ref, own_ref, sib_ref, lhs_ref, xt_ref):
    def piece(ref, i):
        return ref[at_ref[0, i], pl.ds(pl.multiple_of(at_ref[1, i], 64), 64), :]

    for i in range(8):
        lhs_ref[pl.ds(64 * i, 64), :512] = piece(own_ref, i)
        lhs_ref[pl.ds(64 * i, 64), 512:] = piece(sib_ref, i)
    for i in range(8):
        pair = [piece(own_ref, 8 + 2 * i), piece(own_ref, 9 + 2 * i)]
        xt_ref[:, pl.ds(128 * i, 128)] = jnp.concatenate(pair, axis=0).T


def arrange(at, own, sib):
    return pl.pallas_call(
        arrange_kernel,
        out_shape=(jax.ShapeDtypeStruct((512, 1024), BF16), jax.ShapeDtypeStruct((512, 1024), BF16)),
        in_specs=[SMEM, whole(own.shape), whole(own.shape)],
        out_specs=(whole((512, 1024)), whole((512, 1024))),
        grid=(1,),
        compiler_params=params(16),
        cost_estimate=cost(0, 4 * MIB),
        name="arrange_tokens",
    )(at, own, sib)


def forward_kernel(path, lhs_ref, go_ref, gs_ref, lo_ref, ls_ref, *outs):
    a, b = lhs_ref[:, :512], lhs_ref[:, 512:]
    for m, (o, s) in enumerate(((go_ref, gs_ref), (lo_ref, ls_ref))):
        p = jnp.dot(a, o[...], preferred_element_type=F32)
        p = p + jnp.dot(b, s[...], preferred_element_type=F32)
        for g in range(4):
            for dy in range(2):
                q = p[g * 128 + dy * 64 : g * 128 + dy * 64 + 64]
                if path == "a":
                    outs[g][dy, m] = q.astype(outs[g].dtype)
                else:
                    outs[dy][g, m] = q.astype(outs[dy].dtype)


def forward(path, first, tiles, lhs, own_gate, sib_gate, own_lift, sib_lift):
    n = tiles * TILE
    if path == "a":
        lead, kinds = 2, (BF16, BF16, F32, F32)
    else:
        lead, kinds = 4, (F32, BF16)
    w = pl.BlockSpec((512, TILE), lambda j: (0, first + j))
    return pl.pallas_call(
        functools.partial(forward_kernel, path),
        out_shape=tuple(jax.ShapeDtypeStruct((lead, 2, 64, n), t) for t in kinds),
        in_specs=[whole((512, 1024)), w, w, w, w],
        out_specs=tuple(pl.BlockSpec((lead, 2, 64, TILE), lambda j: (0, 0, 0, j)) for _ in kinds),
        grid=(tiles,),
        compiler_params=params(24),
        cost_estimate=cost(4 * 512 * 1024 * n, 4 * 1024 * n + 6 * 1024 * n),
        name="forward_" + path,
    )(lhs, own_gate, sib_gate, own_lift, sib_lift)


def gate_kernel(terms, *refs):
    total = refs[0][...].astype(F32)
    for ref in refs[1:terms]:
        total = total + ref[...].astype(F32)
    cot = refs[terms][...].astype(F32)
    gated_ref, grads_ref = refs[-2:]
    gate, lift = total[0], total[1]
    sigma = jax.nn.sigmoid(gate)
    silu = gate * sigma
    gated_ref[...] = (silu * lift).astype(BF16)
    grads_ref[0] = (cot * lift * sigma * (1.0 + gate * (1.0 - sigma))).astype(BF16)
    grads_ref[1] = (cot * silu).astype(BF16)


def gating(first, tiles, terms, cot, gated):
    n = tiles * TILE
    wide = pl.BlockSpec((64, TILE), lambda j: (0, first + j))
    part = pl.BlockSpec((2, 64, TILE), lambda j: (0, 0, j))
    more, alias = ([], {}) if gated is None else ([gated], {len(terms) + 1: 0})
    return pl.pallas_call(
        functools.partial(gate_kernel, len(terms)),
        out_shape=(jax.ShapeDtypeStruct(cot.shape, BF16), jax.ShapeDtypeStruct((2, 64, n), BF16)),
        in_specs=[part] * len(terms) + [wide] + [ANY] * len(more),
        out_specs=(wide, part),
        grid=(tiles,),
        input_output_aliases=alias,
        compiler_params=params(16),
        cost_estimate=cost(0, 64 * n * 20),
        name="gating",
    )(*terms, cot, *more)


def backward_kernel(path, pieces, do_w, do_y, carried, *refs):
    refs = list(refs)
    held = [refs.pop(0) for _ in range(pieces)]
    if do_w:
        xt_ref = refs.pop(0)
    if do_y:
        w_refs = [refs.pop(0), refs.pop(0)]
        if carried:
            y_in = refs.pop(0)
    outs = refs[-(2 * do_w + do_y):]
    if do_y:
        y_ref = outs[-1]

        @pl.when(pl.program_id(0) == 0)
        def _():
            y_ref[...] = y_in[...] if carried else jnp.zeros_like(y_ref)

    both = []
    for m in range(2):
        rows = []
        for dy in range(2):
            for q in range(8):
                if path == "a":
                    rows.append(held[q][dy, m])
                else:
                    rows.append(held[2 * (q // 4) + dy][q % 4, m])
        both.append(jnp.concatenate(rows, axis=0))
    if do_w:
        for m in range(2):
            outs[m][...] = jnp.dot(xt_ref[...], both[m], preferred_element_type=F32).astype(BF16)
    if do_y:
        dims = (((1,), (1,)), ((), ()))
        add = lax.dot_general(both[0], w_refs[0][...], dims, preferred_element_type=F32)
        add = add + lax.dot_general(both[1], w_refs[1][...], dims, preferred_element_type=F32)
        y_ref[...] += add


def backward(path, first, tiles, pieces, xt, gate, lift, grads, y, do_w, do_y):
    n = tiles * TILE
    lead = pieces[0].shape[0]
    wide = pl.BlockSpec((512, TILE), lambda j: (0, first + j))
    args = list(pieces)
    specs = [pl.BlockSpec((lead, 2, 64, TILE), lambda j: (0, 0, 0, j))] * len(pieces)
    alias, shapes, out_specs = {}, [], []
    if do_w:
        args.append(xt)
        specs.append(whole(xt.shape))
        shapes += [jax.ShapeDtypeStruct(gate.shape, BF16)] * 2
        out_specs += [wide, wide]
    if do_y:
        args += [gate, lift]
        specs += [wide, wide]
        if y is not None:
            alias[len(args)] = len(shapes)
            args.append(y)
            specs.append(whole((1024, 512)))
        shapes.append(jax.ShapeDtypeStruct((1024, 512), F32))
        out_specs.append(whole((1024, 512)))
    if do_w and grads is not None:
        for m in range(2):
            alias[len(args)] = m
            args.append(grads[m])
            specs.append(ANY)
    out = pl.pallas_call(
        functools.partial(backward_kernel, path, len(pieces), do_w, do_y, y is not None),
        out_shape=tuple(shapes),
        in_specs=specs,
        out_specs=tuple(out_specs),
        grid=(tiles,),
        input_output_aliases=alias,
        compiler_params=params(40),
        cost_estimate=cost((do_w + do_y) * 4 * 512 * 1024 * n, 8 * 1024 * n + 4 * MIB),
        name="backward_" + path,
    )(*args)
    return (tuple(out[:2]) if do_w else grads), (out[-1] if do_y else y)


def split_kernel(at_ref, y_ref, own_ref, *outs):
    for i in range(8):
        for h in range(2):
            rows = y_ref[pl.ds(pl.multiple_of(at_ref[i, h], 64), 64), :]
            if i == 0:
                own_ref[pl.ds(64 * h, 64), :] = rows
            else:
                outs[i - 1][pl.ds(64 * h, 64), :] = rows.astype(BF16)


def split(at, y):
    kinds = [F32] + [BF16] * 7
    return pl.pallas_call(
        split_kernel,
        out_shape=tuple(jax.ShapeDtypeStruct((128, 512), t) for t in kinds),
        in_specs=[SMEM, whole((1024, 512))],
        out_specs=tuple(whole((128, 512)) for _ in kinds),
        grid=(1,),
        compiler_params=params(16),
        cost_estimate=cost(0, 3 * MIB),
        name="split_rows",
    )(at, y)


def body(inputs, gate_matrix, lift_matrix, out_cotangent):
    r, c = lax.axis_index("row"), lax.axis_index("col")
    x, yh, k = c // 4, (c // 2) % 2, c % 2
    yl, z = r // 4, r % 4

    sib_gate, sib_lift = over_core(gate_matrix), over_core(lift_matrix)
    blocks = [inputs] + [lax.ppermute(inputs, "row", row_step(i)) for i in range(1, 8)]
    own_x = jnp.stack(blocks)
    sib_x = over_core(own_x)

    def held_at(dx, dy):
        block = 2 * ((x + dx) % 4) + (yh + dy) % 2
        return ((yl - block // 4) % 2) * 4 + (z - block % 4) % 4

    fwd = [(2, k), (1 + 2 * k, 1 - k), (1 + 2 * k, k), (0, k)]
    bwd = [(0, k), (3 - 2 * k, k), (3 - 2 * k, 1 - k), (2, k)]
    bwd += [(0, 1 - k), (1 + 2 * k, 1 - k), (1 + 2 * k, k), (2, 1 - k)]
    order = [(held_at(dx, dy), 64 * h) for dx, h in fwd for dy in range(2)]
    order += [(held_at(dx, dy), 64 * h) for dy in range(2) for dx, h in bwd]
    at = jnp.stack([jnp.stack([i for i, _ in order]), jnp.stack([h for _, h in order])]).astype(jnp.int32)
    lhs, xt = arrange(at, own_x, sib_x)

    gated, grads, y = None, None, None
    first, todo = 0, []
    for path, tiles in CHUNKS:
        products = forward(path, first, tiles, lhs, gate_matrix, sib_gate, lift_matrix, sib_lift)
        if path == "a":
            far, near_o, near_k, own = products
        else:
            keep, send = products
            near = keep + over_y(send).astype(F32)
            far, near_o, near_k, own = near[0].astype(BF16), near[1].astype(BF16), near[2], near[3]
        got_far = over_x(far)
        got_o = over_core(over_x(near_o))
        got_k = over_x((near_k + got_far.astype(F32)).astype(BF16))
        if path == "a":
            total = own + got_k.astype(F32) + got_o.astype(F32)
            terms = [total[0], over_y(total[1].astype(BF16))]
        else:
            terms = [own, got_k, got_o]
        gated, own = gating(first, tiles, terms, out_cotangent, gated)

        if path == "a":
            own = jnp.stack([own, over_y(own)])
        sib = over_core(own)
        near_k = over_x(own)
        near_o = over_x(sib)
        far = over_x(near_k)
        if path == "a":
            pieces = [own, near_k, near_o, far]
            pieces = pieces + [sib] + [over_core(v) for v in pieces[1:]]
        else:
            here = jnp.stack([own, near_k, near_o, far])
            there = over_y(here)
            pieces = [here, there, over_core(here), over_core(there)]
        todo.append((path, first, tiles, pieces))
        first += tiles

    for i, (path, first, tiles, pieces) in enumerate(todo):
        rest = (xt, gate_matrix, lift_matrix)
        if i + 1 < len(todo):
            grads, y = backward(path, first, tiles, pieces, *rest, grads, y, True, True)
        else:
            _, y = backward(path, first, tiles, pieces, *rest, None, y, False, True)
            grads, _ = backward(path, first, tiles, pieces, *rest, grads, None, True, False)

    def place(i, h):
        block = ((yl + i // 4) % 2) * 4 + (z + i % 4) % 4
        dx, dy = (block // 2 - x) % 4, (block - yh) % 2
        same = (h == k).astype(jnp.int32)
        q = jnp.where(dx == 0, 4 - 4 * same, jnp.where(dx == 2, 7 - 4 * same, jnp.where(dx == 3 - 2 * k, 2 - same, 5 + same)))
        return 64 * (8 * dy + q)

    where = jnp.stack([jnp.stack([place(i, h) for h in range(2)]) for i in range(8)]).astype(jnp.int32)
    parts = split(where, y)
    total = parts[0]
    for i in range(1, 8):
        total = total + lax.ppermute(parts[i], "row", row_step(i)).astype(F32)
    return (gated, total.astype(BF16), grads[0], grads[1])


def solution(mesh):
    return jax.shard_map(
        body,
        mesh=mesh,
        in_specs=(P("row", "col"), P("col", "row"), P("col", "row"), P("col", "row")),
        out_specs=(P("col", "row"), P("row", "col"), P("col", "row"), P("col", "row")),
        check_vma=False,
    )
```

time: 788 us -> 243 us (0.31)
  waiting for transfers between devices: 692 us -> 111 us
  starting transfers between devices: 0.16 us -> 56.5 us
  Pallas kernels: 0 us -> 50.9 us
  matrix products: 46.6 us -> 0 us
  other arithmetic: 24 us -> 3.36 us
  between operations: 13.8 us -> 1.42 us
    psum x1 -> x0, waiting for transfers between devices: 570 us -> none  [body(): gate, lift = lax.psum((part_gate, part_lift), 'col')]
    ppermute x0 -> x67, waiting for transfers between devices: none -> 111 us  [the longest x24 43.4 us: over_x(): return lax.ppermute(v, 'col', ALONG_X)]
    all_gather x2 -> x0, waiting for transfers between devices: 95.2 us -> none  [the longest x1 52.6 us: body(): full_cot = lax.all_gather(out_cotangent, 'col', axis=0, tiled=True)]
    ppermute x0 -> x67, starting transfers between devices: none -> 56.5 us  [the longest x8 19.9 us: over_y(): return lax.ppermute(v, 'col', ALONG_Y)]
    pallas_call x0 -> x15, Pallas kernels: none -> 50.9 us  [the longest x5 27.1 us: backward(): pl.pallas_call(functools.partial(backward_kernel, path, len(pieces), do_w...]
    dot_general x6 -> x0, matrix products: 46.6 us -> none  [the longest x2 17.8 us: token_contract(): lax.dot_general(left, right, (((0,), (0,)), ((), ())), preferred_element_...]
    reduce_scatter x1 -> x0, waiting for transfers between devices: 24.9 us -> none  [body(): lax.psum_scatter(total + lax.dot_general(grad_liftpre, lift_matrix, (((1,...]
    convert_element_type x3 -> x5, other arithmetic: 24 us -> 1.08 us  [the longest x1 0.79 us: body(): return (gated, total.astype(BF16), grads[0], grads[1])]
  transfers between devices with their start and end apart: 4 -> 67, of which waited for: 4 -> 27; matrix products, arithmetic and copies ran while one was open for 6% -> 4% of each run, Pallas kernels for 0% -> 18%
where the time goes in v1:
time: 243 us; the launch traced here: 242 us
  waiting for transfers between devices  111 us (46%)
  starting transfers between devices  56.5 us (23%)
  Pallas kernels  50.9 us (21%)
  local copies, waits for them, and re-layouts  19.1 us (8%)
  other arithmetic  3.36 us (1%)
    ppermute x24, waiting for transfers between devices, over_x(): return lax.ppermute(v, 'col', ALONG_X)  43.4 us
    ppermute x8, waiting for transfers between devices, over_y(): return lax.ppermute(v, 'col', ALONG_Y)  34.5 us
    pallas_call x5, Pallas kernels, backward(): pl.pallas_call(functools.partial(backward_kernel, path, len(pieces), do_w...  27.1 us
    ppermute x8, starting transfers between devices, over_y(): return lax.ppermute(v, 'col', ALONG_Y)  19.9 us
    ppermute x7, waiting for transfers between devices, body(): lax.ppermute(inputs, 'row', row_step(i))  19.1 us
    unnamed x55, local copies, waits for them, and re-layouts  18 us
    pallas_call x4, Pallas kernels, forward(): pl.pallas_call(functools.partial(forward_kernel, path), out_shape=tuple((...  15.5 us
    ppermute x24, starting transfers between devices, over_x(): return lax.ppermute(v, 'col', ALONG_X)  14.6 us
  transfers between devices with their start and end apart: 67, of which 27 were waited for; matrix products, arithmetic and copies ran while one was open for 4% of the time, Pallas kernels for 18%

profile of v1, /device:TPU:0, one launch (start us, length us, event | category | flops | bytes accessed | tf_op | source)
XLA Modules:
  0.0 241.9 jit_solution(3262518229524497220)
XLA Ops:
  1.2 3.0 %collective-permute-start.4 = (bf16[128,512]{1,0:T(8,128)(2,1)}, bf16[128,512]{1,0:T(8,128)(2,1)S(1)}, u32[]{:S(2)}, u32[]{:S(2)}) collective-permute-start(bf16[128,512]{1,0:T(8,128)(2,1)} %param.4), channel_id=1, source_target_pairs={{0,80},{16,96},{32,112},{48,64},{64,16},{80,32},{96,48},{112,0},{1... | collective-permute-start | bytes 393224 | tf_op jit(solution)/shard_map/ppermute | solution.py:255
  8.2 4.9 %collective-permute-done = bf16[128,512]{1,0:T(8,128)(2,1)S(1)} collective-permute-done((bf16[128,512]{1,0:T(8,128)(2,1)}, bf16[128,512]{1,0:T(8,128)(2,1)S(1)}, u32[]{:S(2)}, u32[]{:S(2)}) %collective-permute-start) | collective-permute-done | bytes 131104 | tf_op jit(solution)/shard_map/ppermute | solution.py:255
  15.3 5.0 %collective-permute-done.1 = bf16[128,512]{1,0:T(8,128)(2,1)S(1)} collective-permute-done((bf16[128,512]{1,0:T(8,128)(2,1)}, bf16[128,512]{1,0:T(8,128)(2,1)S(1)}, u32[]{:S(2)}, u32[]{:S(2)}) %collective-permute-start.1) | collective-permute-done | bytes 131104 | tf_op jit(solution)/shard_map/ppermute | solution.py:255
  25.4 3.9 %collective-permute-start.6 = (bf16[128,512]{1,0:T(8,128)(2,1)}, bf16[128,512]{1,0:T(8,128)(2,1)S(1)}, u32[]{:S(2)}, u32[]{:S(2)}) collective-permute-start(bf16[128,512]{1,0:T(8,128)(2,1)} %param.4), channel_id=1, source_target_pairs={{0,112},{16,64},{32,80},{48,96},{64,48},{80,0},{96,16},{112,32},{1... | collective-permute-start | bytes 393224 | tf_op jit(solution)/shard_map/ppermute | solution.py:255
  31.3 6.2 %collective-permute-done.5 = bf16[128,512]{1,0:T(8,128)(2,1)S(1)} collective-permute-done((bf16[128,512]{1,0:T(8,128)(2,1)}, bf16[128,512]{1,0:T(8,128)(2,1)S(1)}, u32[]{:S(2)}, u32[]{:S(2)}) %collective-permute-start.5) | collective-permute-done | bytes 131104 | tf_op jit(solution)/shard_map/ppermute | solution.py:255
  46.8 3.7 %forward_a.2 = (bf16[2,2,64,768]{3,2,1,0:T(8,128)(2,1)S(1)}, bf16[2,2,64,768]{3,2,1,0:T(8,128)(2,1)S(1)}, f32[2,2,64,768]{3,2,1,0:T(8,128)S(1)}, f32[2,2,64,768]{3,2,1,0:T(8,128)S(1)}) custom-call(bf16[512,1024]{1,0:T(8,128)(2,1)S(1)} %get-tuple-element.45.lhs_ref, bf16[512,3328]{1,0:T(8,128)(2,1)S(1)} %copy-done, ...), custom_call_target="tpu_custom_call" | custom-call | flops 1610612736 | bytes 7864320 | tf_op jit(solution)/shard_map/forward_a/pallas_call | solution.py:104
  52.0 4.5 %forward_a.3 = (bf16[2,2,64,1024]{3,2,1,0:T(8,128)(2,1)S(1)}, bf16[2,2,64,1024]{3,2,1,0:T(8,128)(2,1)S(1)}, f32[2,2,64,1024]{3,2,1,0:T(8,128)S(1)}, f32[2,2,64,1024]{3,2,1,0:T(8,128)S(1)}) custom-call(bf16[512,1024]{1,0:T(8,128)(2,1)S(1)} %get-tuple-element.45.lhs_ref, bf16[512,3328]{1,0:T(8,128)(2,1)S(1)} %copy-done, ...), custom_call_target="tpu_custom_call" | custom-call | flops 2147483648 | bytes 10485760 | tf_op jit(solution)/shard_map/forward_a/pallas_call | solution.py:104
  58.1 3.6 %forward_b.3 = (f32[4,2,64,768]{3,2,1,0:T(8,128)S(1)}, bf16[4,2,64,768]{3,2,1,0:T(8,128)(2,1)S(1)}) custom-call(bf16[512,1024]{1,0:T(8,128)(2,1)S(1)} %get-tuple-element.45.lhs_ref, bf16[512,3328]{1,0:T(8,128)(2,1)S(1)} %copy-done, bf16[512,3328]{1,0:T(8,128)(2,1)} %collective-permute-done.8.gs_ref, bf16[512,3328]{1,0:T(8,128)(2,1)S(1)} %copy-done.1, ...), custom_call_target="tpu_custom_call" | custom-call | flops 1610612736 | bytes 7864320 | tf_op jit(solution)/shard_map/forward_b/pallas_call | solution.py:104
  61.8 3.0 %collective-permute-start.20 = (bf16[4,2,64,768]{3,2,1,0:T(8,128)(2,1)S(1)}, bf16[4,2,64,768]{3,2,1,0:T(8,128)(2,1)S(1)}, u32[]{:S(2)}, u32[]{:S(2)}) collective-permute-start(bf16[4,2,64,768]{3,2,1,0:T(8,128)(2,1)S(1)} %get-tuple-element.53), channel_id=1, source_target_pairs={{0,2},{1,3},{2,0},{3,1},{4,6},{5,7},{6,4},{7,5},{8,10},{9,11},{10,... | collective-permute-start | bytes 2359304 | tf_op jit(solution)/shard_map/ppermute | solution.py:35
  66.4 3.6 %forward_b.2 = (f32[4,2,64,768]{3,2,1,0:T(8,128)S(1)}, bf16[4,2,64,768]{3,2,1,0:T(8,128)(2,1)S(1)}) custom-call(bf16[512,1024]{1,0:T(8,128)(2,1)S(1)} %get-tuple-element.45.lhs_ref, bf16[512,3328]{1,0:T(8,128)(2,1)S(1)} %copy-done, bf16[512,3328]{1,0:T(8,128)(2,1)} %collective-permute-done.8.gs_ref, bf16[512,3328]{1,0:T(8,128)(2,1)S(1)} %copy-done.1, ...), custom_call_target="tpu_custom_call" | custom-call | flops 1610612736 | bytes 7864320 | tf_op jit(solution)/shard_map/forward_b/pallas_call | solution.py:104
  73.9 5.5 %collective-permute-done.27 = bf16[2,2,64,1024]{3,2,1,0:T(8,128)(2,1)S(1)} collective-permute-done((bf16[2,2,64,1024]{3,2,1,0:T(8,128)(2,1)S(1)}, bf16[2,2,64,1024]{3,2,1,0:T(8,128)(2,1)S(1)}, u32[]{:S(2)}, u32[]{:S(2)}) %collective-permute-start.27) | collective-permute-done | bytes 524320 | tf_op jit(solution)/shard_map/ppermute | solution.py:31
  79.4 4.4 %collective-permute-done.20 = bf16[4,2,64,768]{3,2,1,0:T(8,128)(2,1)S(1)} collective-permute-done((bf16[4,2,64,768]{3,2,1,0:T(8,128)(2,1)S(1)}, bf16[4,2,64,768]{3,2,1,0:T(8,128)(2,1)S(1)}, u32[]{:S(2)}, u32[]{:S(2)}) %collective-permute-start.20) | collective-permute-done | bytes 786464 | tf_op jit(solution)/shard_map/ppermute | solution.py:35
  84.0 15.8 %collective-permute-done.10 = bf16[4,2,64,768]{3,2,1,0:T(8,128)(2,1)S(1)} collective-permute-done((bf16[4,2,64,768]{3,2,1,0:T(8,128)(2,1)S(1)}, bf16[4,2,64,768]{3,2,1,0:T(8,128)(2,1)S(1)}, u32[]{:S(2)}, u32[]{:S(2)}) %collective-permute-start.10) | collective-permute-done | bytes 786464 | tf_op jit(solution)/shard_map/ppermute | solution.py:35
  102.4 6.5 %collective-permute-done.21 = bf16[2,64,768]{2,1,0:T(8,128)(2,1)S(1)} collective-permute-done((bf16[2,64,768]{2,1,0:T(8,128)(2,1)S(1)}, bf16[2,64,768]{2,1,0:T(8,128)(2,1)S(1)}, u32[]{:S(2)}, u32[]{:S(2)}) %collective-permute-start.21) | collective-permute-done | bytes 196640 | tf_op jit(solution)/shard_map/ppermute | solution.py:31
  108.9 3.0 %collective-permute-start.19 = (bf16[2,64,768]{2,1,0:T(8,128)(2,1)S(1)}, bf16[2,64,768]{2,1,0:T(8,128)(2,1)S(1)}, u32[]{:S(2)}, u32[]{:S(2)}) collective-permute-start(bf16[2,64,768]{2,1,0:T(8,128)(2,1)S(1)} %fusion.5), channel_id=1, source_target_pairs={{0,2},{1,3},{2,0},{3,1},{4,6},{5,7},{6,4},{7,5},{8,10},{9,11},{10,... | collective-permute-start | bytes 589832 | tf_op jit(solution)/shard_map/ppermute | solution.py:35
  112.3 3.4 %collective-permute-done.11 = bf16[2,64,768]{2,1,0:T(8,128)(2,1)S(1)} collective-permute-done((bf16[2,64,768]{2,1,0:T(8,128)(2,1)S(1)}, bf16[2,64,768]{2,1,0:T(8,128)(2,1)S(1)}, u32[]{:S(2)}, u32[]{:S(2)}) %collective-permute-start.11) | collective-permute-done | bytes 196640 | tf_op jit(solution)/shard_map/ppermute | solution.py:31
  115.7 2.9 %collective-permute-start.29 = (bf16[2,64,1024]{2,1,0:T(8,128)(2,1)S(1)}, bf16[2,64,1024]{2,1,0:T(8,128)(2,1)S(1)}, u32[]{:S(2)}, u32[]{:S(2)}) collective-permute-start(bf16[2,64,1024]{2,1,0:T(8,128)(2,1)S(1)} %fusion.4), channel_id=1, source_target_pairs={{0,2},{1,3},{2,0},{3,1},{4,6},{5,7},{6,4},{7,5},{8,10},{9,11},{10,... | collective-permute-start | bytes 786440 | tf_op jit(solution)/shard_map/ppermute | solution.py:35
  118.8 4.8 %collective-permute-done.29.refs_1_ = bf16[2,64,1024]{2,1,0:T(8,128)(2,1)S(1)} collective-permute-done((bf16[2,64,1024]{2,1,0:T(8,128)(2,1)S(1)}, bf16[2,64,1024]{2,1,0:T(8,128)(2,1)S(1)}, u32[]{:S(2)}, u32[]{:S(2)}) %collective-permute-start.29) | collective-permute-done | bytes 262176 | tf_op jit(solution)/shard_map/ppermute | solution.py:35
  127.8 2.9 %collective-permute-start.37 = (bf16[2,64,768]{2,1,0:T(8,128)(2,1)S(1)}, bf16[2,64,768]{2,1,0:T(8,128)(2,1)S(1)}, u32[]{:S(2)}, u32[]{:S(2)}) collective-permute-start(bf16[2,64,768]{2,1,0:T(8,128)(2,1)S(1)} %get-tuple-element.63), channel_id=1, source_target_pairs={{0,2},{1,3},{2,0},{3,1},{4,6},{5,7},{6,4},{7,5},{8,10},{9,11},{10,... | collective-permute-start | bytes 589832 | tf_op jit(solution)/shard_map/ppermute | solution.py:35
  137.2 3.2 %collective-permute-start.47 = (bf16[2,64,768]{2,1,0:T(8,128)(2,1)S(1)}, bf16[2,64,768]{2,1,0:T(8,128)(2,1)S(1)}, u32[]{:S(2)}, u32[]{:S(2)}) collective-permute-start(bf16[2,64,768]{2,1,0:T(8,128)(2,1)S(1)} %collective-permute-done.46), channel_id=1, source_target_pairs={{0,4},{1,13},{2,6},{3,15},{4,8},{5,1},{6,10},{7,3},{8,12},{9,5},{1... | collective-permute-start | bytes 589832 | tf_op jit(solution)/shard_map/ppermute | solution.py:31
  151.9 3.0 %collective-permute-start.49 = (bf16[4,2,64,768]{3,2,1,0:T(8,128)(2,1)S(1)}, bf16[4,2,64,768]{3,2,1,0:T(8,128)(2,1)}, u32[]{:S(2)}, u32[]{:S(2)}) collective-permute-start(bf16[4,2,64,768]{3,2,1,0:T(8,128)(2,1)S(1)} %pad_maximum_fusion.1.refs_0_), channel_id=1, source_target_pairs={{0,2},{1,3},{2,0},{3,1},{4,6},{5,7},{6,4},{7,5},{8,10},{9,11},{10,... | collective-permute-start | bytes 2359304 | tf_op jit(solution)/shard_map/ppermute | solution.py:35
  157.5 4.3 %collective-permute-done.53.refs_1_ = bf16[2,2,64,1024]{3,2,1,0:T(8,128)(2,1)} collective-permute-done((bf16[2,2,64,1024]{3,2,1,0:T(8,128)(2,1)S(1)}, bf16[2,2,64,1024]{3,2,1,0:T(8,128)(2,1)}, u32[]{:S(2)}, u32[]{:S(2)}) %collective-permute-start.53) | collective-permute-done | bytes 524320 | tf_op jit(solution)/shard_map/ppermute | solution.py:31
  170.2 3.0 %collective-permute-start.34 = (bf16[4,2,64,768]{3,2,1,0:T(8,128)(2,1)}, bf16[4,2,64,768]{3,2,1,0:T(8,128)(2,1)}, u32[]{:S(2)}, u32[]{:S(2)}) collective-permute-start(bf16[4,2,64,768]{3,2,1,0:T(8,128)(2,1)} %pad_maximum_fusion.refs_0_), channel_id=1, source_target_pairs={{0,2},{1,3},{2,0},{3,1},{4,6},{5,7},{6,4},{7,5},{8,10},{9,11},{10,... | collective-permute-start | bytes 2359304 | tf_op jit(solution)/shard_map/ppermute | solution.py:35
  175.9 5.6 %collective-permute-done.56.refs_3_ = bf16[2,2,64,1024]{3,2,1,0:T(8,128)(2,1)} collective-permute-done((bf16[2,2,64,1024]{3,2,1,0:T(8,128)(2,1)}, bf16[2,2,64,1024]{3,2,1,0:T(8,128)(2,1)}, u32[]{:S(2)}, u32[]{:S(2)}) %collective-permute-start.56) | collective-permute-done | bytes 524320 | tf_op jit(solution)/shard_map/ppermute | solution.py:31
  181.9 8.1 %collective-permute-done.34.refs_1_ = bf16[4,2,64,768]{3,2,1,0:T(8,128)(2,1)} collective-permute-done((bf16[4,2,64,768]{3,2,1,0:T(8,128)(2,1)}, bf16[4,2,64,768]{3,2,1,0:T(8,128)(2,1)}, u32[]{:S(2)}, u32[]{:S(2)}) %collective-permute-start.34) | collective-permute-done | bytes 786464 | tf_op jit(solution)/shard_map/ppermute | solution.py:35
  196.4 7.4 %backward_a.2 = (bf16[512,3328]{1,0:T(8,128)(2,1)}, bf16[512,3328]{1,0:T(8,128)(2,1)}, f32[1024,512]{1,0:T(8,128)S(1)}) custom-call(bf16[2,2,64,1024]{3,2,1,0:T(8,128)(2,1)S(1)} %copy-done.13, bf16[2,2,64,1024]{3,2,1,0:T(8,128)(2,1)} %collective-permute-done.53.refs_1_, bf16[2,2,64,1024]{3,2,1,0:T(8,128)(2,1)} %collective-permute-done.55.refs_2_, ...), custom_call_target="tpu_custom_call" | custom-call | flops 4294967296 | bytes 12582912 | tf_op jit(solution)/shard_map/backward_a/pallas_call | solution.py:211
  203.9 6.1 %backward_b.3 = (bf16[512,3328]{1,0:T(8,128)(2,1)}, bf16[512,3328]{1,0:T(8,128)(2,1)}, f32[1024,512]{1,0:T(8,128)S(1)}) custom-call(bf16[4,2,64,768]{3,2,1,0:T(8,128)(2,1)S(1)} %copy-done.7, bf16[4,2,64,768]{3,2,1,0:T(8,128)(2,1)} %collective-permute-done.49.refs_1_, ...), custom_call_target="tpu_custom_call", output_to_operand_aliasing={{2}: (7, {}), {0}: (8, {}), {1}: (9, {})} | custom-call | flops 3221225472 | bytes 10485760 | tf_op jit(solution)/shard_map/backward_b/pallas_call | solution.py:211
  210.0 5.3 %backward_a.3 = (bf16[512,3328]{1,0:T(8,128)(2,1)}, bf16[512,3328]{1,0:T(8,128)(2,1)}, f32[1024,512]{1,0:T(8,128)S(1)}) custom-call(bf16[2,2,64,768]{3,2,1,0:T(8,128)(2,1)S(1)} %copy-done.9, bf16[2,2,64,768]{3,2,1,0:T(8,128)(2,1)S(1)} %copy-done.17, ...), custom_call_target="tpu_custom_call", output_to_operand_aliasing={{2}: (11, {}), {0}: (12, {}), {1}: (13, {})} | custom-call | flops 3221225472 | bytes 10485760 | tf_op jit(solution)/shard_map/backward_a/pallas_call | solution.py:211
  215.3 3.9 %backward_b.4.y_ref = f32[1024,512]{1,0:T(8,128)S(1)} custom-call(bf16[4,2,64,768]{3,2,1,0:T(8,128)(2,1)} %pad_maximum_fusion.refs_0_, bf16[4,2,64,768]{3,2,1,0:T(8,128)(2,1)} %collective-permute-done.34.refs_1_, bf16[4,2,64,768]{3,2,1,0:T(8,128)(2,1)S(1)} %collective-permute-done.35.refs_2_, ...), custom_call_target="tpu_custom_call", output_to_operand_aliasing={{}: (6, {})} | custom-call | flops 1610612736 | bytes 10485760 | tf_op jit(solution)/shard_map/backward_b/pallas_call | solution.py:211
  225.5 7.1 %collective-permute-done.60 = bf16[128,512]{1,0:T(8,128)(2,1)S(1)} collective-permute-done((bf16[128,512]{1,0:T(8,128)(2,1)S(1)}, bf16[128,512]{1,0:T(8,128)(2,1)S(1)}, u32[]{:S(2)}, u32[]{:S(2)}) %collective-permute-start.60) | collective-permute-done | bytes 131104 | tf_op jit(solution)/shard_map/ppermute | solution.py:326
  232.6 4.5 %backward_b.5 = (bf16[512,3328]{1,0:T(8,128)(2,1)}, bf16[512,3328]{1,0:T(8,128)(2,1)}) custom-call(bf16[4,2,64,768]{3,2,1,0:T(8,128)(2,1)} %pad_maximum_fusion.refs_0_, bf16[4,2,64,768]{3,2,1,0:T(8,128)(2,1)} %collective-permute-done.34.refs_1_, ...), custom_call_target="tpu_custom_call", output_to_operand_aliasing={{0}: (5, {}), {1}: (6, {})} | custom-call | flops 1610612736 | bytes 10485760 | tf_op jit(solution)/shard_map/backward_b/pallas_call | solution.py:211
  237.2 3.9 %collective-permute-done.65 = bf16[128,512]{1,0:T(8,128)(2,1)S(1)} collective-permute-done((bf16[128,512]{1,0:T(8,128)(2,1)S(1)}, bf16[128,512]{1,0:T(8,128)(2,1)S(1)}, u32[]{:S(2)}, u32[]{:S(2)}) %collective-permute-start.65) | collective-permute-done | bytes 131104 | tf_op jit(solution)/shard_map/ppermute | solution.py:326
  (202 shorter events, 84.5 us)
Async XLA Ops:
  0.6 44.2 %collective-permute-start.8 = (bf16[512,3328]{1,0:T(8,128)(2,1)}, bf16[512,3328]{1,0:T(8,128)(2,1)}, u32[]{:S(2)}, u32[]{:S(2)}) collective-permute-start(bf16[512,3328]{1,0:T(8,128)(2,1)} %refs_4_.1), channel_id=1, source_target_pairs={{0,1},{1,0},{2,3},{3,2},{4,5},{5,4},{6,7},{7,6},{8,9},{9,8},{10,11... | collective-permute-start | bytes 10223624 | tf_op jit(solution)/shard_map/ppermute | solution.py:39
  0.7 44.1 %collective-permute-start.9 = (bf16[512,3328]{1,0:T(8,128)(2,1)}, bf16[512,3328]{1,0:T(8,128)(2,1)}, u32[]{:S(2)}, u32[]{:S(2)}) collective-permute-start(bf16[512,3328]{1,0:T(8,128)(2,1)} %refs_5_.3), channel_id=1, source_target_pairs={{0,1},{1,0},{2,3},{3,2},{4,5},{5,4},{6,7},{7,6},{8,9},{9,8},{10,11... | collective-permute-start | bytes 10223624 | tf_op jit(solution)/shard_map/ppermute | solution.py:39
  1.2 29.4 %collective-permute-start.4 = (bf16[128,512]{1,0:T(8,128)(2,1)}, bf16[128,512]{1,0:T(8,128)(2,1)S(1)}, u32[]{:S(2)}, u32[]{:S(2)}) collective-permute-start(bf16[128,512]{1,0:T(8,128)(2,1)} %param.4), channel_id=1, source_target_pairs={{0,80},{16,96},{32,112},{48,64},{64,16},{80,32},{96,48},{112,0},{1... | collective-permute-start | bytes 393224 | tf_op jit(solution)/shard_map/ppermute | solution.py:255
  4.2 25.7 %collective-permute-start.3 = (bf16[128,512]{1,0:T(8,128)(2,1)}, bf16[128,512]{1,0:T(8,128)(2,1)S(1)}, u32[]{:S(2)}, u32[]{:S(2)}) collective-permute-start(bf16[128,512]{1,0:T(8,128)(2,1)} %param.4), channel_id=1, source_target_pairs={{0,64},{16,80},{32,96},{48,112},{64,0},{80,16},{96,32},{112,48},{1... | collective-permute-start | bytes 393224 | tf_op jit(solution)/shard_map/ppermute | solution.py:255
  50.5 19.6 %collective-permute-start.15 = (bf16[2,2,64,768]{3,2,1,0:T(8,128)(2,1)S(1)}, bf16[2,2,64,768]{3,2,1,0:T(8,128)(2,1)S(1)}, u32[]{:S(2)}, u32[]{:S(2)}) collective-permute-start(bf16[2,2,64,768]{3,2,1,0:T(8,128)(2,1)S(1)} %get-tuple-element.50), channel_id=1, source_target_pairs={{0,4},{1,13},{2,6},{3,15},{4,8},{5,1},{6,10},{7,3},{8,12},{9,5},{1... | collective-permute-start | bytes 1179656 | tf_op jit(solution)/shard_map/ppermute | solution.py:31
  56.6 17.2 %collective-permute-start.25 = (bf16[2,2,64,1024]{3,2,1,0:T(8,128)(2,1)S(1)}, bf16[2,2,64,1024]{3,2,1,0:T(8,128)(2,1)S(1)}, u32[]{:S(2)}, u32[]{:S(2)}) collective-permute-start(bf16[2,2,64,1024]{3,2,1,0:T(8,128)(2,1)S(1)} %get-tuple-element.56), channel_id=1, source_target_pairs={{0,4},{1,13},{2,6},{3,15},{4,8},{5,1},{6,10},{7,3},{8,12},{9,5},{1... | collective-permute-start | bytes 1572872 | tf_op jit(solution)/shard_map/ppermute | solution.py:31
  61.8 22.0 %collective-permute-start.20 = (bf16[4,2,64,768]{3,2,1,0:T(8,128)(2,1)S(1)}, bf16[4,2,64,768]{3,2,1,0:T(8,128)(2,1)S(1)}, u32[]{:S(2)}, u32[]{:S(2)}) collective-permute-start(bf16[4,2,64,768]{3,2,1,0:T(8,128)(2,1)S(1)} %get-tuple-element.53), channel_id=1, source_target_pairs={{0,2},{1,3},{2,0},{3,1},{4,6},{5,7},{6,4},{7,5},{8,10},{9,11},{10,... | collective-permute-start | bytes 2359304 | tf_op jit(solution)/shard_map/ppermute | solution.py:35
  66.0 13.4 %collective-permute-start.27 = (bf16[2,2,64,1024]{3,2,1,0:T(8,128)(2,1)S(1)}, bf16[2,2,64,1024]{3,2,1,0:T(8,128)(2,1)S(1)}, u32[]{:S(2)}, u32[]{:S(2)}) collective-permute-start(bf16[2,2,64,1024]{3,2,1,0:T(8,128)(2,1)S(1)} %get-tuple-element.57), channel_id=1, source_target_pairs={{0,4},{1,13},{2,6},{3,15},{4,8},{5,1},{6,10},{7,3},{8,12},{9,5},{1... | collective-permute-start | bytes 1572872 | tf_op jit(solution)/shard_map/ppermute | solution.py:31
  70.1 29.7 %collective-permute-start.10 = (bf16[4,2,64,768]{3,2,1,0:T(8,128)(2,1)S(1)}, bf16[4,2,64,768]{3,2,1,0:T(8,128)(2,1)S(1)}, u32[]{:S(2)}, u32[]{:S(2)}) collective-permute-start(bf16[4,2,64,768]{3,2,1,0:T(8,128)(2,1)S(1)} %get-tuple-element.47), channel_id=1, source_target_pairs={{0,2},{1,3},{2,0},{3,1},{4,6},{5,7},{6,4},{7,5},{8,10},{9,11},{10,... | collective-permute-start | bytes 2359304 | tf_op jit(solution)/shard_map/ppermute | solution.py:35
  73.8 27.6 %collective-permute-start.16 = (bf16[2,2,64,768]{3,2,1,0:T(8,128)(2,1)S(1)}, bf16[2,2,64,768]{3,2,1,0:T(8,128)(2,1)S(1)}, u32[]{:S(2)}, u32[]{:S(2)}) collective-permute-start(bf16[2,2,64,768]{3,2,1,0:T(8,128)(2,1)S(1)} %add_convert_fusion.1), channel_id=1, source_target_pairs={{0,4},{1,13},{2,6},{3,15},{4,8},{5,1},{6,10},{7,3},{8,12},{9,5},{1... | collective-permute-start | bytes 1179656 | tf_op jit(solution)/shard_map/ppermute | solution.py:31
  73.8 27.7 %collective-permute-start.18 = (bf16[2,2,64,768]{3,2,1,0:T(8,128)(2,1)S(1)}, bf16[2,2,64,768]{3,2,1,0:T(8,128)(2,1)S(1)}, u32[]{:S(2)}, u32[]{:S(2)}) collective-permute-start(bf16[2,2,64,768]{3,2,1,0:T(8,128)(2,1)S(1)} %collective-permute-done.17), channel_id=1, source_target_pairs={{0,1},{1,0},{2,3},{3,2},{4,5},{5,4},{6,7},{7,6},{8,9},{9,8},{10,11... | collective-permute-start | bytes 1179656 | tf_op jit(solution)/shard_map/ppermute | solution.py:39
  79.4 32.5 %collective-permute-start.26 = (bf16[2,2,64,1024]{3,2,1,0:T(8,128)(2,1)S(1)}, bf16[2,2,64,1024]{3,2,1,0:T(8,128)(2,1)S(1)}, u32[]{:S(2)}, u32[]{:S(2)}) collective-permute-start(bf16[2,2,64,1024]{3,2,1,0:T(8,128)(2,1)S(1)} %add_convert_fusion), channel_id=1, source_target_pairs={{0,4},{1,13},{2,6},{3,15},{4,8},{5,1},{6,10},{7,3},{8,12},{9,5},{1... | collective-permute-start | bytes 1572872 | tf_op jit(solution)/shard_map/ppermute | solution.py:31
  83.8 28.1 %collective-permute-start.28 = (bf16[2,2,64,1024]{3,2,1,0:T(8,128)(2,1)S(1)}, bf16[2,2,64,1024]{3,2,1,0:T(8,128)(2,1)S(1)}, u32[]{:S(2)}, u32[]{:S(2)}) collective-permute-start(bf16[2,2,64,1024]{3,2,1,0:T(8,128)(2,1)S(1)} %collective-permute-done.27), channel_id=1, source_target_pairs={{0,1},{1,0},{2,3},{3,2},{4,5},{5,4},{6,7},{7,6},{8,9},{9,8},{10,11... | collective-permute-start | bytes 1572872 | tf_op jit(solution)/shard_map/ppermute | solution.py:39
  101.5 17.3 %collective-permute-start.13 = (bf16[2,64,768]{2,1,0:T(8,128)(2,1)S(1)}, bf16[2,64,768]{2,1,0:T(8,128)(2,1)S(1)}, u32[]{:S(2)}, u32[]{:S(2)}) collective-permute-start(bf16[2,64,768]{2,1,0:T(8,128)(2,1)S(1)} %get-tuple-element.92), channel_id=1, source_target_pairs={{0,4},{1,13},{2,6},{3,15},{4,8},{5,1},{6,10},{7,3},{8,12},{9,5},{1... | collective-permute-start | bytes 589832 | tf_op jit(solution)/shard_map/ppermute | solution.py:31
  108.9 17.6 %collective-permute-start.19 = (bf16[2,64,768]{2,1,0:T(8,128)(2,1)S(1)}, bf16[2,64,768]{2,1,0:T(8,128)(2,1)S(1)}, u32[]{:S(2)}, u32[]{:S(2)}) collective-permute-start(bf16[2,64,768]{2,1,0:T(8,128)(2,1)S(1)} %fusion.5), channel_id=1, source_target_pairs={{0,2},{1,3},{2,0},{3,1},{4,6},{5,7},{6,4},{7,5},{8,10},{9,11},{10,... | collective-permute-start | bytes 589832 | tf_op jit(solution)/shard_map/ppermute | solution.py:35
  111.9 13.2 %collective-permute-start.22 = (bf16[2,64,768]{2,1,0:T(8,128)(2,1)S(1)}, bf16[2,64,768]{2,1,0:T(8,128)(2,1)S(1)}, u32[]{:S(2)}, u32[]{:S(2)}) collective-permute-start(bf16[2,64,768]{2,1,0:T(8,128)(2,1)S(1)} %fusion.1), channel_id=1, source_target_pairs={{0,4},{1,13},{2,6},{3,15},{4,8},{5,1},{6,10},{7,3},{8,12},{9,5},{1... | collective-permute-start | bytes 589832 | tf_op jit(solution)/shard_map/ppermute | solution.py:31
  151.9 21.2 %collective-permute-start.49 = (bf16[4,2,64,768]{3,2,1,0:T(8,128)(2,1)S(1)}, bf16[4,2,64,768]{3,2,1,0:T(8,128)(2,1)}, u32[]{:S(2)}, u32[]{:S(2)}) collective-permute-start(bf16[4,2,64,768]{3,2,1,0:T(8,128)(2,1)S(1)} %pad_maximum_fusion.1.refs_0_), channel_id=1, source_target_pairs={{0,2},{1,3},{2,0},{3,1},{4,6},{5,7},{6,4},{7,5},{8,10},{9,11},{10,... | collective-permute-start | bytes 2359304 | tf_op jit(solution)/shard_map/ppermute | solution.py:35
  156.1 17.0 %collective-permute-start.50 = (bf16[4,2,64,768]{3,2,1,0:T(8,128)(2,1)S(1)}, bf16[4,2,64,768]{3,2,1,0:T(8,128)(2,1)S(1)}, u32[]{:S(2)}, u32[]{:S(2)}) collective-permute-start(bf16[4,2,64,768]{3,2,1,0:T(8,128)(2,1)S(1)} %pad_maximum_fusion.1.refs_0_), channel_id=1, source_target_pairs={{0,1},{1,0},{2,3},{3,2},{4,5},{5,4},{6,7},{7,6},{8,9},{9,8},{10,11... | collective-permute-start | bytes 2359304 | tf_op jit(solution)/shard_map/ppermute | solution.py:39
  161.9 14.0 %collective-permute-start.55 = (bf16[2,2,64,1024]{3,2,1,0:T(8,128)(2,1)S(1)}, bf16[2,2,64,1024]{3,2,1,0:T(8,128)(2,1)}, u32[]{:S(2)}, u32[]{:S(2)}) collective-permute-start(bf16[2,2,64,1024]{3,2,1,0:T(8,128)(2,1)S(1)} %collective-permute-done.54.refs_4_), channel_id=1, source_target_pairs={{0,4},{1,13},{2,6},{3,15},{4,8},{5,1},{6,10},{7,3},{8,12},{9,5},{1... | collective-permute-start | bytes 1572872 | tf_op jit(solution)/shard_map/ppermute | solution.py:31
  166.7 14.8 %collective-permute-start.56 = (bf16[2,2,64,1024]{3,2,1,0:T(8,128)(2,1)}, bf16[2,2,64,1024]{3,2,1,0:T(8,128)(2,1)}, u32[]{:S(2)}, u32[]{:S(2)}) collective-permute-start(bf16[2,2,64,1024]{3,2,1,0:T(8,128)(2,1)} %collective-permute-done.53.refs_1_), channel_id=1, source_target_pairs={{0,4},{1,13},{2,6},{3,15},{4,8},{5,1},{6,10},{7,3},{8,12},{9,5},{1... | collective-permute-start | bytes 1572872 | tf_op jit(solution)/shard_map/ppermute | solution.py:31
  170.2 19.8 %collective-permute-start.34 = (bf16[4,2,64,768]{3,2,1,0:T(8,128)(2,1)}, bf16[4,2,64,768]{3,2,1,0:T(8,128)(2,1)}, u32[]{:S(2)}, u32[]{:S(2)}) collective-permute-start(bf16[4,2,64,768]{3,2,1,0:T(8,128)(2,1)} %pad_maximum_fusion.refs_0_), channel_id=1, source_target_pairs={{0,2},{1,3},{2,0},{3,1},{4,6},{5,7},{6,4},{7,5},{8,10},{9,11},{10,... | collective-permute-start | bytes 2359304 | tf_op jit(solution)/shard_map/ppermute | solution.py:35
  173.2 17.8 %collective-permute-start.51 = (bf16[4,2,64,768]{3,2,1,0:T(8,128)(2,1)}, bf16[4,2,64,768]{3,2,1,0:T(8,128)(2,1)}, u32[]{:S(2)}, u32[]{:S(2)}) collective-permute-start(bf16[4,2,64,768]{3,2,1,0:T(8,128)(2,1)} %collective-permute-done.49.refs_1_), channel_id=1, source_target_pairs={{0,1},{1,0},{2,3},{3,2},{4,5},{5,4},{6,7},{7,6},{8,9},{9,8},{10,11... | collective-permute-start | bytes 2359304 | tf_op jit(solution)/shard_map/ppermute | solution.py:39
  174.1 15.9 %collective-permute-start.57 = (bf16[2,2,64,1024]{3,2,1,0:T(8,128)(2,1)}, bf16[2,2,64,1024]{3,2,1,0:T(8,128)(2,1)}, u32[]{:S(2)}, u32[]{:S(2)}) collective-permute-start(bf16[2,2,64,1024]{3,2,1,0:T(8,128)(2,1)} %collective-permute-done.53.refs_1_), channel_id=1, source_target_pairs={{0,1},{1,0},{2,3},{3,2},{4,5},{5,4},{6,7},{7,6},{8,9},{9,8},{10,11... | collective-permute-start | bytes 1572872 | tf_op jit(solution)/shard_map/ppermute | solution.py:39
  175.9 14.6 %collective-permute-start.58 = (bf16[2,2,64,1024]{3,2,1,0:T(8,128)(2,1)}, bf16[2,2,64,1024]{3,2,1,0:T(8,128)(2,1)}, u32[]{:S(2)}, u32[]{:S(2)}) collective-permute-start(bf16[2,2,64,1024]{3,2,1,0:T(8,128)(2,1)} %collective-permute-done.55.refs_2_), channel_id=1, source_target_pairs={{0,1},{1,0},{2,3},{3,2},{4,5},{5,4},{6,7},{7,6},{8,9},{9,8},{10,11... | collective-permute-start | bytes 1572872 | tf_op jit(solution)/shard_map/ppermute | solution.py:39
  190.0 25.3 %collective-permute-start.35 = (bf16[4,2,64,768]{3,2,1,0:T(8,128)(2,1)}, bf16[4,2,64,768]{3,2,1,0:T(8,128)(2,1)S(1)}, u32[]{:S(2)}, u32[]{:S(2)}) collective-permute-start(bf16[4,2,64,768]{3,2,1,0:T(8,128)(2,1)} %pad_maximum_fusion.refs_0_), channel_id=1, source_target_pairs={{0,1},{1,0},{2,3},{3,2},{4,5},{5,4},{6,7},{7,6},{8,9},{9,8},{10,11... | collective-permute-start | bytes 2359304 | tf_op jit(solution)/shard_map/ppermute | solution.py:39
  190.0 20.0 %collective-permute-start.42 = (bf16[2,2,64,768]{3,2,1,0:T(8,128)(2,1)}, bf16[2,2,64,768]{3,2,1,0:T(8,128)(2,1)S(1)}, u32[]{:S(2)}, u32[]{:S(2)}) collective-permute-start(bf16[2,2,64,768]{3,2,1,0:T(8,128)(2,1)} %copy-done.16), channel_id=1, source_target_pairs={{0,1},{1,0},{2,3},{3,2},{4,5},{5,4},{6,7},{7,6},{8,9},{9,8},{10,11... | collective-permute-start | bytes 1179656 | tf_op jit(solution)/shard_map/ppermute | solution.py:39
  190.5 19.4 %collective-permute-start.43 = (bf16[2,2,64,768]{3,2,1,0:T(8,128)(2,1)}, bf16[2,2,64,768]{3,2,1,0:T(8,128)(2,1)S(1)}, u32[]{:S(2)}, u32[]{:S(2)}) collective-permute-start(bf16[2,2,64,768]{3,2,1,0:T(8,128)(2,1)} %copy-done.18), channel_id=1, source_target_pairs={{0,1},{1,0},{2,3},{3,2},{4,5},{5,4},{6,7},{7,6},{8,9},{9,8},{10,11... | collective-permute-start | bytes 1179656 | tf_op jit(solution)/shard_map/ppermute | solution.py:39
  190.6 19.4 %collective-permute-start.44 = (bf16[2,2,64,768]{3,2,1,0:T(8,128)(2,1)}, bf16[2,2,64,768]{3,2,1,0:T(8,128)(2,1)S(1)}, u32[]{:S(2)}, u32[]{:S(2)}) collective-permute-start(bf16[2,2,64,768]{3,2,1,0:T(8,128)(2,1)} %copy-done.20), channel_id=1, source_target_pairs={{0,1},{1,0},{2,3},{3,2},{4,5},{5,4},{6,7},{7,6},{8,9},{9,8},{10,11... | collective-permute-start | bytes 1179656 | tf_op jit(solution)/shard_map/ppermute | solution.py:39
  191.0 24.3 %collective-permute-start.36 = (bf16[4,2,64,768]{3,2,1,0:T(8,128)(2,1)}, bf16[4,2,64,768]{3,2,1,0:T(8,128)(2,1)S(1)}, u32[]{:S(2)}, u32[]{:S(2)}) collective-permute-start(bf16[4,2,64,768]{3,2,1,0:T(8,128)(2,1)} %collective-permute-done.34.refs_1_), channel_id=1, source_target_pairs={{0,1},{1,0},{2,3},{3,2},{4,5},{5,4},{6,7},{7,6},{8,9},{9,8},{10,11... | collective-permute-start | bytes 2359304 | tf_op jit(solution)/shard_map/ppermute | solution.py:39
  221.4 15.8 %collective-permute-start.62 = (bf16[128,512]{1,0:T(8,128)(2,1)S(1)}, bf16[128,512]{1,0:T(8,128)(2,1)S(1)}, u32[]{:S(2)}, u32[]{:S(2)}) collective-permute-start(bf16[128,512]{1,0:T(8,128)(2,1)S(1)} %get-tuple-element.77), channel_id=1, source_target_pairs={{0,48},{16,0},{32,16},{48,32},{64,112},{80,64},{96,80},{112,96},{1... | collective-permute-start | bytes 393224 | tf_op jit(solution)/shard_map/ppermute | solution.py:326
  223.2 14.0 %collective-permute-start.63 = (bf16[128,512]{1,0:T(8,128)(2,1)S(1)}, bf16[128,512]{1,0:T(8,128)(2,1)S(1)}, u32[]{:S(2)}, u32[]{:S(2)}) collective-permute-start(bf16[128,512]{1,0:T(8,128)(2,1)S(1)} %get-tuple-element.78), channel_id=1, source_target_pairs={{0,64},{16,80},{32,96},{48,112},{64,0},{80,16},{96,32},{112,48},{1... | collective-permute-start | bytes 393224 | tf_op jit(solution)/shard_map/ppermute | solution.py:326
  223.3 13.9 %collective-permute-start.64 = (bf16[128,512]{1,0:T(8,128)(2,1)S(1)}, bf16[128,512]{1,0:T(8,128)(2,1)S(1)}, u32[]{:S(2)}, u32[]{:S(2)}) collective-permute-start(bf16[128,512]{1,0:T(8,128)(2,1)S(1)} %get-tuple-element.79), channel_id=1, source_target_pairs={{0,80},{16,96},{32,112},{48,64},{64,16},{80,32},{96,48},{112,0},{1... | collective-permute-start | bytes 393224 | tf_op jit(solution)/shard_map/ppermute | solution.py:326
  (59 other events, 483.3 us)

commit v2 on v1

--- a/solution.py
+++ b/solution.py
@@ -9,7 +9,15 @@
 
 F32, BF16 = jnp.float32, jnp.bfloat16
 TILE = 256
-CHUNKS = (("a", 4), ("b", 3), ("a", 3), ("b", 3))
+CHUNKS = (("b", 3), ("a", 4), ("a", 3), ("b", 3))
+ORDER = (
+    (0, "f"), (1, "f"), (3, "f"), (1, "a1"), (0, "b1"), (2, "f"), (1, "ac"), (0, "b2"),
+    (1, "a2"), (2, "a1"), (0, "bc"), (3, "b1"), (0, "g"), (1, "g"), (0, "c1"), (2, "ac"),
+    (3, "b2"), (2, "a2"), (0, "c2"), (1, "b1"), (1, "b2"), (3, "bc"), (2, "g"), (3, "g"),
+    (0, "c3"), (2, "b1"), (3, "c1"), (1, "b3"), (3, "c2"), (1, "b4"), (2, "b2"), (3, "c3"),
+    (0, "c4"), (1, "d"), (1, "K"), (2, "b3"), (0, "d"), (0, "K"), (2, "b4"), (3, "c4"),
+    (2, "d"), (2, "K"), (3, "d"), (3, "Ky"), (3, "Kw"),
+)
 MIB = 1 << 20
 
 
@@ -52,7 +60,7 @@
 
 
 def cost(flops, bytes_accessed):
-    return pl.CostEstimate(flops=flops, bytes_accessed=bytes_accessed, transcendentals=0)
+    return pl.CostEstimate(flops=flops // 1000, bytes_accessed=bytes_accessed // 1000, transcendentals=0)
 
 
 def arrange_kernel(at_ref, own_ref, sib_ref, lhs_ref, xt_ref):
@@ -145,16 +153,16 @@
     )(*terms, cot, *more)
 
 
-def backward_kernel(path, pieces, do_w, do_y, carried, *refs):
+def backward_kernel(arrays, table, do_w, do_y, carried, *refs):
     refs = list(refs)
-    held = [refs.pop(0) for _ in range(pieces)]
+    held = [refs.pop(0) for _ in range(arrays)]
     if do_w:
         xt_ref = refs.pop(0)
     if do_y:
         w_refs = [refs.pop(0), refs.pop(0)]
         if carried:
             y_in = refs.pop(0)
-    outs = refs[-(2 * do_w + do_y):]
+    outs = refs[-(2 * do_w + do_y) :]
     if do_y:
         y_ref = outs[-1]
 
@@ -162,16 +170,7 @@
         def _():
             y_ref[...] = y_in[...] if carried else jnp.zeros_like(y_ref)
 
-    both = []
-    for m in range(2):
-        rows = []
-        for dy in range(2):
-            for q in range(8):
-                if path == "a":
-                    rows.append(held[q][dy, m])
-                else:
-                    rows.append(held[2 * (q // 4) + dy][q % 4, m])
-        both.append(jnp.concatenate(rows, axis=0))
+    both = [jnp.concatenate([held[i][j, m] for i, j in table], axis=0) for m in range(2)]
     if do_w:
         for m in range(2):
             outs[m][...] = jnp.dot(xt_ref[...], both[m], preferred_element_type=F32).astype(BF16)
@@ -182,12 +181,11 @@
         y_ref[...] += add
 
 
-def backward(path, first, tiles, pieces, xt, gate, lift, grads, y, do_w, do_y):
+def backward(first, tiles, pieces, table, xt, gate, lift, grads, y, do_w, do_y):
     n = tiles * TILE
-    lead = pieces[0].shape[0]
     wide = pl.BlockSpec((512, TILE), lambda j: (0, first + j))
     args = list(pieces)
-    specs = [pl.BlockSpec((lead, 2, 64, TILE), lambda j: (0, 0, 0, j))] * len(pieces)
+    specs = [pl.BlockSpec((v.shape[0], 2, 64, TILE), lambda j: (0, 0, 0, j)) for v in pieces]
     alias, shapes, out_specs = {}, [], []
     if do_w:
         args.append(xt)
@@ -198,7 +196,6 @@
         args += [gate, lift]
         specs += [wide, wide]
         if y is not None:
-            alias[len(args)] = len(shapes)
             args.append(y)
             specs.append(whole((1024, 512)))
         shapes.append(jax.ShapeDtypeStruct((1024, 512), F32))
@@ -209,15 +206,15 @@
             args.append(grads[m])
             specs.append(ANY)
     out = pl.pallas_call(
-        functools.partial(backward_kernel, path, len(pieces), do_w, do_y, y is not None),
+        functools.partial(backward_kernel, len(pieces), table, do_w, do_y, y is not None),
         out_shape=tuple(shapes),
         in_specs=specs,
         out_specs=tuple(out_specs),
         grid=(tiles,),
         input_output_aliases=alias,
-        compiler_params=params(40),
+        compiler_params=params(28),
         cost_estimate=cost((do_w + do_y) * 4 * 512 * 1024 * n, 8 * 1024 * n + 4 * MIB),
-        name="backward_" + path,
+        name="backward",
     )(*args)
     return (tuple(out[:2]) if do_w else grads), (out[-1] if do_y else y)
 
@@ -246,77 +243,214 @@
     )(at, y)
 
 
+class Sequence:
+    def __init__(self):
+        self.last = None
+
+    def __call__(self, *values):
+        if self.last is not None:
+            *values, self.last = lax.optimization_barrier((*values, self.last))
+        return values[0] if len(values) == 1 else values
+
+    def done(self, value):
+        self.last = value
+
+
+def x_first(seq, first, tiles, use):
+    s = {}
+    n = tiles * TILE
+
+    def products():
+        s["far"], s["near_o"], s["near_k"], s["own"] = forward("a", first, tiles, seq(use["lhs"]), *use["weights"])
+        seq.done(s["near_k"])
+        s["far"] = over_x(s["far"])
+
+    def relay():
+        far, near_k, near_o = seq(s["far"], s["near_k"], s["near_o"])
+        near = jnp.stack([(near_k + far.astype(F32)).astype(BF16), near_o])
+        seq.done(near)
+        s["near"] = over_x(near)
+
+    def swap():
+        s["near"] = seq(s["near"])
+        other = s["near"][1]
+        seq.done(other)
+        s["other"] = over_core(other)
+
+    def sum_x():
+        near, other, own = seq(s["near"], s["other"], s["own"])
+        total = own + near[0].astype(F32) + other.astype(F32)
+        send = total[1].astype(BF16)
+        seq.done(send)
+        s["own"], s["other"] = total[0], over_y(send)
+
+    def gate():
+        own, other = seq(s["own"], s["other"])
+        use["gated"], s["own"] = gating(first, tiles, [own, other], use["cot"], use["gated"])
+        seq.done(s["own"])
+        s["other"] = over_y(s["own"])
+
+    def spread():
+        own, other = seq(s["own"], s["other"])
+        s["own"] = jnp.stack([own, other])
+        seq.done(s["own"])
+        s["sib"] = over_core(s["own"])
+
+    def spread_x():
+        own, sib = seq(s["own"], s["sib"])
+        s["full"] = jnp.stack([own, sib])
+        seq.done(s["full"])
+        s["near"] = over_x(s["full"])
+
+    def pass_on():
+        s["near"] = seq(s["near"])
+        far = s["near"][0]
+        seq.done(far)
+        s["far"] = over_x(far)
+
+    def swap_near():
+        near, far = seq(s["near"], s["far"])
+        s["held"] = jnp.concatenate([near, far[None]])
+        seq.done(s["held"])
+        s["swapped"] = over_core(s["held"])
+
+    def arrived():
+        s["swapped"] = seq(s["swapped"])
+        seq.done(s["swapped"])
+
+    def pieces():
+        return [s[name].reshape(-1, 2, 64, n) for name in ("full", "held", "swapped")]
+
+    parts = [(0, 0), (1, 0), (1, 1), (1, 2), (0, 1), (2, 0), (2, 1), (2, 2)]
+    table = [(i, 2 * j + dy) for dy in range(2) for i, j in parts]
+    return dict(
+        f=products, a1=relay, ac=swap, a2=sum_x, g=gate, b1=spread, b2=spread_x, b3=pass_on, b4=swap_near, d=arrived,
+        pieces=pieces, table=table,
+    )
+
+
+def y_first(seq, first, tiles, use):
+    s = {}
+
+    def products():
+        s["keep"], send = forward("b", first, tiles, seq(use["lhs"]), *use["weights"])
+        seq.done(s["keep"])
+        s["other"] = over_y(send)
+
+    def sum_y():
+        keep, other = seq(s["keep"], s["other"])
+        total = keep + other.astype(F32)
+        far = total[0].astype(BF16)
+        s["near_o"], s["near_k"], s["own"] = total[1].astype(BF16), total[2], total[3]
+        seq.done(far)
+        s["far"] = over_x(far)
+
+    def relay():
+        far, near_k, near_o = seq(s["far"], s["near_k"], s["near_o"])
+        near = jnp.stack([(near_k + far.astype(F32)).astype(BF16), near_o])
+        seq.done(near)
+        s["near"] = over_x(near)
+
+    def swap():
+        s["near"] = seq(s["near"])
+        other = s["near"][1]
+        seq.done(other)
+        s["other"] = over_core(other)
+
+    def gate():
+        own, near, other = seq(s["own"], s["near"], s["other"])
+        use["gated"], s["own"] = gating(first, tiles, [own, near[0], other], use["cot"], use["gated"])
+        seq.done(s["own"])
+        s["sib"] = over_core(s["own"])
+
+    def spread_x():
+        own, s["sib"] = seq(s["own"], s["sib"])
+        full = jnp.stack([own, s["sib"]])
+        seq.done(full)
+        s["near"] = over_x(full)
+
+    def pass_on():
+        s["near"] = seq(s["near"])
+        far = s["near"][0]
+        seq.done(far)
+        s["far"] = over_x(far)
+
+    def collect():
+        own, near, far = seq(s["own"], s["near"], s["far"])
+        s["here"] = jnp.concatenate([own[None], near, far[None]])
+        seq.done(s["here"])
+        s["there"] = over_y(s["here"])
+
+    def swap_all():
+        here, s["there"] = seq(s["here"], s["there"])
+        both = jnp.concatenate([here[1:], s["there"]])
+        seq.done(both)
+        s["swapped"] = over_core(both)
+
+    def arrived():
+        s["swapped"] = seq(s["swapped"])
+        seq.done(s["swapped"])
+
+    def pieces():
+        return [s["here"], s["there"], s["sib"][None], s["swapped"]]
+
+    table = [(0, q) for q in range(4)] + [(2, 0)] + [(3, q) for q in range(3)]
+    table += [(1, q) for q in range(4)] + [(3, q) for q in range(3, 7)]
+    return dict(
+        f=products, b1=sum_y, b2=relay, bc=swap, g=gate, c1=spread_x, c2=pass_on, c3=collect, c4=swap_all, d=arrived,
+        pieces=pieces, table=table,
+    )
+
+
 def body(inputs, gate_matrix, lift_matrix, out_cotangent):
     r, c = lax.axis_index("row"), lax.axis_index("col")
     x, yh, k = c // 4, (c // 2) % 2, c % 2
-    yl, z = r // 4, r % 4
 
     sib_gate, sib_lift = over_core(gate_matrix), over_core(lift_matrix)
-    blocks = [inputs] + [lax.ppermute(inputs, "row", row_step(i)) for i in range(1, 8)]
-    own_x = jnp.stack(blocks)
+    own_x = lax.all_to_all(jnp.broadcast_to(inputs[None], (8, 128, 512)), "row", 0, 0)
     sib_x = over_core(own_x)
 
-    def held_at(dx, dy):
-        block = 2 * ((x + dx) % 4) + (yh + dy) % 2
-        return ((yl - block // 4) % 2) * 4 + (z - block % 4) % 4
+    def block(dx, dy):
+        return 2 * ((x + dx) % 4) + (yh + dy) % 2
 
     fwd = [(2, k), (1 + 2 * k, 1 - k), (1 + 2 * k, k), (0, k)]
     bwd = [(0, k), (3 - 2 * k, k), (3 - 2 * k, 1 - k), (2, k)]
     bwd += [(0, 1 - k), (1 + 2 * k, 1 - k), (1 + 2 * k, k), (2, 1 - k)]
-    order = [(held_at(dx, dy), 64 * h) for dx, h in fwd for dy in range(2)]
-    order += [(held_at(dx, dy), 64 * h) for dy in range(2) for dx, h in bwd]
+    order = [(block(dx, dy), 64 * h) for dx, h in fwd for dy in range(2)]
+    order += [(block(dx, dy), 64 * h) for dy in range(2) for dx, h in bwd]
     at = jnp.stack([jnp.stack([i for i, _ in order]), jnp.stack([h for _, h in order])]).astype(jnp.int32)
     lhs, xt = arrange(at, own_x, sib_x)
 
-    gated, grads, y = None, None, None
-    first, todo = 0, []
+    weights = (gate_matrix, sib_gate, lift_matrix, sib_lift)
+    use = dict(lhs=lhs, weights=weights, cot=out_cotangent, gated=None)
+    seq = Sequence()
+    first, steps, spans = 0, [], []
     for path, tiles in CHUNKS:
-        products = forward(path, first, tiles, lhs, gate_matrix, sib_gate, lift_matrix, sib_lift)
-        if path == "a":
-            far, near_o, near_k, own = products
+        steps.append((x_first if path == "a" else y_first)(seq, first, tiles, use))
+        spans.append((first, tiles))
+        first += tiles
+
+    grads, y, parts = None, None, None
+    rest = (xt, gate_matrix, lift_matrix)
+    for i, step in ORDER:
+        if step[0] != "K":
+            steps[i][step]()
+            continue
+        if step == "Kw":
+            pieces = steps[i]["pieces"]()
         else:
-            keep, send = products
-            near = keep + over_y(send).astype(F32)
-            far, near_o, near_k, own = near[0].astype(BF16), near[1].astype(BF16), near[2], near[3]
-        got_far = over_x(far)
-        got_o = over_core(over_x(near_o))
-        got_k = over_x((near_k + got_far.astype(F32)).astype(BF16))
-        if path == "a":
-            total = own + got_k.astype(F32) + got_o.astype(F32)
-            terms = [total[0], over_y(total[1].astype(BF16))]
-        else:
-            terms = [own, got_k, got_o]
-        gated, own = gating(first, tiles, terms, out_cotangent, gated)
-
-        if path == "a":
-            own = jnp.stack([own, over_y(own)])
-        sib = over_core(own)
-        near_k = over_x(own)
-        near_o = over_x(sib)
-        far = over_x(near_k)
-        if path == "a":
-            pieces = [own, near_k, near_o, far]
-            pieces = pieces + [sib] + [over_core(v) for v in pieces[1:]]
-        else:
-            here = jnp.stack([own, near_k, near_o, far])
-            there = over_y(here)
-            pieces = [here, there, over_core(here), over_core(there)]
-        todo.append((path, first, tiles, pieces))
-        first += tiles
-
-    for i, (path, first, tiles, pieces) in enumerate(todo):
-        rest = (xt, gate_matrix, lift_matrix)
-        if i + 1 < len(todo):
-            grads, y = backward(path, first, tiles, pieces, *rest, grads, y, True, True)
-        else:
-            _, y = backward(path, first, tiles, pieces, *rest, None, y, False, True)
-            grads, _ = backward(path, first, tiles, pieces, *rest, grads, None, True, False)
+            pieces = seq(*steps[i]["pieces"]())
+        do = (step != "Ky", step != "Kw")
+        grads, y = backward(*spans[i], pieces, steps[i]["table"], *rest, grads, y, *do)
+        if step != "Kw":
+            seq.done(y)
 
     def place(i, h):
-        block = ((yl + i // 4) % 2) * 4 + (z + i % 4) % 4
-        dx, dy = (block // 2 - x) % 4, (block - yh) % 2
+        row = (r // 4 + i // 4) % 2 * 4 + (r % 4 + i % 4) % 4
+        dx, dy = (row // 2 - x) % 4, (row - yh) % 2
         same = (h == k).astype(jnp.int32)
-        q = jnp.where(dx == 0, 4 - 4 * same, jnp.where(dx == 2, 7 - 4 * same, jnp.where(dx == 3 - 2 * k, 2 - same, 5 + same)))
+        near = jnp.where(dx == 3 - 2 * k, 2 - same, 5 + same)
+        q = jnp.where(dx == 0, 4 - 4 * same, jnp.where(dx == 2, 7 - 4 * same, near))
         return 64 * (8 * dy + q)
 
     where = jnp.stack([jnp.stack([place(i, h) for h in range(2)]) for i in range(8)]).astype(jnp.int32)
@@ -324,7 +458,7 @@
     total = parts[0]
     for i in range(1, 8):
         total = total + lax.ppermute(parts[i], "row", row_step(i)).astype(F32)
-    return (gated, total.astype(BF16), grads[0], grads[1])
+    return (seq(use["gated"]), total.astype(BF16), grads[0], grads[1])
 
 
 def solution(mesh):

time: 243 us -> 213 us (0.88)
  starting transfers between devices: 56.5 us -> 32 us
  blocking collectives: 0 us -> 22.6 us
  waiting for transfers between devices: 111 us -> 90.5 us
  local copies, waits for them, and re-layouts: 19.1 us -> 10.5 us
    all_to_all x0 -> x1, blocking collectives: none -> 22.6 us  [body(): lax.all_to_all(jnp.broadcast_to(inputs[None], (8, 128, 512)), 'row', 0, 0)]
    ppermute x7 -> x0, waiting for transfers between devices: 19.1 us -> none  [body(): lax.ppermute(inputs, 'row', row_step(i))]
    ppermute x8, waiting for transfers between devices: 34.5 us -> 18.6 us  [over_y(): return lax.ppermute(v, 'col', ALONG_Y)]
    ppermute x7 -> x0, starting transfers between devices: 12.3 us -> none  [body(): lax.ppermute(inputs, 'row', row_step(i))]
    ppermute x21 -> x15, waiting for transfers between devices: 2.58 us -> 12.8 us  [over_core(): return lax.ppermute(v, 'col', CORE)]
    unnamed x55 -> x34, local copies, waits for them, and re-layouts: 18 us -> 8.69 us
    ppermute x24 -> x16, starting transfers between devices: 14.6 us -> 6.93 us  [over_x(): return lax.ppermute(v, 'col', ALONG_X)]
    ppermute x24 -> x16, waiting for transfers between devices: 43.4 us -> 49.4 us  [over_x(): return lax.ppermute(v, 'col', ALONG_X)]
  transfers between devices with their start and end apart: 67 -> 46, of which waited for: 27 -> 25; matrix products, arithmetic and copies ran while one was open for 4% -> 2% of each run, Pallas kernels for 18% -> 17%
where the time goes in v2:
time: 213 us; the launch traced here: 212 us
  waiting for transfers between devices  90.5 us (42%)
  Pallas kernels  49.7 us (23%)
  starting transfers between devices  32 us (15%)
  blocking collectives  22.6 us (11%)
  local copies, waits for them, and re-layouts  10.5 us (5%)
  other arithmetic  5.66 us (3%)
    ppermute x16, waiting for transfers between devices, over_x(): return lax.ppermute(v, 'col', ALONG_X)  49.4 us
    pallas_call x5, Pallas kernels, backward(): pl.pallas_call(functools.partial(backward_kernel, len(pieces), table, do_...  25.9 us
    all_to_all x1, blocking collectives, body(): lax.all_to_all(jnp.broadcast_to(inputs[None], (8, 128, 512)), 'row', 0, 0)  22.6 us
    ppermute x8, waiting for transfers between devices, over_y(): return lax.ppermute(v, 'col', ALONG_Y)  18.6 us
    ppermute x8, starting transfers between devices, over_y(): return lax.ppermute(v, 'col', ALONG_Y)  16.8 us
    pallas_call x4, Pallas kernels, forward(): pl.pallas_call(functools.partial(forward_kernel, path), out_shape=tuple((...  15.5 us
    ppermute x15, waiting for transfers between devices, over_core(): return lax.ppermute(v, 'col', CORE)  12.8 us
    ppermute x7, waiting for transfers between devices, body(): total = total + lax.ppermute(parts[i], 'row', row_step(i)).astype(F32)  9.67 us
  transfers between devices with their start and end apart: 46, of which 25 were waited for; matrix products, arithmetic and copies ran while one was open for 2% of the time, Pallas kernels for 17%

profile of v2, /device:TPU:0, one launch (start us, length us, event | category | flops | bytes accessed | tf_op | source)
XLA Modules:
  0.0 212.5 jit_solution(4540941490564461239)
XLA Ops:
  2.2 22.6 %all_to_all.5.own_ref = bf16[8,128,512]{2,1,0:T(8,128)(2,1)} all-to-all(bf16[8,128,512]{2,1,0:T(8,128)(2,1)S(1)} %broadcast_in_dim.27), channel_id=1, replica_groups=mesh['row'=8,'col'=16] {'row'}, dimensions={0} | all-to-all | bytes 2097152 | tf_op jit(solution)/shard_map/all_to_all | solution.py:410
  25.0 2.8 %collective-permute-done.sib_ref = bf16[8,128,512]{2,1,0:T(8,128)(2,1)} collective-permute-done((bf16[8,128,512]{2,1,0:T(8,128)(2,1)}, bf16[8,128,512]{2,1,0:T(8,128)(2,1)}, u32[]{:S(2)}, u32[]{:S(2)}) %collective-permute-start) | collective-permute-done | bytes 1048608 | tf_op jit(solution)/shard_map/ppermute | solution.py:47
  32.1 3.6 %forward_b.2 = (f32[4,2,64,768]{3,2,1,0:T(8,128)S(1)}, bf16[4,2,64,768]{3,2,1,0:T(8,128)(2,1)S(1)}) custom-call(bf16[512,1024]{1,0:T(8,128)(2,1)S(1)} %get-tuple-element.148.lhs_ref, bf16[512,3328]{1,0:T(8,128)(2,1)S(1)} %copy-done, bf16[512,3328]{1,0:T(8,128)(2,1)} %collective-permute-done.1.gs_ref, bf16[512,3328]{1,0:T(8,128)(2,1)S(1)} %copy-done.1, ...), custom_call_target="tpu_custom_call" | custom-call | flops 1610612 | bytes 7864 | tf_op jit(solution)/shard_map/forward_b/pallas_call | solution.py:112
  35.8 4.6 %forward_a.2 = (bf16[2,2,64,1024]{3,2,1,0:T(8,128)(2,1)S(1)}, bf16[2,2,64,1024]{3,2,1,0:T(8,128)(2,1)S(1)}, f32[2,2,64,1024]{3,2,1,0:T(8,128)S(1)}, f32[2,2,64,1024]{3,2,1,0:T(8,128)S(1)}) custom-call(bf16[512,1024]{1,0:T(8,128)(2,1)S(1)} %get-tuple-element.148.lhs_ref, bf16[512,3328]{1,0:T(8,128)(2,1)S(1)} %copy-done, ...), custom_call_target="tpu_custom_call" | custom-call | flops 2147483 | bytes 10485 | tf_op jit(solution)/shard_map/forward_a/pallas_call | solution.py:112
  41.9 2.9 %collective-permute-start.4 = (bf16[4,2,64,768]{3,2,1,0:T(8,128)(2,1)S(1)}, bf16[4,2,64,768]{3,2,1,0:T(8,128)(2,1)S(1)}, u32[]{:S(2)}, u32[]{:S(2)}) collective-permute-start(bf16[4,2,64,768]{3,2,1,0:T(8,128)(2,1)S(1)} %get-tuple-element.140), channel_id=1, source_target_pairs={{0,2},{1,3},{2,0},{3,1},{4,6},{5,7},{6,4},{7,5},{8,10},{9,11},{10,... | collective-permute-start | bytes 2359304 | tf_op jit(solution)/shard_map/ppermute | solution.py:43
  44.8 3.6 %forward_b.3 = (f32[4,2,64,768]{3,2,1,0:T(8,128)S(1)}, bf16[4,2,64,768]{3,2,1,0:T(8,128)(2,1)S(1)}) custom-call(bf16[512,1024]{1,0:T(8,128)(2,1)S(1)} %get-tuple-element.148.lhs_ref, bf16[512,3328]{1,0:T(8,128)(2,1)S(1)} %copy-done, bf16[512,3328]{1,0:T(8,128)(2,1)} %collective-permute-done.1.gs_ref, bf16[512,3328]{1,0:T(8,128)(2,1)S(1)} %copy-done.1, ...), custom_call_target="tpu_custom_call" | custom-call | flops 1610612 | bytes 7864 | tf_op jit(solution)/shard_map/forward_b/pallas_call | solution.py:112
  48.5 2.3 %collective-permute-done.5 = bf16[2,2,64,1024]{3,2,1,0:T(8,128)(2,1)S(1)} collective-permute-done((bf16[2,2,64,1024]{3,2,1,0:T(8,128)(2,1)S(1)}, bf16[2,2,64,1024]{3,2,1,0:T(8,128)(2,1)S(1)}, u32[]{:S(2)}, u32[]{:S(2)}) %collective-permute-start.5) | collective-permute-done | bytes 524320 | tf_op jit(solution)/shard_map/ppermute | solution.py:39
  51.4 2.9 %collective-permute-start.3 = (bf16[4,2,64,768]{3,2,1,0:T(8,128)(2,1)S(1)}, bf16[4,2,64,768]{3,2,1,0:T(8,128)(2,1)S(1)}, u32[]{:S(2)}, u32[]{:S(2)}) collective-permute-start(bf16[4,2,64,768]{3,2,1,0:T(8,128)(2,1)S(1)} %get-tuple-element.139), channel_id=1, source_target_pairs={{0,2},{1,3},{2,0},{3,1},{4,6},{5,7},{6,4},{7,5},{8,10},{9,11},{10,... | collective-permute-start | bytes 2359304 | tf_op jit(solution)/shard_map/ppermute | solution.py:43
  54.3 9.4 %collective-permute-done.4 = bf16[4,2,64,768]{3,2,1,0:T(8,128)(2,1)S(1)} collective-permute-done((bf16[4,2,64,768]{3,2,1,0:T(8,128)(2,1)S(1)}, bf16[4,2,64,768]{3,2,1,0:T(8,128)(2,1)S(1)}, u32[]{:S(2)}, u32[]{:S(2)}) %collective-permute-start.4) | collective-permute-done | bytes 786464 | tf_op jit(solution)/shard_map/ppermute | solution.py:43
  65.7 3.7 %forward_a.3 = (bf16[2,2,64,768]{3,2,1,0:T(8,128)(2,1)S(1)}, bf16[2,2,64,768]{3,2,1,0:T(8,128)(2,1)S(1)}, f32[2,2,64,768]{3,2,1,0:T(8,128)S(1)}, f32[2,2,64,768]{3,2,1,0:T(8,128)S(1)}) custom-call(bf16[512,1024]{1,0:T(8,128)(2,1)S(1)} %get-tuple-element.148.lhs_ref, bf16[512,3328]{1,0:T(8,128)(2,1)S(1)} %copy-done, ...), custom_call_target="tpu_custom_call" | custom-call | flops 1610612 | bytes 7864 | tf_op jit(solution)/shard_map/forward_a/pallas_call | solution.py:112
  73.0 3.0 %collective-permute-start.15 = (bf16[2,64,1024]{2,1,0:T(8,128)(2,1)S(1)}, bf16[2,64,1024]{2,1,0:T(8,128)(2,1)S(1)}, u32[]{:S(2)}, u32[]{:S(2)}) collective-permute-start(bf16[2,64,1024]{2,1,0:T(8,128)(2,1)S(1)} %fusion.4), channel_id=1, source_target_pairs={{0,2},{1,3},{2,0},{3,1},{4,6},{5,7},{6,4},{7,5},{8,10},{9,11},{10,... | collective-permute-start | bytes 786440 | tf_op jit(solution)/shard_map/ppermute | solution.py:43
  76.0 2.5 %collective-permute-done.9 = bf16[2,2,64,768]{3,2,1,0:T(8,128)(2,1)S(1)} collective-permute-done((bf16[2,2,64,768]{3,2,1,0:T(8,128)(2,1)S(1)}, bf16[2,2,64,768]{3,2,1,0:T(8,128)(2,1)S(1)}, u32[]{:S(2)}, u32[]{:S(2)}) %collective-permute-start.9) | collective-permute-done | bytes 393248 | tf_op jit(solution)/shard_map/ppermute | solution.py:39
  78.7 4.0 %collective-permute-done.8 = bf16[2,2,64,768]{3,2,1,0:T(8,128)(2,1)S(1)} collective-permute-done((bf16[2,2,64,768]{3,2,1,0:T(8,128)(2,1)S(1)}, bf16[2,2,64,768]{3,2,1,0:T(8,128)(2,1)S(1)}, u32[]{:S(2)}, u32[]{:S(2)}) %collective-permute-start.8) | collective-permute-done | bytes 393248 | tf_op jit(solution)/shard_map/ppermute | solution.py:39
  87.6 4.2 %collective-permute-done.12 = bf16[2,2,2,64,768]{4,3,2,1,0:T(8,128)(2,1)S(1)} collective-permute-done((bf16[2,2,2,64,768]{4,3,2,1,0:T(8,128)(2,1)S(1)}, bf16[2,2,2,64,768]{4,3,2,1,0:T(8,128)(2,1)S(1)}, u32[]{:S(2)}, u32[]{:S(2)}) %collective-permute-start.12) | collective-permute-done | bytes 786464 | tf_op jit(solution)/shard_map/ppermute | solution.py:39
  92.1 3.0 %collective-permute-start.17 = (bf16[2,64,1024]{2,1,0:T(8,128)(2,1)S(1)}, bf16[2,64,1024]{2,1,0:T(8,128)(2,1)S(1)}, u32[]{:S(2)}, u32[]{:S(2)}) collective-permute-start(bf16[2,64,1024]{2,1,0:T(8,128)(2,1)S(1)} %get-tuple-element.185), channel_id=1, source_target_pairs={{0,2},{1,3},{2,0},{3,1},{4,6},{5,7},{6,4},{7,5},{8,10},{9,11},{10,... | collective-permute-start | bytes 786440 | tf_op jit(solution)/shard_map/ppermute | solution.py:43
  95.3 8.7 %collective-permute-done.18 = bf16[2,2,64,768]{3,2,1,0:T(8,128)(2,1)S(1)} collective-permute-done((bf16[2,2,64,768]{3,2,1,0:T(8,128)(2,1)S(1)}, bf16[2,2,64,768]{3,2,1,0:T(8,128)(2,1)S(1)}, u32[]{:S(2)}, u32[]{:S(2)}) %collective-permute-start.18) | collective-permute-done | bytes 393248 | tf_op jit(solution)/shard_map/ppermute | solution.py:39
  106.8 6.7 %collective-permute-done.16 = bf16[2,2,64,768]{3,2,1,0:T(8,128)(2,1)S(1)} collective-permute-done((bf16[2,2,64,768]{3,2,1,0:T(8,128)(2,1)S(1)}, bf16[2,2,64,768]{3,2,1,0:T(8,128)(2,1)S(1)}, u32[]{:S(2)}, u32[]{:S(2)}) %collective-permute-start.16) | collective-permute-done | bytes 393248 | tf_op jit(solution)/shard_map/ppermute | solution.py:39
  117.9 5.9 %collective-permute-done.24 = bf16[2,64,768]{2,1,0:T(8,128)(2,1)S(1)} collective-permute-done((bf16[2,64,768]{2,1,0:T(8,128)(2,1)S(1)}, bf16[2,64,768]{2,1,0:T(8,128)(2,1)S(1)}, u32[]{:S(2)}, u32[]{:S(2)}) %collective-permute-start.24) | collective-permute-done | bytes 196640 | tf_op jit(solution)/shard_map/ppermute | solution.py:43
  124.0 2.8 %collective-permute-done.27 = bf16[2,2,2,64,1024]{4,3,2,1,0:T(8,128)(2,1)S(1)} collective-permute-done((bf16[2,2,2,64,1024]{4,3,2,1,0:T(8,128)(2,1)S(1)}, bf16[2,2,2,64,1024]{4,3,2,1,0:T(8,128)(2,1)S(1)}, u32[]{:S(2)}, u32[]{:S(2)}) %collective-permute-start.27) | collective-permute-done | bytes 1048608 | tf_op jit(solution)/shard_map/ppermute | solution.py:39
  128.2 4.8 %collective-permute-done.26 = bf16[2,2,64,768]{3,2,1,0:T(8,128)(2,1)S(1)} collective-permute-done((bf16[2,2,64,768]{3,2,1,0:T(8,128)(2,1)S(1)}, bf16[2,2,64,768]{3,2,1,0:T(8,128)(2,1)S(1)}, u32[]{:S(2)}, u32[]{:S(2)}) %collective-permute-start.26) | collective-permute-done | bytes 393248 | tf_op jit(solution)/shard_map/ppermute | solution.py:39
  133.0 5.6 %collective-permute-done.30 = bf16[2,2,64,1024]{3,2,1,0:T(8,128)(2,1)S(1)} collective-permute-done((bf16[2,2,64,1024]{3,2,1,0:T(8,128)(2,1)S(1)}, bf16[2,2,64,1024]{3,2,1,0:T(8,128)(2,1)S(1)}, u32[]{:S(2)}, u32[]{:S(2)}) %collective-permute-start.30) | collective-permute-done | bytes 524320 | tf_op jit(solution)/shard_map/ppermute | solution.py:39
  139.3 3.5 %collective-permute-done.29 = bf16[2,2,64,768]{3,2,1,0:T(8,128)(2,1)S(1)} collective-permute-done((bf16[2,2,64,768]{3,2,1,0:T(8,128)(2,1)S(1)}, bf16[2,2,64,768]{3,2,1,0:T(8,128)(2,1)S(1)}, u32[]{:S(2)}, u32[]{:S(2)}) %collective-permute-start.29) | collective-permute-done | bytes 393248 | tf_op jit(solution)/shard_map/ppermute | solution.py:47
  142.9 3.2 %collective-permute-done.28 = bf16[2,64,768]{2,1,0:T(8,128)(2,1)S(1)} collective-permute-done((bf16[2,64,768]{2,1,0:T(8,128)(2,1)S(1)}, bf16[2,64,768]{2,1,0:T(8,128)(2,1)S(1)}, u32[]{:S(2)}, u32[]{:S(2)}) %collective-permute-start.28) | collective-permute-done | bytes 196640 | tf_op jit(solution)/shard_map/ppermute | solution.py:39
  148.9 6.6 %backward.5 = (bf16[512,3328]{1,0:T(8,128)(2,1)}, bf16[512,3328]{1,0:T(8,128)(2,1)}, f32[1024,512]{1,0:T(8,128)S(1)}) custom-call(bf16[4,2,64,1024]{3,2,1,0:T(8,128)(2,1)S(1)} %bitcast.131, bf16[6,2,64,1024]{3,2,1,0:T(8,128)(2,1)S(1)} %bitcast.130, bf16[6,2,64,1024]{3,2,1,0:T(8,128)(2,1)S(1)} %bitcast.136, ...), custom_call_target="tpu_custom_call" | custom-call | flops 4294967 | bytes 12582 | tf_op jit(solution)/shard_map/backward/pallas_call | solution.py:208
  156.3 5.0 %backward.6 = (bf16[512,3328]{1,0:T(8,128)(2,1)}, bf16[512,3328]{1,0:T(8,128)(2,1)}, f32[1024,512]{1,0:T(8,128)S(1)}) custom-call(bf16[4,2,64,768]{3,2,1,0:T(8,128)(2,1)S(1)} %pad_maximum_fusion.7.refs_0_, bf16[4,2,64,768]{3,2,1,0:T(8,128)(2,1)S(1)} %collective-permute-done.34.refs_1_, ...), custom_call_target="tpu_custom_call", output_to_operand_aliasing={{0}: (8, {}), {1}: (9, {})} | custom-call | flops 3221225 | bytes 10485 | tf_op jit(solution)/shard_map/backward/pallas_call | solution.py:208
  161.3 3.9 %collective-permute-done.35 = bf16[2,2,64,768]{3,2,1,0:T(8,128)(2,1)S(1)} collective-permute-done((bf16[2,2,64,768]{3,2,1,0:T(8,128)(2,1)S(1)}, bf16[2,2,64,768]{3,2,1,0:T(8,128)(2,1)S(1)}, u32[]{:S(2)}, u32[]{:S(2)}) %collective-permute-start.35) | collective-permute-done | bytes 393248 | tf_op jit(solution)/shard_map/ppermute | solution.py:39
  171.2 4.0 %collective-permute-done.38 = bf16[3,2,2,64,768]{4,3,2,1,0:T(8,128)(2,1)} collective-permute-done((bf16[3,2,2,64,768]{4,3,2,1,0:T(8,128)(2,1)}, bf16[3,2,2,64,768]{4,3,2,1,0:T(8,128)(2,1)}, u32[]{:S(2)}, u32[]{:S(2)}) %collective-permute-start.38) | collective-permute-done | bytes 1179680 | tf_op jit(solution)/shard_map/ppermute | solution.py:47
  181.1 5.9 %backward.7 = (bf16[512,3328]{1,0:T(8,128)(2,1)}, bf16[512,3328]{1,0:T(8,128)(2,1)}, f32[1024,512]{1,0:T(8,128)S(1)}) custom-call(bf16[4,2,64,768]{3,2,1,0:T(8,128)(2,1)S(1)} %bitcast.132, bf16[6,2,64,768]{3,2,1,0:T(8,128)(2,1)} %bitcast.66.refs_1_, bf16[6,2,64,768]{3,2,1,0:T(8,128)(2,1)} %bitcast.67.refs_2_, ...), custom_call_target="tpu_custom_call", output_to_operand_aliasing={{0}: (7, {}), {1}: (8, {})} | custom-call | flops 3221225 | bytes 10485 | tf_op jit(solution)/shard_map/backward/pallas_call | solution.py:208
  187.1 3.8 %backward.8.y_ref = f32[1024,512]{1,0:T(8,128)S(1)} custom-call(bf16[4,2,64,768]{3,2,1,0:T(8,128)(2,1)S(1)} %copy-done.7, bf16[4,2,64,768]{3,2,1,0:T(8,128)(2,1)S(1)} %copy-done.9, bf16[1,2,64,768]{3,2,1,0:T(8,128)(2,1)S(1)} %bitcast.134, bf16[7,2,64,768]{3,2,1,0:T(8,128)(2,1)} %collective-permute-done.37.refs_3_, bf16[512,3328]{1,0:T(8,128)(2,1)S(1)} %copy-done, ...), custom_call_target="tpu_custom_call" | custom-call | flops 1610612 | bytes 10485 | tf_op jit(solution)/shard_map/backward/pallas_call | solution.py:208
  197.4 6.5 %collective-permute-done.39 = bf16[128,512]{1,0:T(8,128)(2,1)S(1)} collective-permute-done((bf16[128,512]{1,0:T(8,128)(2,1)S(1)}, bf16[128,512]{1,0:T(8,128)(2,1)S(1)}, u32[]{:S(2)}, u32[]{:S(2)}) %collective-permute-start.39) | collective-permute-done | bytes 131104 | tf_op jit(solution)/shard_map/ppermute | solution.py:460
  204.0 4.5 %backward.9 = (bf16[512,3328]{1,0:T(8,128)(2,1)}, bf16[512,3328]{1,0:T(8,128)(2,1)}) custom-call(bf16[4,2,64,768]{3,2,1,0:T(8,128)(2,1)S(1)} %copy-done.7, bf16[4,2,64,768]{3,2,1,0:T(8,128)(2,1)S(1)} %copy-done.9, bf16[1,2,64,768]{3,2,1,0:T(8,128)(2,1)S(1)} %bitcast.135, ...), custom_call_target="tpu_custom_call", output_to_operand_aliasing={{0}: (5, {}), {1}: (6, {})} | custom-call | flops 1610612 | bytes 10485 | tf_op jit(solution)/shard_map/backward/pallas_call | solution.py:208
  208.5 3.1 %collective-permute-done.44 = bf16[128,512]{1,0:T(8,128)(2,1)S(1)} collective-permute-done((bf16[128,512]{1,0:T(8,128)(2,1)S(1)}, bf16[128,512]{1,0:T(8,128)(2,1)S(1)}, u32[]{:S(2)}, u32[]{:S(2)}) %collective-permute-start.44) | collective-permute-done | bytes 131104 | tf_op jit(solution)/shard_map/ppermute | solution.py:460
  (164 shorter events, 51.3 us)
Async XLA Ops:
  0.6 29.1 %collective-permute-start.1 = (bf16[512,3328]{1,0:T(8,128)(2,1)}, bf16[512,3328]{1,0:T(8,128)(2,1)}, u32[]{:S(2)}, u32[]{:S(2)}) collective-permute-start(bf16[512,3328]{1,0:T(8,128)(2,1)} %refs_4_.5), channel_id=1, source_target_pairs={{0,1},{1,0},{2,3},{3,2},{4,5},{5,4},{6,7},{7,6},{8,9},{9,8},{10,11... | collective-permute-start | bytes 10223624 | tf_op jit(solution)/shard_map/ppermute | solution.py:47
  0.7 29.1 %collective-permute-start.2 = (bf16[512,3328]{1,0:T(8,128)(2,1)}, bf16[512,3328]{1,0:T(8,128)(2,1)}, u32[]{:S(2)}, u32[]{:S(2)}) collective-permute-start(bf16[512,3328]{1,0:T(8,128)(2,1)} %refs_5_.7), channel_id=1, source_target_pairs={{0,1},{1,0},{2,3},{3,2},{4,5},{5,4},{6,7},{7,6},{8,9},{9,8},{10,11... | collective-permute-start | bytes 10223624 | tf_op jit(solution)/shard_map/ppermute | solution.py:47
  40.3 10.5 %collective-permute-start.5 = (bf16[2,2,64,1024]{3,2,1,0:T(8,128)(2,1)S(1)}, bf16[2,2,64,1024]{3,2,1,0:T(8,128)(2,1)S(1)}, u32[]{:S(2)}, u32[]{:S(2)}) collective-permute-start(bf16[2,2,64,1024]{3,2,1,0:T(8,128)(2,1)S(1)} %get-tuple-element.141), channel_id=1, source_target_pairs={{0,4},{1,13},{2,6},{3,15},{4,8},{5,1},{6,10},{7,3},{8,12},{9,5},{1... | collective-permute-start | bytes 1572872 | tf_op jit(solution)/shard_map/ppermute | solution.py:39
  41.9 21.8 %collective-permute-start.4 = (bf16[4,2,64,768]{3,2,1,0:T(8,128)(2,1)S(1)}, bf16[4,2,64,768]{3,2,1,0:T(8,128)(2,1)S(1)}, u32[]{:S(2)}, u32[]{:S(2)}) collective-permute-start(bf16[4,2,64,768]{3,2,1,0:T(8,128)(2,1)S(1)} %get-tuple-element.140), channel_id=1, source_target_pairs={{0,2},{1,3},{2,0},{3,1},{4,6},{5,7},{6,4},{7,5},{8,10},{9,11},{10,... | collective-permute-start | bytes 2359304 | tf_op jit(solution)/shard_map/ppermute | solution.py:43
  51.1 19.6 %collective-permute-start.7 = (bf16[2,2,2,64,1024]{4,3,2,1,0:T(8,128)(2,1)S(1)}, bf16[2,2,2,64,1024]{4,3,2,1,0:T(8,128)(2,1)S(1)}, u32[]{:S(2)}, u32[]{:S(2)}) collective-permute-start(bf16[2,2,2,64,1024]{4,3,2,1,0:T(8,128)(2,1)S(1)} %pad_maximum_fusion.4), channel_id=1, source_target_pairs={{0,4},{1,13},{2,6},{3,15},{4,8},{5,1},{6,10},{7,3},{8,12},{9,5},{1... | collective-permute-start | bytes 3145736 | tf_op jit(solution)/shard_map/ppermute | solution.py:39
  51.4 31.4 %collective-permute-start.3 = (bf16[4,2,64,768]{3,2,1,0:T(8,128)(2,1)S(1)}, bf16[4,2,64,768]{3,2,1,0:T(8,128)(2,1)S(1)}, u32[]{:S(2)}, u32[]{:S(2)}) collective-permute-start(bf16[4,2,64,768]{3,2,1,0:T(8,128)(2,1)S(1)} %get-tuple-element.139), channel_id=1, source_target_pairs={{0,2},{1,3},{2,0},{3,1},{4,6},{5,7},{6,4},{7,5},{8,10},{9,11},{10,... | collective-permute-start | bytes 2359304 | tf_op jit(solution)/shard_map/ppermute | solution.py:43
  69.4 9.1 %collective-permute-start.9 = (bf16[2,2,64,768]{3,2,1,0:T(8,128)(2,1)S(1)}, bf16[2,2,64,768]{3,2,1,0:T(8,128)(2,1)S(1)}, u32[]{:S(2)}, u32[]{:S(2)}) collective-permute-start(bf16[2,2,64,768]{3,2,1,0:T(8,128)(2,1)S(1)} %get-tuple-element.154), channel_id=1, source_target_pairs={{0,4},{1,13},{2,6},{3,15},{4,8},{5,1},{6,10},{7,3},{8,12},{9,5},{1... | collective-permute-start | bytes 1179656 | tf_op jit(solution)/shard_map/ppermute | solution.py:39
  71.0 11.7 %collective-permute-start.8 = (bf16[2,2,64,768]{3,2,1,0:T(8,128)(2,1)S(1)}, bf16[2,2,64,768]{3,2,1,0:T(8,128)(2,1)S(1)}, u32[]{:S(2)}, u32[]{:S(2)}) collective-permute-start(bf16[2,2,64,768]{3,2,1,0:T(8,128)(2,1)S(1)} %pad_maximum_fusion.11), channel_id=1, source_target_pairs={{0,4},{1,13},{2,6},{3,15},{4,8},{5,1},{6,10},{7,3},{8,12},{9,5},{1... | collective-permute-start | bytes 1179656 | tf_op jit(solution)/shard_map/ppermute | solution.py:39
  73.0 13.2 %collective-permute-start.15 = (bf16[2,64,1024]{2,1,0:T(8,128)(2,1)S(1)}, bf16[2,64,1024]{2,1,0:T(8,128)(2,1)S(1)}, u32[]{:S(2)}, u32[]{:S(2)}) collective-permute-start(bf16[2,64,1024]{2,1,0:T(8,128)(2,1)S(1)} %fusion.4), channel_id=1, source_target_pairs={{0,2},{1,3},{2,0},{3,1},{4,6},{5,7},{6,4},{7,5},{8,10},{9,11},{10,... | collective-permute-start | bytes 786440 | tf_op jit(solution)/shard_map/ppermute | solution.py:43
  78.6 13.3 %collective-permute-start.12 = (bf16[2,2,2,64,768]{4,3,2,1,0:T(8,128)(2,1)S(1)}, bf16[2,2,2,64,768]{4,3,2,1,0:T(8,128)(2,1)S(1)}, u32[]{:S(2)}, u32[]{:S(2)}) collective-permute-start(bf16[2,2,2,64,768]{4,3,2,1,0:T(8,128)(2,1)S(1)} %pad_maximum_fusion.6), channel_id=1, source_target_pairs={{0,4},{1,13},{2,6},{3,15},{4,8},{5,1},{6,10},{7,3},{8,12},{9,5},{1... | collective-permute-start | bytes 2359304 | tf_op jit(solution)/shard_map/ppermute | solution.py:39
  83.1 12.0 %collective-permute-start.11 = (bf16[2,64,768]{2,1,0:T(8,128)(2,1)S(1)}, bf16[2,64,768]{2,1,0:T(8,128)(2,1)S(1)}, u32[]{:S(2)}, u32[]{:S(2)}) collective-permute-start(bf16[2,64,768]{2,1,0:T(8,128)(2,1)S(1)} %get-tuple-element.271), channel_id=1, source_target_pairs={{0,4},{1,13},{2,6},{3,15},{4,8},{5,1},{6,10},{7,3},{8,12},{9,5},{1... | collective-permute-start | bytes 589832 | tf_op jit(solution)/shard_map/ppermute | solution.py:39
  92.1 12.0 %collective-permute-start.17 = (bf16[2,64,1024]{2,1,0:T(8,128)(2,1)S(1)}, bf16[2,64,1024]{2,1,0:T(8,128)(2,1)S(1)}, u32[]{:S(2)}, u32[]{:S(2)}) collective-permute-start(bf16[2,64,1024]{2,1,0:T(8,128)(2,1)S(1)} %get-tuple-element.185), channel_id=1, source_target_pairs={{0,2},{1,3},{2,0},{3,1},{4,6},{5,7},{6,4},{7,5},{8,10},{9,11},{10,... | collective-permute-start | bytes 786440 | tf_op jit(solution)/shard_map/ppermute | solution.py:43
  95.0 9.0 %collective-permute-start.18 = (bf16[2,2,64,768]{3,2,1,0:T(8,128)(2,1)S(1)}, bf16[2,2,64,768]{3,2,1,0:T(8,128)(2,1)S(1)}, u32[]{:S(2)}, u32[]{:S(2)}) collective-permute-start(bf16[2,2,64,768]{3,2,1,0:T(8,128)(2,1)S(1)} %pad_maximum_fusion.12), channel_id=1, source_target_pairs={{0,4},{1,13},{2,6},{3,15},{4,8},{5,1},{6,10},{7,3},{8,12},{9,5},{1... | collective-permute-start | bytes 1179656 | tf_op jit(solution)/shard_map/ppermute | solution.py:39
  104.2 9.2 %collective-permute-start.16 = (bf16[2,2,64,768]{3,2,1,0:T(8,128)(2,1)S(1)}, bf16[2,2,64,768]{3,2,1,0:T(8,128)(2,1)S(1)}, u32[]{:S(2)}, u32[]{:S(2)}) collective-permute-start(bf16[2,2,64,768]{3,2,1,0:T(8,128)(2,1)S(1)} %pad_maximum_fusion.13), channel_id=1, source_target_pairs={{0,4},{1,13},{2,6},{3,15},{4,8},{5,1},{6,10},{7,3},{8,12},{9,5},{1... | collective-permute-start | bytes 1179656 | tf_op jit(solution)/shard_map/ppermute | solution.py:39
  104.5 9.1 %collective-permute-start.22 = (bf16[2,64,768]{2,1,0:T(8,128)(2,1)S(1)}, bf16[2,64,768]{2,1,0:T(8,128)(2,1)S(1)}, u32[]{:S(2)}, u32[]{:S(2)}) collective-permute-start(bf16[2,64,768]{2,1,0:T(8,128)(2,1)S(1)} %fusion.7), channel_id=1, source_target_pairs={{0,2},{1,3},{2,0},{3,1},{4,6},{5,7},{6,4},{7,5},{8,10},{9,11},{10,... | collective-permute-start | bytes 589832 | tf_op jit(solution)/shard_map/ppermute | solution.py:43
  105.7 12.1 %collective-permute-start.25 = (bf16[2,64,768]{2,1,0:T(8,128)(2,1)S(1)}, bf16[2,64,768]{2,1,0:T(8,128)(2,1)S(1)}, u32[]{:S(2)}, u32[]{:S(2)}) collective-permute-start(bf16[2,64,768]{2,1,0:T(8,128)(2,1)S(1)} %slice_bitcast_fusion.17), channel_id=1, source_target_pairs={{0,4},{1,13},{2,6},{3,15},{4,8},{5,1},{6,10},{7,3},{8,12},{9,5},{1... | collective-permute-start | bytes 589832 | tf_op jit(solution)/shard_map/ppermute | solution.py:39
  106.2 20.6 %collective-permute-start.27 = (bf16[2,2,2,64,1024]{4,3,2,1,0:T(8,128)(2,1)S(1)}, bf16[2,2,2,64,1024]{4,3,2,1,0:T(8,128)(2,1)S(1)}, u32[]{:S(2)}, u32[]{:S(2)}) collective-permute-start(bf16[2,2,2,64,1024]{4,3,2,1,0:T(8,128)(2,1)S(1)} %pad_maximum_fusion.5), channel_id=1, source_target_pairs={{0,4},{1,13},{2,6},{3,15},{4,8},{5,1},{6,10},{7,3},{8,12},{9,5},{1... | collective-permute-start | bytes 3145736 | tf_op jit(solution)/shard_map/ppermute | solution.py:39
  115.0 8.8 %collective-permute-start.24 = (bf16[2,64,768]{2,1,0:T(8,128)(2,1)S(1)}, bf16[2,64,768]{2,1,0:T(8,128)(2,1)S(1)}, u32[]{:S(2)}, u32[]{:S(2)}) collective-permute-start(bf16[2,64,768]{2,1,0:T(8,128)(2,1)S(1)} %get-tuple-element.203), channel_id=1, source_target_pairs={{0,2},{1,3},{2,0},{3,1},{4,6},{5,7},{6,4},{7,5},{8,10},{9,11},{10,... | collective-permute-start | bytes 589832 | tf_op jit(solution)/shard_map/ppermute | solution.py:43
  123.9 9.1 %collective-permute-start.26 = (bf16[2,2,64,768]{3,2,1,0:T(8,128)(2,1)S(1)}, bf16[2,2,64,768]{3,2,1,0:T(8,128)(2,1)S(1)}, u32[]{:S(2)}, u32[]{:S(2)}) collective-permute-start(bf16[2,2,64,768]{3,2,1,0:T(8,128)(2,1)S(1)} %pad_maximum_fusion.15), channel_id=1, source_target_pairs={{0,4},{1,13},{2,6},{3,15},{4,8},{5,1},{6,10},{7,3},{8,12},{9,5},{1... | collective-permute-start | bytes 1179656 | tf_op jit(solution)/shard_map/ppermute | solution.py:39
  126.8 11.7 %collective-permute-start.30 = (bf16[2,2,64,1024]{3,2,1,0:T(8,128)(2,1)S(1)}, bf16[2,2,64,1024]{3,2,1,0:T(8,128)(2,1)S(1)}, u32[]{:S(2)}, u32[]{:S(2)}) collective-permute-start(bf16[2,2,64,1024]{3,2,1,0:T(8,128)(2,1)S(1)} %slice_bitcast_fusion.1), channel_id=1, source_target_pairs={{0,4},{1,13},{2,6},{3,15},{4,8},{5,1},{6,10},{7,3},{8,12},{9,5},{1... | collective-permute-start | bytes 1572872 | tf_op jit(solution)/shard_map/ppermute | solution.py:39
  126.9 20.0 %collective-permute-start.34 = (bf16[4,2,64,768]{3,2,1,0:T(8,128)(2,1)S(1)}, bf16[4,2,64,768]{3,2,1,0:T(8,128)(2,1)S(1)}, u32[]{:S(2)}, u32[]{:S(2)}) collective-permute-start(bf16[4,2,64,768]{3,2,1,0:T(8,128)(2,1)S(1)} %pad_maximum_fusion.7.refs_0_), channel_id=1, source_target_pairs={{0,2},{1,3},{2,0},{3,1},{4,6},{5,7},{6,4},{7,5},{8,10},{9,11},{10,... | collective-permute-start | bytes 2359304 | tf_op jit(solution)/shard_map/ppermute | solution.py:43
  138.7 9.8 %collective-permute-start.33 = (bf16[3,2,2,64,1024]{4,3,2,1,0:T(8,128)(2,1)S(1)}, bf16[3,2,2,64,1024]{4,3,2,1,0:T(8,128)(2,1)S(1)}, u32[]{:S(2)}, u32[]{:S(2)}) collective-permute-start(bf16[3,2,2,64,1024]{4,3,2,1,0:T(8,128)(2,1)S(1)} %pad_maximum_fusion), channel_id=1, source_target_pairs={{0,1},{1,0},{2,3},{3,2},{4,5},{5,4},{6,7},{7,6},{8,9},{9,8},{10,11... | collective-permute-start | bytes 4718600 | tf_op jit(solution)/shard_map/ppermute | solution.py:47
  142.8 13.3 %collective-permute-start.32 = (bf16[2,2,2,64,768]{4,3,2,1,0:T(8,128)(2,1)S(1)}, bf16[2,2,2,64,768]{4,3,2,1,0:T(8,128)(2,1)S(1)}, u32[]{:S(2)}, u32[]{:S(2)}) collective-permute-start(bf16[2,2,2,64,768]{4,3,2,1,0:T(8,128)(2,1)S(1)} %pad_maximum_fusion.8), channel_id=1, source_target_pairs={{0,4},{1,13},{2,6},{3,15},{4,8},{5,1},{6,10},{7,3},{8,12},{9,5},{1... | collective-permute-start | bytes 2359304 | tf_op jit(solution)/shard_map/ppermute | solution.py:39
  147.1 9.2 %collective-permute-start.36 = (bf16[7,2,64,768]{3,2,1,0:T(8,128)(2,1)S(1)}, bf16[7,2,64,768]{3,2,1,0:T(8,128)(2,1)S(1)}, u32[]{:S(2)}, u32[]{:S(2)}) collective-permute-start(bf16[7,2,64,768]{3,2,1,0:T(8,128)(2,1)S(1)} %pad_maximum_fusion.1), channel_id=1, source_target_pairs={{0,1},{1,0},{2,3},{3,2},{4,5},{5,4},{6,7},{7,6},{8,9},{9,8},{10,11... | collective-permute-start | bytes 4128776 | tf_op jit(solution)/shard_map/ppermute | solution.py:47
  147.2 21.5 %collective-permute-start.31 = (bf16[4,2,64,768]{3,2,1,0:T(8,128)(2,1)S(1)}, bf16[4,2,64,768]{3,2,1,0:T(8,128)(2,1)S(1)}, u32[]{:S(2)}, u32[]{:S(2)}) collective-permute-start(bf16[4,2,64,768]{3,2,1,0:T(8,128)(2,1)S(1)} %pad_maximum_fusion.9.refs_0_), channel_id=1, source_target_pairs={{0,2},{1,3},{2,0},{3,1},{4,6},{5,7},{6,4},{7,5},{8,10},{9,11},{10,... | collective-permute-start | bytes 2359304 | tf_op jit(solution)/shard_map/ppermute | solution.py:43
  156.2 9.1 %collective-permute-start.35 = (bf16[2,2,64,768]{3,2,1,0:T(8,128)(2,1)S(1)}, bf16[2,2,64,768]{3,2,1,0:T(8,128)(2,1)S(1)}, u32[]{:S(2)}, u32[]{:S(2)}) collective-permute-start(bf16[2,2,64,768]{3,2,1,0:T(8,128)(2,1)S(1)} %slice_bitcast_fusion.8), channel_id=1, source_target_pairs={{0,4},{1,13},{2,6},{3,15},{4,8},{5,1},{6,10},{7,3},{8,12},{9,5},{1... | collective-permute-start | bytes 1179656 | tf_op jit(solution)/shard_map/ppermute | solution.py:39
  170.1 17.0 %collective-permute-start.37 = (bf16[7,2,64,768]{3,2,1,0:T(8,128)(2,1)}, bf16[7,2,64,768]{3,2,1,0:T(8,128)(2,1)}, u32[]{:S(2)}, u32[]{:S(2)}) collective-permute-start(bf16[7,2,64,768]{3,2,1,0:T(8,128)(2,1)} %pad_maximum_fusion.2), channel_id=1, source_target_pairs={{0,1},{1,0},{2,3},{3,2},{4,5},{5,4},{6,7},{7,6},{8,9},{9,8},{10,11... | collective-permute-start | bytes 4128776 | tf_op jit(solution)/shard_map/ppermute | solution.py:47
  191.6 12.3 %collective-permute-start.39 = (bf16[128,512]{1,0:T(8,128)(2,1)S(1)}, bf16[128,512]{1,0:T(8,128)(2,1)S(1)}, u32[]{:S(2)}, u32[]{:S(2)}) collective-permute-start(bf16[128,512]{1,0:T(8,128)(2,1)S(1)} %get-tuple-element.251), channel_id=1, source_target_pairs={{0,16},{16,32},{32,48},{48,0},{64,80},{80,96},{96,112},{112,64},{1... | collective-permute-start | bytes 393224 | tf_op jit(solution)/shard_map/ppermute | solution.py:460
  191.9 12.1 %collective-permute-start.40 = (bf16[128,512]{1,0:T(8,128)(2,1)S(1)}, bf16[128,512]{1,0:T(8,128)(2,1)S(1)}, u32[]{:S(2)}, u32[]{:S(2)}) collective-permute-start(bf16[128,512]{1,0:T(8,128)(2,1)S(1)} %get-tuple-element.252), channel_id=1, source_target_pairs={{0,32},{16,48},{32,0},{48,16},{64,96},{80,112},{96,64},{112,80},{1... | collective-permute-start | bytes 393224 | tf_op jit(solution)/shard_map/ppermute | solution.py:460
  193.9 14.6 %collective-permute-start.41 = (bf16[128,512]{1,0:T(8,128)(2,1)S(1)}, bf16[128,512]{1,0:T(8,128)(2,1)S(1)}, u32[]{:S(2)}, u32[]{:S(2)}) collective-permute-start(bf16[128,512]{1,0:T(8,128)(2,1)S(1)} %get-tuple-element.253), channel_id=1, source_target_pairs={{0,48},{16,0},{32,16},{48,32},{64,112},{80,64},{96,80},{112,96},{1... | collective-permute-start | bytes 393224 | tf_op jit(solution)/shard_map/ppermute | solution.py:460
  195.2 13.3 %collective-permute-start.42 = (bf16[128,512]{1,0:T(8,128)(2,1)S(1)}, bf16[128,512]{1,0:T(8,128)(2,1)S(1)}, u32[]{:S(2)}, u32[]{:S(2)}) collective-permute-start(bf16[128,512]{1,0:T(8,128)(2,1)S(1)} %get-tuple-element.254), channel_id=1, source_target_pairs={{0,64},{16,80},{32,96},{48,112},{64,0},{80,16},{96,32},{112,48},{1... | collective-permute-start | bytes 393224 | tf_op jit(solution)/shard_map/ppermute | solution.py:460
  195.4 13.2 %collective-permute-start.43 = (bf16[128,512]{1,0:T(8,128)(2,1)S(1)}, bf16[128,512]{1,0:T(8,128)(2,1)S(1)}, u32[]{:S(2)}, u32[]{:S(2)}) collective-permute-start(bf16[128,512]{1,0:T(8,128)(2,1)S(1)} %get-tuple-element.255), channel_id=1, source_target_pairs={{0,80},{16,96},{32,112},{48,64},{64,16},{80,32},{96,48},{112,0},{1... | collective-permute-start | bytes 393224 | tf_op jit(solution)/shard_map/ppermute | solution.py:460
  (31 other events, 295.1 us)

commit v3 on v2

--- a/solution.py
+++ b/solution.py
@@ -9,16 +9,10 @@
 
 F32, BF16 = jnp.float32, jnp.bfloat16
 TILE = 256
-CHUNKS = (("b", 3), ("a", 4), ("a", 3), ("b", 3))
-ORDER = (
-    (0, "f"), (1, "f"), (3, "f"), (1, "a1"), (0, "b1"), (2, "f"), (1, "ac"), (0, "b2"),
-    (1, "a2"), (2, "a1"), (0, "bc"), (3, "b1"), (0, "g"), (1, "g"), (0, "c1"), (2, "ac"),
-    (3, "b2"), (2, "a2"), (0, "c2"), (1, "b1"), (1, "b2"), (3, "bc"), (2, "g"), (3, "g"),
-    (0, "c3"), (2, "b1"), (3, "c1"), (1, "b3"), (3, "c2"), (1, "b4"), (2, "b2"), (3, "c3"),
-    (0, "c4"), (1, "d"), (1, "K"), (2, "b3"), (0, "d"), (0, "K"), (2, "b4"), (3, "c4"),
-    (2, "d"), (2, "K"), (3, "d"), (3, "Ky"), (3, "Kw"),
-)
+CHUNKS = (('b', 3), ('a', 4), ('a', 3), ('a', 3))
+ORDER = ((2, 'f'), (3, 'f'), (2, 'a1'), (0, 'f'), (3, 'a1'), (1, 'f'), (2, 'ac'), (0, 'b1'), (3, 'ac'), (2, 'a2'), (1, 'a1'), (3, 'a2'), (2, 'g'), (0, 'b2'), (2, 'b1'), (3, 'g'), (1, 'ac'), (2, 'b2'), (0, 'bc'), (1, 'a2'), (0, 'g'), (0, 'c1'), (1, 'g'), (3, 'b1'), (2, 'b3'), (0, 'c2'), (2, 'b4'), (3, 'b2'), (0, 'c3'), (1, 'b1'), (1, 'b2'), (2, 'd'), (2, 'K'), (3, 'b3'), (0, 'c4'), (1, 'b3'), (3, 'b4'), (0, 'd'), (0, 'K'), (3, 'd'), (1, 'b4'), (3, 'K'), (1, 'd'), (1, 'Ky'), (1, 'Kw'))
 MIB = 1 << 20
+COST = {'f': 0, 'g': 0.001, 'k': 0.3}
 
 
 def column(x, y, core):
@@ -51,41 +45,50 @@
     return pltpu.CompilerParams(vmem_limit_bytes=mib * MIB)
 
 
+def in_hbm(v):
+    return pltpu.with_memory_space_constraint(v, pltpu.HBM)
+
+
 def whole(shape):
-    return pl.BlockSpec(shape, lambda *_: (0,) * len(shape))
+    return pl.BlockSpec(shape, lambda *_: (0,) * len(shape), pipeline_mode=pl.Buffered(1))
 
 
 SMEM = pl.BlockSpec(memory_space=pltpu.SMEM)
 ANY = pl.BlockSpec(memory_space=pl.ANY)
 
 
-def cost(flops, bytes_accessed):
-    return pl.CostEstimate(flops=flops // 1000, bytes_accessed=bytes_accessed // 1000, transcendentals=0)
-
-
-def arrange_kernel(at_ref, own_ref, sib_ref, lhs_ref, xt_ref):
-    def piece(ref, i):
-        return ref[at_ref[0, i], pl.ds(pl.multiple_of(at_ref[1, i], 64), 64), :]
-
+def cost(kind, flops, bytes_accessed):
+    part = COST[kind]
+    return pl.CostEstimate(flops=int(flops * part), bytes_accessed=int(bytes_accessed * part), transcendentals=0)
+
+
+def piece(at_ref, ref, i):
+    return ref[at_ref[0, i], pl.ds(pl.multiple_of(at_ref[1, i], 64), 64), :]
+
+
+def arrange_kernel(at_ref, own_ref, sib_ref, lhs_ref):
     for i in range(8):
-        lhs_ref[pl.ds(64 * i, 64), :512] = piece(own_ref, i)
-        lhs_ref[pl.ds(64 * i, 64), 512:] = piece(sib_ref, i)
+        lhs_ref[pl.ds(64 * i, 64), :512] = piece(at_ref, own_ref, i)
+        lhs_ref[pl.ds(64 * i, 64), 512:] = piece(at_ref, sib_ref, i)
+
+
+def turn_kernel(at_ref, own_ref, xt_ref):
     for i in range(8):
-        pair = [piece(own_ref, 8 + 2 * i), piece(own_ref, 9 + 2 * i)]
+        pair = [piece(at_ref, own_ref, 8 + 2 * i), piece(at_ref, own_ref, 9 + 2 * i)]
         xt_ref[:, pl.ds(128 * i, 128)] = jnp.concatenate(pair, axis=0).T
 
 
-def arrange(at, own, sib):
+def arrange(kernel, at, *blocks):
     return pl.pallas_call(
-        arrange_kernel,
-        out_shape=(jax.ShapeDtypeStruct((512, 1024), BF16), jax.ShapeDtypeStruct((512, 1024), BF16)),
-        in_specs=[SMEM, whole(own.shape), whole(own.shape)],
-        out_specs=(whole((512, 1024)), whole((512, 1024))),
+        kernel,
+        out_shape=jax.ShapeDtypeStruct((512, 1024), BF16),
+        in_specs=[SMEM] + [whole(v.shape) for v in blocks],
+        out_specs=pl.BlockSpec((512, 1024), lambda j: (0, 0)),
         grid=(1,),
-        compiler_params=params(16),
-        cost_estimate=cost(0, 4 * MIB),
+        compiler_params=params(8),
+        cost_estimate=cost("f", 0, 4 * MIB),
         name="arrange_tokens",
-    )(at, own, sib)
+    )(at, *blocks)
 
 
 def forward_kernel(path, lhs_ref, go_ref, gs_ref, lo_ref, ls_ref, *outs):
@@ -115,8 +118,8 @@
         in_specs=[whole((512, 1024)), w, w, w, w],
         out_specs=tuple(pl.BlockSpec((lead, 2, 64, TILE), lambda j: (0, 0, 0, j)) for _ in kinds),
         grid=(tiles,),
-        compiler_params=params(24),
-        cost_estimate=cost(4 * 512 * 1024 * n, 4 * 1024 * n + 6 * 1024 * n),
+        compiler_params=params(12),
+        cost_estimate=cost("f", 4 * 512 * 1024 * n, 4 * 1024 * n + 6 * 1024 * n),
         name="forward_" + path,
     )(lhs, own_gate, sib_gate, own_lift, sib_lift)
 
@@ -135,112 +138,107 @@
     grads_ref[1] = (cot * silu).astype(BF16)
 
 
-def gating(first, tiles, terms, cot, gated):
+def gating(first, tiles, terms, cot):
     n = tiles * TILE
-    wide = pl.BlockSpec((64, TILE), lambda j: (0, first + j))
-    part = pl.BlockSpec((2, 64, TILE), lambda j: (0, 0, j))
-    more, alias = ([], {}) if gated is None else ([gated], {len(terms) + 1: 0})
     return pl.pallas_call(
         functools.partial(gate_kernel, len(terms)),
-        out_shape=(jax.ShapeDtypeStruct(cot.shape, BF16), jax.ShapeDtypeStruct((2, 64, n), BF16)),
-        in_specs=[part] * len(terms) + [wide] + [ANY] * len(more),
-        out_specs=(wide, part),
-        grid=(tiles,),
-        input_output_aliases=alias,
-        compiler_params=params(16),
-        cost_estimate=cost(0, 64 * n * 20),
+        out_shape=(jax.ShapeDtypeStruct((64, n), BF16), jax.ShapeDtypeStruct((2, 64, n), BF16)),
+        in_specs=[whole((2, 64, n))] * len(terms) + [whole((64, n))],
+        out_specs=(pl.BlockSpec((64, n), lambda j: (0, 0)), pl.BlockSpec((2, 64, n), lambda j: (0, 0, 0))),
+        grid=(1,),
+        compiler_params=params(8),
+        cost_estimate=cost("g", 0, 64 * n * 20),
         name="gating",
-    )(*terms, cot, *more)
-
-
-def backward_kernel(arrays, table, do_w, do_y, carried, *refs):
-    refs = list(refs)
-    held = [refs.pop(0) for _ in range(arrays)]
-    if do_w:
-        xt_ref = refs.pop(0)
-    if do_y:
-        w_refs = [refs.pop(0), refs.pop(0)]
-        if carried:
-            y_in = refs.pop(0)
-    outs = refs[-(2 * do_w + do_y) :]
-    if do_y:
-        y_ref = outs[-1]
+    )(*terms, cot[:, first * TILE : first * TILE + n])
+
+
+def tokens(held, table, m):
+    return jnp.concatenate([held[i][j, m] for i, j in table], axis=0)
+
+
+def backward_kernel(arrays, table, with_y, *refs):
+    held, (xt_ref, gate_ref, lift_ref) = refs[:arrays], refs[arrays : arrays + 3]
+    outs = refs[-3:] if with_y else refs[-2:]
+    both = [tokens(held, table, m) for m in range(2)]
+    for m in range(2):
+        outs[m][...] = jnp.dot(xt_ref[...], both[m], preferred_element_type=F32).astype(BF16)
+    if with_y:
+        grad = jnp.concatenate(both, axis=1)
+        weight = jnp.concatenate([gate_ref[...], lift_ref[...]], axis=1)
+        part = lax.dot_general(grad, weight, (((1,), (1,)), ((), ())), preferred_element_type=F32)
 
         @pl.when(pl.program_id(0) == 0)
         def _():
-            y_ref[...] = y_in[...] if carried else jnp.zeros_like(y_ref)
-
-    both = [jnp.concatenate([held[i][j, m] for i, j in table], axis=0) for m in range(2)]
-    if do_w:
-        for m in range(2):
-            outs[m][...] = jnp.dot(xt_ref[...], both[m], preferred_element_type=F32).astype(BF16)
-    if do_y:
-        dims = (((1,), (1,)), ((), ()))
-        add = lax.dot_general(both[0], w_refs[0][...], dims, preferred_element_type=F32)
-        add = add + lax.dot_general(both[1], w_refs[1][...], dims, preferred_element_type=F32)
-        y_ref[...] += add
-
-
-def backward(first, tiles, pieces, table, xt, gate, lift, grads, y, do_w, do_y):
-    n = tiles * TILE
-    wide = pl.BlockSpec((512, TILE), lambda j: (0, first + j))
-    args = list(pieces)
-    specs = [pl.BlockSpec((v.shape[0], 2, 64, TILE), lambda j: (0, 0, 0, j)) for v in pieces]
-    alias, shapes, out_specs = {}, [], []
-    if do_w:
-        args.append(xt)
-        specs.append(whole(xt.shape))
-        shapes += [jax.ShapeDtypeStruct(gate.shape, BF16)] * 2
-        out_specs += [wide, wide]
-    if do_y:
-        args += [gate, lift]
-        specs += [wide, wide]
-        if y is not None:
-            args.append(y)
-            specs.append(whole((1024, 512)))
+            outs[2][...] = part
+
+        @pl.when(pl.program_id(0) > 0)
+        def _():
+            outs[2][...] += part
+
+
+def backward(first, tiles, pieces, table, xt, gate, lift, grads, with_y):
+    n = TILE
+    wide = pl.BlockSpec((512, n), lambda j: (0, first + j))
+    args = [*pieces, xt, gate, lift]
+    specs = [pl.BlockSpec((v.shape[0], 2, 64, n), lambda j: (0, 0, 0, j)) for v in pieces]
+    specs += [whole(xt.shape), wide, wide]
+    alias, shapes, out_specs = {}, [jax.ShapeDtypeStruct(gate.shape, BF16)] * 2, [wide, wide]
+    if with_y:
         shapes.append(jax.ShapeDtypeStruct((1024, 512), F32))
-        out_specs.append(whole((1024, 512)))
-    if do_w and grads is not None:
+        out_specs.append(pl.BlockSpec((1024, 512), lambda j: (0, 0)))
+    if grads is not None:
         for m in range(2):
             alias[len(args)] = m
             args.append(grads[m])
             specs.append(ANY)
-    out = pl.pallas_call(
-        functools.partial(backward_kernel, len(pieces), table, do_w, do_y, y is not None),
+    return pl.pallas_call(
+        functools.partial(backward_kernel, len(pieces), table, with_y),
         out_shape=tuple(shapes),
         in_specs=specs,
         out_specs=tuple(out_specs),
         grid=(tiles,),
         input_output_aliases=alias,
-        compiler_params=params(28),
-        cost_estimate=cost((do_w + do_y) * 4 * 512 * 1024 * n, 8 * 1024 * n + 4 * MIB),
+        compiler_params=params(16),
+        cost_estimate=cost("k", (1 + with_y) * 4 * 512 * 1024 * n * tiles, 8 * 1024 * n * tiles + 4 * MIB),
         name="backward",
     )(*args)
-    return (tuple(out[:2]) if do_w else grads), (out[-1] if do_y else y)
-
-
-def split_kernel(at_ref, y_ref, own_ref, *outs):
+
+
+def split_kernel(arrays, table, others, at_ref, *refs):
+    held, (gate_ref, lift_ref) = refs[:arrays], refs[arrays : arrays + 2]
+    y_refs, outs = refs[arrays + 2 : arrays + 2 + others], refs[arrays + 2 + others : -1]
+    total_ref = refs[-1]
+    grad = jnp.concatenate([tokens(held, table, m) for m in range(2)], axis=1)
+    weight = jnp.concatenate([gate_ref[...], lift_ref[...]], axis=1)
+    total = lax.dot_general(grad, weight, (((1,), (1,)), ((), ())), preferred_element_type=F32)
+    for ref in y_refs:
+        total = total + ref[...]
+    total_ref[...] = total
     for i in range(8):
         for h in range(2):
-            rows = y_ref[pl.ds(pl.multiple_of(at_ref[i, h], 64), 64), :]
-            if i == 0:
-                own_ref[pl.ds(64 * h, 64), :] = rows
-            else:
-                outs[i - 1][pl.ds(64 * h, 64), :] = rows.astype(BF16)
-
-
-def split(at, y):
+            rows = total_ref[pl.ds(pl.multiple_of(at_ref[i, h], 64), 64), :]
+            outs[i][pl.ds(64 * h, 64), :] = rows.astype(outs[i].dtype)
+
+
+def split(at, first, tiles, pieces, table, gate, lift, ys):
+    assert first % tiles == 0
+    n = tiles * TILE
     kinds = [F32] + [BF16] * 7
+    w = pl.BlockSpec((256, n), lambda j: (j, first // tiles))
     return pl.pallas_call(
-        split_kernel,
+        functools.partial(split_kernel, len(pieces), table, len(ys)),
         out_shape=tuple(jax.ShapeDtypeStruct((128, 512), t) for t in kinds),
-        in_specs=[SMEM, whole((1024, 512))],
-        out_specs=tuple(whole((128, 512)) for _ in kinds),
-        grid=(1,),
-        compiler_params=params(16),
-        cost_estimate=cost(0, 3 * MIB),
+        in_specs=[SMEM]
+        + [whole(v.shape) for v in pieces]
+        + [w, w]
+        + [pl.BlockSpec((1024, 256), lambda j: (0, j))] * len(ys),
+        out_specs=tuple(pl.BlockSpec((128, 256), lambda j: (0, j)) for _ in kinds),
+        scratch_shapes=[pltpu.VMEM((1024, 256), F32)],
+        grid=(2,),
+        compiler_params=params(20),
+        cost_estimate=cost("k", 4 * 512 * 1024 * n, 8 * 1024 * n + 4 * MIB),
         name="split_rows",
-    )(at, y)
+    )(at, *pieces, gate, lift, *ys)
 
 
 class Sequence:
@@ -286,7 +284,7 @@
 
     def gate():
         own, other = seq(s["own"], s["other"])
-        use["gated"], s["own"] = gating(first, tiles, [own, other], use["cot"], use["gated"])
+        use["gated"][first], s["own"] = gating(first, tiles, [own, other], use["cot"])
         seq.done(s["own"])
         s["other"] = over_y(s["own"])
 
@@ -359,7 +357,7 @@
 
     def gate():
         own, near, other = seq(s["own"], s["near"], s["other"])
-        use["gated"], s["own"] = gating(first, tiles, [own, near[0], other], use["cot"], use["gated"])
+        use["gated"][first], s["own"] = gating(first, tiles, [own, near[0], other], use["cot"])
         seq.done(s["own"])
         s["sib"] = over_core(s["own"])
 
@@ -419,32 +417,6 @@
     order = [(block(dx, dy), 64 * h) for dx, h in fwd for dy in range(2)]
     order += [(block(dx, dy), 64 * h) for dy in range(2) for dx, h in bwd]
     at = jnp.stack([jnp.stack([i for i, _ in order]), jnp.stack([h for _, h in order])]).astype(jnp.int32)
-    lhs, xt = arrange(at, own_x, sib_x)
-
-    weights = (gate_matrix, sib_gate, lift_matrix, sib_lift)
-    use = dict(lhs=lhs, weights=weights, cot=out_cotangent, gated=None)
-    seq = Sequence()
-    first, steps, spans = 0, [], []
-    for path, tiles in CHUNKS:
-        steps.append((x_first if path == "a" else y_first)(seq, first, tiles, use))
-        spans.append((first, tiles))
-        first += tiles
-
-    grads, y, parts = None, None, None
-    rest = (xt, gate_matrix, lift_matrix)
-    for i, step in ORDER:
-        if step[0] != "K":
-            steps[i][step]()
-            continue
-        if step == "Kw":
-            pieces = steps[i]["pieces"]()
-        else:
-            pieces = seq(*steps[i]["pieces"]())
-        do = (step != "Ky", step != "Kw")
-        grads, y = backward(*spans[i], pieces, steps[i]["table"], *rest, grads, y, *do)
-        if step != "Kw":
-            seq.done(y)
-
     def place(i, h):
         row = (r // 4 + i // 4) % 2 * 4 + (r % 4 + i % 4) % 4
         dx, dy = (row // 2 - x) % 4, (row - yh) % 2
@@ -454,11 +426,46 @@
         return 64 * (8 * dy + q)
 
     where = jnp.stack([jnp.stack([place(i, h) for h in range(2)]) for i in range(8)]).astype(jnp.int32)
-    parts = split(where, y)
+    at, where = lax.optimization_barrier((at, where))
+    lhs = arrange(arrange_kernel, at, own_x, sib_x)
+
+    own_gate, own_lift = in_hbm(gate_matrix), in_hbm(lift_matrix)
+    weights = (own_gate, sib_gate, own_lift, sib_lift)
+    use = dict(lhs=lhs, weights=weights, cot=out_cotangent, gated={})
+    seq = Sequence()
+    steps, spans, last = [], [], ORDER[-1][0]
+    for i, (path, tiles) in enumerate(CHUNKS):
+        first = sum(t for j, (_, t) in enumerate(CHUNKS) if (j != last, t, j) < (i != last, tiles, i))
+        steps.append((x_first if path == "a" else y_first)(seq, first, tiles, use))
+        spans.append((first, tiles))
+
+    grads, ys, xt = None, [], None
+    for i, step in ORDER:
+        if step == "a2" and xt is None:
+            xt = arrange(turn_kernel, at, seq(own_x))
+            seq.done(xt)
+        if step[0] != "K":
+            steps[i][step]()
+            continue
+        pieces = seq(*steps[i]["pieces"]())
+        table = steps[i]["table"]
+        if step == "Ky":
+            assert len(ys) == len(CHUNKS) - 1
+            parts = split(where, *spans[i], pieces, table, own_gate, own_lift, ys)
+            got = {i: lax.ppermute(parts[i], "row", row_step(i)) for i in (6, 2, 5, 7, 1, 3, 4)}
+            got[6], got[2] = seq(got[6], got[2])
+            seq.done(got[2])
+            continue
+        grads = backward(*spans[i], pieces, table, xt, own_gate, own_lift, grads, step == "K")
+        if step == "K":
+            seq.done(grads[2])
+            ys.append(grads[2])
+
     total = parts[0]
     for i in range(1, 8):
-        total = total + lax.ppermute(parts[i], "row", row_step(i)).astype(F32)
-    return (seq(use["gated"]), total.astype(BF16), grads[0], grads[1])
+        total = total + got[i].astype(F32)
+    gated = jnp.concatenate([use["gated"][first] for first in sorted(use["gated"])], axis=1)
+    return (gated, total.astype(BF16), grads[0], grads[1])
 
 
 def solution(mesh):

time: 213 us -> 192 us (0.901)
  waiting for transfers between devices: 90.5 us -> 60.4 us
  starting transfers between devices: 32 us -> 46.6 us
  local copies, waits for them, and re-layouts: 10.5 us -> 6.64 us
    ppermute x16, waiting for transfers between devices: 49.4 us -> 18.9 us  [over_x(): return lax.ppermute(v, 'col', ALONG_X)]
    ppermute x8, waiting for transfers between devices: 18.6 us -> 35.8 us  [over_y(): return lax.ppermute(v, 'col', ALONG_Y)]
    ppermute x15, waiting for transfers between devices: 12.8 us -> 2.75 us  [over_core(): return lax.ppermute(v, 'col', CORE)]
    ppermute x16, starting transfers between devices: 6.93 us -> 16.8 us  [over_x(): return lax.ppermute(v, 'col', ALONG_X)]
    ppermute x7, waiting for transfers between devices: 9.67 us -> 2.98 us  [body(): lax.ppermute(parts[i], 'row', row_step(i))]
    pallas_call x4, Pallas kernels: 5.61 us -> 0.63 us  [gating(): pl.pallas_call(functools.partial(gate_kernel, len(terms)), out_shape=(jax...]
    unnamed x34, local copies, waits for them, and re-layouts: 8.69 us -> 3.97 us
    pallas_call x7, Pallas kernels: 28.5 us -> 32.9 us  [the longest x4 24.8 us: backward(): pl.pallas_call(functools.partial(backward_kernel, len(pieces), table, wit...]
  transfers between devices with their start and end apart: 46 -> 46, of which waited for: 25 -> 18; matrix products, arithmetic and copies ran while one was open for 2% -> 3% of each run, Pallas kernels for 17% -> 21%
where the time goes in v3:
time: 192 us; the launch traced here: 191 us
  waiting for transfers between devices  60.4 us (31%)
  Pallas kernels  49.6 us (26%)
  starting transfers between devices  46.6 us (24%)
  blocking collectives  22.3 us (12%)
  local copies, waits for them, and re-layouts  6.64 us (3%)
  other arithmetic  4.58 us (2%)
    ppermute x8, waiting for transfers between devices, over_y(): return lax.ppermute(v, 'col', ALONG_Y)  35.8 us
    pallas_call x4, Pallas kernels, backward(): pl.pallas_call(functools.partial(backward_kernel, len(pieces), table, wit...  24.8 us
    all_to_all x1, blocking collectives, body(): lax.all_to_all(jnp.broadcast_to(inputs[None], (8, 128, 512)), 'row', 0, 0)  22.3 us
    ppermute x16, waiting for transfers between devices, over_x(): return lax.ppermute(v, 'col', ALONG_X)  18.9 us
    ppermute x16, starting transfers between devices, over_x(): return lax.ppermute(v, 'col', ALONG_X)  16.8 us
    pallas_call x4, Pallas kernels, forward(): pl.pallas_call(functools.partial(forward_kernel, path), out_shape=tuple((...  16.1 us
    ppermute x8, starting transfers between devices, over_y(): return lax.ppermute(v, 'col', ALONG_Y)  16 us
    ppermute x7, starting transfers between devices, body(): lax.ppermute(parts[i], 'row', row_step(i))  10 us
  transfers between devices with their start and end apart: 46, of which 18 were waited for; matrix products, arithmetic and copies ran while one was open for 3% of the time, Pallas kernels for 21%

profile of v3, /device:TPU:0, one launch (start us, length us, event | category | flops | bytes accessed | tf_op | source)
XLA Modules:
  0.0 191.5 jit_solution(5830707742262175125)
XLA Ops:
  2.2 22.3 %all_to_all.5.own_ref = bf16[8,128,512]{2,1,0:T(8,128)(2,1)} all-to-all(bf16[8,128,512]{2,1,0:T(8,128)(2,1)S(1)} %broadcast_in_dim.22), channel_id=1, replica_groups=mesh['row'=8,'col'=16] {'row'}, dimensions={0} | all-to-all | bytes 2097152 | tf_op jit(solution)/shard_map/all_to_all | solution.py:408
  29.2 3.8 %forward_a.3 = (bf16[2,2,64,768]{3,2,1,0:T(8,128)(2,1)S(1)}, bf16[2,2,64,768]{3,2,1,0:T(8,128)(2,1)S(1)}, f32[2,2,64,768]{3,2,1,0:T(8,128)S(1)}, f32[2,2,64,768]{3,2,1,0:T(8,128)S(1)}) custom-call(bf16[512,1024]{1,0:T(8,128)(2,1)S(1)} %arrange_tokens.2.lhs_ref, bf16[512,3328]{1,0:T(8,128)(2,1)} %refs_4_.7, ...), custom_call_target="tpu_custom_call" | custom-call | tf_op jit(solution)/shard_map/forward_a/pallas_call | solution.py:115
  34.6 3.8 %forward_a.4 = (bf16[2,2,64,768]{3,2,1,0:T(8,128)(2,1)S(1)}, bf16[2,2,64,768]{3,2,1,0:T(8,128)(2,1)S(1)}, f32[2,2,64,768]{3,2,1,0:T(8,128)S(1)}, f32[2,2,64,768]{3,2,1,0:T(8,128)S(1)}) custom-call(bf16[512,1024]{1,0:T(8,128)(2,1)S(1)} %arrange_tokens.2.lhs_ref, bf16[512,3328]{1,0:T(8,128)(2,1)} %refs_4_.7, ...), custom_call_target="tpu_custom_call" | custom-call | tf_op jit(solution)/shard_map/forward_a/pallas_call | solution.py:115
  39.9 2.1 %collective-permute-done.4 = bf16[2,2,64,768]{3,2,1,0:T(8,128)(2,1)S(1)} collective-permute-done((bf16[2,2,64,768]{3,2,1,0:T(8,128)(2,1)S(1)}, bf16[2,2,64,768]{3,2,1,0:T(8,128)(2,1)S(1)}, u32[]{:S(2)}, u32[]{:S(2)}) %collective-permute-start.4) | collective-permute-done | bytes 393248 | tf_op jit(solution)/shard_map/ppermute | solution.py:33
  42.6 3.8 %forward_b.1 = (f32[4,2,64,768]{3,2,1,0:T(8,128)S(1)}, bf16[4,2,64,768]{3,2,1,0:T(8,128)(2,1)S(1)}) custom-call(bf16[512,1024]{1,0:T(8,128)(2,1)S(1)} %arrange_tokens.2.lhs_ref, bf16[512,3328]{1,0:T(8,128)(2,1)} %refs_4_.7, bf16[512,3328]{1,0:T(8,128)(2,1)S(1)} %collective-permute-done.1.gs_ref, bf16[512,3328]{1,0:T(8,128)(2,1)} %refs_5_.7, ...), custom_call_target="tpu_custom_call" | custom-call | tf_op jit(solution)/shard_map/forward_b/pallas_call | solution.py:115
  46.4 3.0 %collective-permute-start.9 = (bf16[4,2,64,768]{3,2,1,0:T(8,128)(2,1)S(1)}, bf16[4,2,64,768]{3,2,1,0:T(8,128)(2,1)S(1)}, u32[]{:S(2)}, u32[]{:S(2)}) collective-permute-start(bf16[4,2,64,768]{3,2,1,0:T(8,128)(2,1)S(1)} %get-tuple-element.160), channel_id=1, source_target_pairs={{0,2},{1,3},{2,0},{3,1},{4,6},{5,7},{6,4},{7,5},{8,10},{9,11},{10,... | collective-permute-start | bytes 2359304 | tf_op jit(solution)/shard_map/ppermute | solution.py:37
  51.1 4.7 %forward_a.5 = (bf16[2,2,64,1024]{3,2,1,0:T(8,128)(2,1)S(1)}, bf16[2,2,64,1024]{3,2,1,0:T(8,128)(2,1)S(1)}, f32[2,2,64,1024]{3,2,1,0:T(8,128)S(1)}, f32[2,2,64,1024]{3,2,1,0:T(8,128)S(1)}) custom-call(bf16[512,1024]{1,0:T(8,128)(2,1)S(1)} %arrange_tokens.2.lhs_ref, bf16[512,3328]{1,0:T(8,128)(2,1)} %refs_4_.7, ...), custom_call_target="tpu_custom_call" | custom-call | tf_op jit(solution)/shard_map/forward_a/pallas_call | solution.py:115
  57.2 11.0 %collective-permute-done.9 = bf16[4,2,64,768]{3,2,1,0:T(8,128)(2,1)S(1)} collective-permute-done((bf16[4,2,64,768]{3,2,1,0:T(8,128)(2,1)S(1)}, bf16[4,2,64,768]{3,2,1,0:T(8,128)(2,1)S(1)}, u32[]{:S(2)}, u32[]{:S(2)}) %collective-permute-start.9) | collective-permute-done | bytes 786464 | tf_op jit(solution)/shard_map/ppermute | solution.py:37
  70.6 3.2 %collective-permute-start.13 = (bf16[2,64,768]{2,1,0:T(8,128)(2,1)S(1)}, bf16[2,64,768]{2,1,0:T(8,128)(2,1)S(1)}, u32[]{:S(2)}, u32[]{:S(2)}) collective-permute-start(bf16[2,64,768]{2,1,0:T(8,128)(2,1)S(1)} %fusion.8), channel_id=1, source_target_pairs={{0,2},{1,3},{2,0},{3,1},{4,6},{5,7},{6,4},{7,5},{8,10},{9,11},{10,... | collective-permute-start | bytes 589832 | tf_op jit(solution)/shard_map/ppermute | solution.py:37
  74.1 1.8 collective-permute-start.10
  76.6 2.8 %collective-permute-done.13.refs_1_ = bf16[2,64,768]{2,1,0:T(8,128)(2,1)S(1)} collective-permute-done((bf16[2,64,768]{2,1,0:T(8,128)(2,1)S(1)}, bf16[2,64,768]{2,1,0:T(8,128)(2,1)S(1)}, u32[]{:S(2)}, u32[]{:S(2)}) %collective-permute-start.13) | collective-permute-done | bytes 196640 | tf_op jit(solution)/shard_map/ppermute | solution.py:37
  79.6 3.2 %collective-permute-start.14 = (bf16[2,64,768]{2,1,0:T(8,128)(2,1)S(1)}, bf16[2,64,768]{2,1,0:T(8,128)(2,1)S(1)}, u32[]{:S(2)}, u32[]{:S(2)}) collective-permute-start(bf16[2,64,768]{2,1,0:T(8,128)(2,1)S(1)} %get-tuple-element.181), channel_id=1, source_target_pairs={{0,2},{1,3},{2,0},{3,1},{4,6},{5,7},{6,4},{7,5},{8,10},{9,11},{10,... | collective-permute-start | bytes 589832 | tf_op jit(solution)/shard_map/ppermute | solution.py:37
  82.9 2.3 %collective-permute-start.17 = (bf16[2,2,64,768]{3,2,1,0:T(8,128)(2,1)S(1)}, bf16[2,2,64,768]{3,2,1,0:T(8,128)(2,1)S(1)}, u32[]{:S(2)}, u32[]{:S(2)}) collective-permute-start(bf16[2,2,64,768]{3,2,1,0:T(8,128)(2,1)S(1)} %pad_maximum_fusion.13), channel_id=1, source_target_pairs={{0,4},{1,13},{2,6},{3,15},{4,8},{5,1},{6,10},{7,3},{8,12},{9,5},{1... | collective-permute-start | bytes 1179656 | tf_op jit(solution)/shard_map/ppermute | solution.py:33
  85.2 4.3 %collective-permute-done.14 = bf16[2,64,768]{2,1,0:T(8,128)(2,1)S(1)} collective-permute-done((bf16[2,64,768]{2,1,0:T(8,128)(2,1)S(1)}, bf16[2,64,768]{2,1,0:T(8,128)(2,1)S(1)}, u32[]{:S(2)}, u32[]{:S(2)}) %collective-permute-start.14) | collective-permute-done | bytes 196640 | tf_op jit(solution)/shard_map/ppermute | solution.py:37
  98.6 6.5 %collective-permute-done.19.refs_1_ = bf16[2,64,1024]{2,1,0:T(8,128)(2,1)S(1)} collective-permute-done((bf16[2,64,1024]{2,1,0:T(8,128)(2,1)S(1)}, bf16[2,64,1024]{2,1,0:T(8,128)(2,1)S(1)}, u32[]{:S(2)}, u32[]{:S(2)}) %collective-permute-start.19) | collective-permute-done | bytes 262176 | tf_op jit(solution)/shard_map/ppermute | solution.py:37
  110.0 4.5 %collective-permute-done.28 = bf16[2,2,64,768]{3,2,1,0:T(8,128)(2,1)S(1)} collective-permute-done((bf16[2,2,64,768]{3,2,1,0:T(8,128)(2,1)S(1)}, bf16[2,2,64,768]{3,2,1,0:T(8,128)(2,1)S(1)}, u32[]{:S(2)}, u32[]{:S(2)}) %collective-permute-start.28) | collective-permute-done | bytes 393248 | tf_op jit(solution)/shard_map/ppermute | solution.py:33
  114.6 1.9 collective-permute-done.26
  120.3 1.7 collective-permute-start.31
  122.0 6.3 %backward.4 = (bf16[512,3328]{1,0:T(8,128)(2,1)}, bf16[512,3328]{1,0:T(8,128)(2,1)}, f32[1024,512]{1,0:T(8,128)S(1)}) custom-call(bf16[4,2,64,768]{3,2,1,0:T(8,128)(2,1)S(1)} %bitcast.138, bf16[6,2,64,768]{3,2,1,0:T(8,128)(2,1)S(1)} %bitcast.136, bf16[6,2,64,768]{3,2,1,0:T(8,128)(2,1)S(1)} %bitcast.140, bf16[512,1024]{1,0:T(8,128)(2,1)S(1)} %arrange_tokens.3.refs_3_.refs_4_, ...), custom_call_target="tpu_custom_call" | custom-call | flops 966367616 | bytes 3145728 | tf_op jit(solution)/shard_map/backward/pallas_call | solution.py:194
  128.3 2.2 %collective-permute-done.32 = bf16[2,2,2,64,768]{4,3,2,1,0:T(8,128)(2,1)S(1)} collective-permute-done((bf16[2,2,2,64,768]{4,3,2,1,0:T(8,128)(2,1)S(1)}, bf16[2,2,2,64,768]{4,3,2,1,0:T(8,128)(2,1)S(1)}, u32[]{:S(2)}, u32[]{:S(2)}) %collective-permute-start.32) | collective-permute-done | bytes 786464 | tf_op jit(solution)/shard_map/ppermute | solution.py:33
  130.8 11.2 %collective-permute-done.31.refs_1_ = bf16[4,2,64,768]{3,2,1,0:T(8,128)(2,1)S(1)} collective-permute-done((bf16[4,2,64,768]{3,2,1,0:T(8,128)(2,1)S(1)}, bf16[4,2,64,768]{3,2,1,0:T(8,128)(2,1)S(1)}, u32[]{:S(2)}, u32[]{:S(2)}) %collective-permute-start.31) | collective-permute-done | bytes 786464 | tf_op jit(solution)/shard_map/ppermute | solution.py:37
  142.3 3.7 %collective-permute-done.35 = bf16[2,2,64,768]{3,2,1,0:T(8,128)(2,1)S(1)} collective-permute-done((bf16[2,2,64,768]{3,2,1,0:T(8,128)(2,1)S(1)}, bf16[2,2,64,768]{3,2,1,0:T(8,128)(2,1)S(1)}, u32[]{:S(2)}, u32[]{:S(2)}) %collective-permute-start.35) | collective-permute-done | bytes 393248 | tf_op jit(solution)/shard_map/ppermute | solution.py:33
  146.4 6.3 %backward.5 = (bf16[512,3328]{1,0:T(8,128)(2,1)}, bf16[512,3328]{1,0:T(8,128)(2,1)}, f32[1024,512]{1,0:T(8,128)S(1)}) custom-call(bf16[4,2,64,768]{3,2,1,0:T(8,128)(2,1)S(1)} %pad_maximum_fusion.10.refs_0_, bf16[4,2,64,768]{3,2,1,0:T(8,128)(2,1)S(1)} %collective-permute-done.31.refs_1_, ...), custom_call_target="tpu_custom_call", output_to_operand_aliasing={{0}: (7, {}), {1}: (8, {})} | custom-call | flops 966367616 | bytes 3145728 | tf_op jit(solution)/shard_map/backward/pallas_call | solution.py:194
  154.1 2.5 %collective-permute-done.34 = bf16[2,2,64,1024]{3,2,1,0:T(8,128)(2,1)S(1)} collective-permute-done((bf16[2,2,64,1024]{3,2,1,0:T(8,128)(2,1)S(1)}, bf16[2,2,64,1024]{3,2,1,0:T(8,128)(2,1)S(1)}, u32[]{:S(2)}, u32[]{:S(2)}) %collective-permute-start.34) | collective-permute-done | bytes 524320 | tf_op jit(solution)/shard_map/ppermute | solution.py:33
  159.7 6.5 %backward.6 = (bf16[512,3328]{1,0:T(8,128)(2,1)}, bf16[512,3328]{1,0:T(8,128)(2,1)}, f32[1024,512]{1,0:T(8,128)S(1)}) custom-call(bf16[4,2,64,768]{3,2,1,0:T(8,128)(2,1)S(1)} %bitcast.137, bf16[6,2,64,768]{3,2,1,0:T(8,128)(2,1)S(1)} %bitcast.135, bf16[6,2,64,768]{3,2,1,0:T(8,128)(2,1)S(1)} %bitcast.139, ...), custom_call_target="tpu_custom_call", output_to_operand_aliasing={{0}: (6, {}), {1}: (7, {})} | custom-call | flops 966367616 | bytes 3145728 | tf_op jit(solution)/shard_map/backward/pallas_call | solution.py:194
  166.3 4.8 %split_rows.1 = (f32[128,512]{1,0:T(8,128)S(1)}, bf16[128,512]{1,0:T(8,128)(2,1)S(1)}, bf16[128,512]{1,0:T(8,128)(2,1)S(1)}, bf16[128,512]{1,0:T(8,128)(2,1)S(1)...) custom-call(s32[8,2]{1,0:T(8,128)S(1)} %copy.22.at_ref, ...), custom_call_target="tpu_custom_call" | custom-call | flops 644245120 | bytes 3774873 | tf_op jit(solution)/shard_map/split_rows/pallas_call | solution.py:228
  171.7 2.5 %collective-permute-start.41 = (bf16[128,512]{1,0:T(8,128)(2,1)S(1)}, bf16[128,512]{1,0:T(8,128)(2,1)S(1)}, u32[]{:S(2)}, u32[]{:S(2)}) collective-permute-start(bf16[128,512]{1,0:T(8,128)(2,1)S(1)} %get-tuple-element.258), channel_id=1, source_target_pairs={{0,32},{16,48},{32,0},{48,16},{64,96},{80,112},{96,64},{112,80},{1... | collective-permute-start | bytes 393224 | tf_op jit(solution)/shard_map/ppermute | solution.py:455
  175.0 2.4 %collective-permute-start.42 = (bf16[128,512]{1,0:T(8,128)(2,1)S(1)}, bf16[128,512]{1,0:T(8,128)(2,1)S(1)}, u32[]{:S(2)}, u32[]{:S(2)}) collective-permute-start(bf16[128,512]{1,0:T(8,128)(2,1)S(1)} %get-tuple-element.260), channel_id=1, source_target_pairs={{0,48},{16,0},{32,16},{48,32},{64,112},{80,64},{96,80},{112,96},{1... | collective-permute-start | bytes 393224 | tf_op jit(solution)/shard_map/ppermute | solution.py:455
  177.4 2.0 %collective-permute-start.43 = (bf16[128,512]{1,0:T(8,128)(2,1)S(1)}, bf16[128,512]{1,0:T(8,128)(2,1)S(1)}, u32[]{:S(2)}, u32[]{:S(2)}) collective-permute-start(bf16[128,512]{1,0:T(8,128)(2,1)S(1)} %get-tuple-element.261), channel_id=1, source_target_pairs={{0,64},{16,80},{32,96},{48,112},{64,0},{80,16},{96,32},{112,48},{1... | collective-permute-start | bytes 393224 | tf_op jit(solution)/shard_map/ppermute | solution.py:455
  180.0 2.4 %collective-permute-done.41 = bf16[128,512]{1,0:T(8,128)(2,1)S(1)} collective-permute-done((bf16[128,512]{1,0:T(8,128)(2,1)S(1)}, bf16[128,512]{1,0:T(8,128)(2,1)S(1)}, u32[]{:S(2)}, u32[]{:S(2)}) %collective-permute-start.41) | collective-permute-done | bytes 131104 | tf_op jit(solution)/shard_map/ppermute | solution.py:455
  182.4 1.7 collective-permute-start.45
  184.9 5.7 %backward.7 = (bf16[512,3328]{1,0:T(8,128)(2,1)}, bf16[512,3328]{1,0:T(8,128)(2,1)}) custom-call(bf16[4,2,64,1024]{3,2,1,0:T(8,128)(2,1)S(1)} %bitcast.134, bf16[6,2,64,1024]{3,2,1,0:T(8,128)(2,1)S(1)} %bitcast.132, bf16[6,2,64,1024]{3,2,1,0:T(8,128)(2,1)} %bitcast.93.refs_2_, ...), custom_call_target="tpu_custom_call", output_to_operand_aliasing={{0}: (6, {}), {1}: (7, {})} | custom-call | flops 644245120 | bytes 3774873 | tf_op jit(solution)/shard_map/backward/pallas_call | solution.py:194
  (178 shorter events, 43.2 us)
Async XLA Ops:
  0.6 28.5 %collective-permute-start.1 = (bf16[512,3328]{1,0:T(8,128)(2,1)}, bf16[512,3328]{1,0:T(8,128)(2,1)S(1)}, u32[]{:S(2)}, u32[]{:S(2)}) collective-permute-start(bf16[512,3328]{1,0:T(8,128)(2,1)} %refs_4_.7), channel_id=1, source_target_pairs={{0,1},{1,0},{2,3},{3,2},{4,5},{5,4},{6,7},{7,6},{8,9},{9,8},{10,11... | collective-permute-start | bytes 10223624 | tf_op jit(solution)/shard_map/ppermute | solution.py:41
  0.7 28.4 %collective-permute-start.2 = (bf16[512,3328]{1,0:T(8,128)(2,1)}, bf16[512,3328]{1,0:T(8,128)(2,1)}, u32[]{:S(2)}, u32[]{:S(2)}) collective-permute-start(bf16[512,3328]{1,0:T(8,128)(2,1)} %refs_5_.7), channel_id=1, source_target_pairs={{0,1},{1,0},{2,3},{3,2},{4,5},{5,4},{6,7},{7,6},{8,9},{9,8},{10,11... | collective-permute-start | bytes 10223624 | tf_op jit(solution)/shard_map/ppermute | solution.py:41
  33.0 9.1 %collective-permute-start.4 = (bf16[2,2,64,768]{3,2,1,0:T(8,128)(2,1)S(1)}, bf16[2,2,64,768]{3,2,1,0:T(8,128)(2,1)S(1)}, u32[]{:S(2)}, u32[]{:S(2)}) collective-permute-start(bf16[2,2,64,768]{3,2,1,0:T(8,128)(2,1)S(1)} %get-tuple-element.144), channel_id=1, source_target_pairs={{0,4},{1,13},{2,6},{3,15},{4,8},{5,1},{6,10},{7,3},{8,12},{9,5},{1... | collective-permute-start | bytes 1179656 | tf_op jit(solution)/shard_map/ppermute | solution.py:33
  38.4 11.0 %collective-permute-start.3 = (bf16[2,2,64,768]{3,2,1,0:T(8,128)(2,1)S(1)}, bf16[2,2,64,768]{3,2,1,0:T(8,128)(2,1)S(1)}, u32[]{:S(2)}, u32[]{:S(2)}) collective-permute-start(bf16[2,2,64,768]{3,2,1,0:T(8,128)(2,1)S(1)} %get-tuple-element.141), channel_id=1, source_target_pairs={{0,4},{1,13},{2,6},{3,15},{4,8},{5,1},{6,10},{7,3},{8,12},{9,5},{1... | collective-permute-start | bytes 1179656 | tf_op jit(solution)/shard_map/ppermute | solution.py:33
  42.2 14.8 %collective-permute-start.6 = (bf16[2,2,2,64,768]{4,3,2,1,0:T(8,128)(2,1)S(1)}, bf16[2,2,2,64,768]{4,3,2,1,0:T(8,128)(2,1)S(1)}, u32[]{:S(2)}, u32[]{:S(2)}) collective-permute-start(bf16[2,2,2,64,768]{4,3,2,1,0:T(8,128)(2,1)S(1)} %pad_maximum_fusion.6), channel_id=1, source_target_pairs={{0,4},{1,13},{2,6},{3,15},{4,8},{5,1},{6,10},{7,3},{8,12},{9,5},{1... | collective-permute-start | bytes 2359304 | tf_op jit(solution)/shard_map/ppermute | solution.py:33
  46.4 21.8 %collective-permute-start.9 = (bf16[4,2,64,768]{3,2,1,0:T(8,128)(2,1)S(1)}, bf16[4,2,64,768]{3,2,1,0:T(8,128)(2,1)S(1)}, u32[]{:S(2)}, u32[]{:S(2)}) collective-permute-start(bf16[4,2,64,768]{3,2,1,0:T(8,128)(2,1)S(1)} %get-tuple-element.160), channel_id=1, source_target_pairs={{0,2},{1,3},{2,0},{3,1},{4,6},{5,7},{6,4},{7,5},{8,10},{9,11},{10,... | collective-permute-start | bytes 2359304 | tf_op jit(solution)/shard_map/ppermute | solution.py:37
  49.6 19.0 %collective-permute-start.8 = (bf16[2,2,2,64,768]{4,3,2,1,0:T(8,128)(2,1)S(1)}, bf16[2,2,2,64,768]{4,3,2,1,0:T(8,128)(2,1)S(1)}, u32[]{:S(2)}, u32[]{:S(2)}) collective-permute-start(bf16[2,2,2,64,768]{4,3,2,1,0:T(8,128)(2,1)S(1)} %pad_maximum_fusion.7), channel_id=1, source_target_pairs={{0,4},{1,13},{2,6},{3,15},{4,8},{5,1},{6,10},{7,3},{8,12},{9,5},{1... | collective-permute-start | bytes 2359304 | tf_op jit(solution)/shard_map/ppermute | solution.py:33
  55.8 18.0 %collective-permute-start.5 = (bf16[2,2,64,1024]{3,2,1,0:T(8,128)(2,1)S(1)}, bf16[2,2,64,1024]{3,2,1,0:T(8,128)(2,1)S(1)}, u32[]{:S(2)}, u32[]{:S(2)}) collective-permute-start(bf16[2,2,64,1024]{3,2,1,0:T(8,128)(2,1)S(1)} %get-tuple-element.155), channel_id=1, source_target_pairs={{0,4},{1,13},{2,6},{3,15},{4,8},{5,1},{6,10},{7,3},{8,12},{9,5},{1... | collective-permute-start | bytes 1572872 | tf_op jit(solution)/shard_map/ppermute | solution.py:33
  57.1 13.3 %collective-permute-start.7 = (bf16[2,2,64,768]{3,2,1,0:T(8,128)(2,1)S(1)}, bf16[2,2,64,768]{3,2,1,0:T(8,128)(2,1)S(1)}, u32[]{:S(2)}, u32[]{:S(2)}) collective-permute-start(bf16[2,2,64,768]{3,2,1,0:T(8,128)(2,1)S(1)} %slice_bitcast_fusion.10), channel_id=1, source_target_pairs={{0,1},{1,0},{2,3},{3,2},{4,5},{5,4},{6,7},{7,6},{8,9},{9,8},{10,11... | collective-permute-start | bytes 1179656 | tf_op jit(solution)/shard_map/ppermute | solution.py:41
  68.5 14.4 %collective-permute-start.15 = (bf16[2,64,768]{2,1,0:T(8,128)(2,1)S(1)}, bf16[2,64,768]{2,1,0:T(8,128)(2,1)S(1)}, u32[]{:S(2)}, u32[]{:S(2)}) collective-permute-start(bf16[2,64,768]{2,1,0:T(8,128)(2,1)S(1)} %get-tuple-element.277), channel_id=1, source_target_pairs={{0,4},{1,13},{2,6},{3,15},{4,8},{5,1},{6,10},{7,3},{8,12},{9,5},{1... | collective-permute-start | bytes 589832 | tf_op jit(solution)/shard_map/ppermute | solution.py:33
  74.1 16.1 %collective-permute-start.10 = (bf16[2,2,2,64,1024]{4,3,2,1,0:T(8,128)(2,1)S(1)}, bf16[2,2,2,64,1024]{4,3,2,1,0:T(8,128)(2,1)S(1)}, u32[]{:S(2)}, u32[]{:S(2)}) collective-permute-start(bf16[2,2,2,64,1024]{4,3,2,1,0:T(8,128)(2,1)S(1)} %pad_maximum_fusion.4), channel_id=1, source_target_pairs={{0,4},{1,13},{2,6},{3,15},{4,8},{5,1},{6,10},{7,3},{8,12},{9,5},{1... | collective-permute-start | bytes 3145736 | tf_op jit(solution)/shard_map/ppermute | solution.py:33
  76.1 13.7 %collective-permute-start.12 = (bf16[2,64,768]{2,1,0:T(8,128)(2,1)S(1)}, bf16[2,64,768]{2,1,0:T(8,128)(2,1)S(1)}, u32[]{:S(2)}, u32[]{:S(2)}) collective-permute-start(bf16[2,64,768]{2,1,0:T(8,128)(2,1)S(1)} %fusion.9), channel_id=1, source_target_pairs={{0,2},{1,3},{2,0},{3,1},{4,6},{5,7},{6,4},{7,5},{8,10},{9,11},{10,... | collective-permute-start | bytes 589832 | tf_op jit(solution)/shard_map/ppermute | solution.py:37
  79.6 9.9 %collective-permute-start.14 = (bf16[2,64,768]{2,1,0:T(8,128)(2,1)S(1)}, bf16[2,64,768]{2,1,0:T(8,128)(2,1)S(1)}, u32[]{:S(2)}, u32[]{:S(2)}) collective-permute-start(bf16[2,64,768]{2,1,0:T(8,128)(2,1)S(1)} %get-tuple-element.181), channel_id=1, source_target_pairs={{0,2},{1,3},{2,0},{3,1},{4,6},{5,7},{6,4},{7,5},{8,10},{9,11},{10,... | collective-permute-start | bytes 589832 | tf_op jit(solution)/shard_map/ppermute | solution.py:37
  82.9 11.5 %collective-permute-start.17 = (bf16[2,2,64,768]{3,2,1,0:T(8,128)(2,1)S(1)}, bf16[2,2,64,768]{3,2,1,0:T(8,128)(2,1)S(1)}, u32[]{:S(2)}, u32[]{:S(2)}) collective-permute-start(bf16[2,2,64,768]{3,2,1,0:T(8,128)(2,1)S(1)} %pad_maximum_fusion.13), channel_id=1, source_target_pairs={{0,4},{1,13},{2,6},{3,15},{4,8},{5,1},{6,10},{7,3},{8,12},{9,5},{1... | collective-permute-start | bytes 1179656 | tf_op jit(solution)/shard_map/ppermute | solution.py:33
  90.5 14.8 %collective-permute-start.25 = (bf16[2,64,768]{2,1,0:T(8,128)(2,1)S(1)}, bf16[2,64,768]{2,1,0:T(8,128)(2,1)S(1)}, u32[]{:S(2)}, u32[]{:S(2)}) collective-permute-start(bf16[2,64,768]{2,1,0:T(8,128)(2,1)S(1)} %get-tuple-element.208), channel_id=1, source_target_pairs={{0,2},{1,3},{2,0},{3,1},{4,6},{5,7},{6,4},{7,5},{8,10},{9,11},{10,... | collective-permute-start | bytes 589832 | tf_op jit(solution)/shard_map/ppermute | solution.py:37
  92.0 13.3 %collective-permute-start.24 = (bf16[2,2,2,64,768]{4,3,2,1,0:T(8,128)(2,1)S(1)}, bf16[2,2,2,64,768]{4,3,2,1,0:T(8,128)(2,1)S(1)}, u32[]{:S(2)}, u32[]{:S(2)}) collective-permute-start(bf16[2,2,2,64,768]{4,3,2,1,0:T(8,128)(2,1)S(1)} %pad_maximum_fusion.8), channel_id=1, source_target_pairs={{0,4},{1,13},{2,6},{3,15},{4,8},{5,1},{6,10},{7,3},{8,12},{9,5},{1... | collective-permute-start | bytes 2359304 | tf_op jit(solution)/shard_map/ppermute | solution.py:33
  95.2 9.9 %collective-permute-start.19 = (bf16[2,64,1024]{2,1,0:T(8,128)(2,1)S(1)}, bf16[2,64,1024]{2,1,0:T(8,128)(2,1)S(1)}, u32[]{:S(2)}, u32[]{:S(2)}) collective-permute-start(bf16[2,64,1024]{2,1,0:T(8,128)(2,1)S(1)} %fusion.6), channel_id=1, source_target_pairs={{0,2},{1,3},{2,0},{3,1},{4,6},{5,7},{6,4},{7,5},{8,10},{9,11},{10,... | collective-permute-start | bytes 786440 | tf_op jit(solution)/shard_map/ppermute | solution.py:37
  98.1 11.4 %collective-permute-start.23 = (bf16[2,2,64,768]{3,2,1,0:T(8,128)(2,1)S(1)}, bf16[2,2,64,768]{3,2,1,0:T(8,128)(2,1)S(1)}, u32[]{:S(2)}, u32[]{:S(2)}) collective-permute-start(bf16[2,2,64,768]{3,2,1,0:T(8,128)(2,1)S(1)} %pad_maximum_fusion.15), channel_id=1, source_target_pairs={{0,4},{1,13},{2,6},{3,15},{4,8},{5,1},{6,10},{7,3},{8,12},{9,5},{1... | collective-permute-start | bytes 1179656 | tf_op jit(solution)/shard_map/ppermute | solution.py:33
  105.4 9.1 %collective-permute-start.28 = (bf16[2,2,64,768]{3,2,1,0:T(8,128)(2,1)S(1)}, bf16[2,2,64,768]{3,2,1,0:T(8,128)(2,1)S(1)}, u32[]{:S(2)}, u32[]{:S(2)}) collective-permute-start(bf16[2,2,64,768]{3,2,1,0:T(8,128)(2,1)S(1)} %slice_bitcast_fusion.8), channel_id=1, source_target_pairs={{0,4},{1,13},{2,6},{3,15},{4,8},{5,1},{6,10},{7,3},{8,12},{9,5},{1... | collective-permute-start | bytes 1179656 | tf_op jit(solution)/shard_map/ppermute | solution.py:33
  106.9 9.7 %collective-permute-start.22 = (bf16[2,64,1024]{2,1,0:T(8,128)(2,1)S(1)}, bf16[2,64,1024]{2,1,0:T(8,128)(2,1)S(1)}, u32[]{:S(2)}, u32[]{:S(2)}) collective-permute-start(bf16[2,64,1024]{2,1,0:T(8,128)(2,1)S(1)} %get-tuple-element.219), channel_id=1, source_target_pairs={{0,2},{1,3},{2,0},{3,1},{4,6},{5,7},{6,4},{7,5},{8,10},{9,11},{10,... | collective-permute-start | bytes 786440 | tf_op jit(solution)/shard_map/ppermute | solution.py:37
  117.3 13.2 %collective-permute-start.32 = (bf16[2,2,2,64,768]{4,3,2,1,0:T(8,128)(2,1)S(1)}, bf16[2,2,2,64,768]{4,3,2,1,0:T(8,128)(2,1)S(1)}, u32[]{:S(2)}, u32[]{:S(2)}) collective-permute-start(bf16[2,2,2,64,768]{4,3,2,1,0:T(8,128)(2,1)S(1)} %pad_maximum_fusion.9), channel_id=1, source_target_pairs={{0,4},{1,13},{2,6},{3,15},{4,8},{5,1},{6,10},{7,3},{8,12},{9,5},{1... | collective-permute-start | bytes 2359304 | tf_op jit(solution)/shard_map/ppermute | solution.py:33
  118.8 23.4 %collective-permute-start.30 = (bf16[2,2,2,64,1024]{4,3,2,1,0:T(8,128)(2,1)S(1)}, bf16[2,2,2,64,1024]{4,3,2,1,0:T(8,128)(2,1)S(1)}, u32[]{:S(2)}, u32[]{:S(2)}) collective-permute-start(bf16[2,2,2,64,1024]{4,3,2,1,0:T(8,128)(2,1)S(1)} %pad_maximum_fusion.5), channel_id=1, source_target_pairs={{0,4},{1,13},{2,6},{3,15},{4,8},{5,1},{6,10},{7,3},{8,12},{9,5},{1... | collective-permute-start | bytes 3145736 | tf_op jit(solution)/shard_map/ppermute | solution.py:33
  120.3 21.7 %collective-permute-start.31 = (bf16[4,2,64,768]{3,2,1,0:T(8,128)(2,1)S(1)}, bf16[4,2,64,768]{3,2,1,0:T(8,128)(2,1)S(1)}, u32[]{:S(2)}, u32[]{:S(2)}) collective-permute-start(bf16[4,2,64,768]{3,2,1,0:T(8,128)(2,1)S(1)} %pad_maximum_fusion.10.refs_0_), channel_id=1, source_target_pairs={{0,2},{1,3},{2,0},{3,1},{4,6},{5,7},{6,4},{7,5},{8,10},{9,11},{10,... | collective-permute-start | bytes 2359304 | tf_op jit(solution)/shard_map/ppermute | solution.py:37
  130.5 15.4 %collective-permute-start.35 = (bf16[2,2,64,768]{3,2,1,0:T(8,128)(2,1)S(1)}, bf16[2,2,64,768]{3,2,1,0:T(8,128)(2,1)S(1)}, u32[]{:S(2)}, u32[]{:S(2)}) collective-permute-start(bf16[2,2,64,768]{3,2,1,0:T(8,128)(2,1)S(1)} %slice_bitcast_fusion.7), channel_id=1, source_target_pairs={{0,4},{1,13},{2,6},{3,15},{4,8},{5,1},{6,10},{7,3},{8,12},{9,5},{1... | collective-permute-start | bytes 1179656 | tf_op jit(solution)/shard_map/ppermute | solution.py:33
  146.2 10.5 %collective-permute-start.34 = (bf16[2,2,64,1024]{3,2,1,0:T(8,128)(2,1)S(1)}, bf16[2,2,64,1024]{3,2,1,0:T(8,128)(2,1)S(1)}, u32[]{:S(2)}, u32[]{:S(2)}) collective-permute-start(bf16[2,2,64,1024]{3,2,1,0:T(8,128)(2,1)S(1)} %slice_bitcast_fusion.1), channel_id=1, source_target_pairs={{0,4},{1,13},{2,6},{3,15},{4,8},{5,1},{6,10},{7,3},{8,12},{9,5},{1... | collective-permute-start | bytes 1572872 | tf_op jit(solution)/shard_map/ppermute | solution.py:33
  156.8 9.4 %collective-permute-start.38 = (bf16[3,2,2,64,1024]{4,3,2,1,0:T(8,128)(2,1)S(1)}, bf16[3,2,2,64,1024]{4,3,2,1,0:T(8,128)(2,1)}, u32[]{:S(2)}, u32[]{:S(2)}) collective-permute-start(bf16[3,2,2,64,1024]{4,3,2,1,0:T(8,128)(2,1)S(1)} %pad_maximum_fusion), channel_id=1, source_target_pairs={{0,1},{1,0},{2,3},{3,2},{4,5},{5,4},{6,7},{7,6},{8,9},{9,8},{10,11... | collective-permute-start | bytes 4718600 | tf_op jit(solution)/shard_map/ppermute | solution.py:41
  171.1 8.9 %collective-permute-start.40 = (bf16[128,512]{1,0:T(8,128)(2,1)S(1)}, bf16[128,512]{1,0:T(8,128)(2,1)S(1)}, u32[]{:S(2)}, u32[]{:S(2)}) collective-permute-start(bf16[128,512]{1,0:T(8,128)(2,1)S(1)} %get-tuple-element.257), channel_id=1, source_target_pairs={{0,96},{16,112},{32,64},{48,80},{64,32},{80,48},{96,0},{112,16},{1... | collective-permute-start | bytes 393224 | tf_op jit(solution)/shard_map/ppermute | solution.py:455
  171.7 10.7 %collective-permute-start.41 = (bf16[128,512]{1,0:T(8,128)(2,1)S(1)}, bf16[128,512]{1,0:T(8,128)(2,1)S(1)}, u32[]{:S(2)}, u32[]{:S(2)}) collective-permute-start(bf16[128,512]{1,0:T(8,128)(2,1)S(1)} %get-tuple-element.258), channel_id=1, source_target_pairs={{0,32},{16,48},{32,0},{48,16},{64,96},{80,112},{96,64},{112,80},{1... | collective-permute-start | bytes 393224 | tf_op jit(solution)/shard_map/ppermute | solution.py:455
  174.2 16.5 %collective-permute-start.39 = (bf16[128,512]{1,0:T(8,128)(2,1)S(1)}, bf16[128,512]{1,0:T(8,128)(2,1)S(1)}, u32[]{:S(2)}, u32[]{:S(2)}) collective-permute-start(bf16[128,512]{1,0:T(8,128)(2,1)S(1)} %get-tuple-element.256), channel_id=1, source_target_pairs={{0,16},{16,32},{32,48},{48,0},{64,80},{80,96},{96,112},{112,64},{1... | collective-permute-start | bytes 393224 | tf_op jit(solution)/shard_map/ppermute | solution.py:455
  175.0 15.6 %collective-permute-start.42 = (bf16[128,512]{1,0:T(8,128)(2,1)S(1)}, bf16[128,512]{1,0:T(8,128)(2,1)S(1)}, u32[]{:S(2)}, u32[]{:S(2)}) collective-permute-start(bf16[128,512]{1,0:T(8,128)(2,1)S(1)} %get-tuple-element.260), channel_id=1, source_target_pairs={{0,48},{16,0},{32,16},{48,32},{64,112},{80,64},{96,80},{112,96},{1... | collective-permute-start | bytes 393224 | tf_op jit(solution)/shard_map/ppermute | solution.py:455
  177.4 13.2 %collective-permute-start.43 = (bf16[128,512]{1,0:T(8,128)(2,1)S(1)}, bf16[128,512]{1,0:T(8,128)(2,1)S(1)}, u32[]{:S(2)}, u32[]{:S(2)}) collective-permute-start(bf16[128,512]{1,0:T(8,128)(2,1)S(1)} %get-tuple-element.261), channel_id=1, source_target_pairs={{0,64},{16,80},{32,96},{48,112},{64,0},{80,16},{96,32},{112,48},{1... | collective-permute-start | bytes 393224 | tf_op jit(solution)/shard_map/ppermute | solution.py:455
  180.0 10.7 %collective-permute-start.44 = (bf16[128,512]{1,0:T(8,128)(2,1)S(1)}, bf16[128,512]{1,0:T(8,128)(2,1)S(1)}, u32[]{:S(2)}, u32[]{:S(2)}) collective-permute-start(bf16[128,512]{1,0:T(8,128)(2,1)S(1)} %get-tuple-element.262), channel_id=1, source_target_pairs={{0,80},{16,96},{32,112},{48,64},{64,16},{80,32},{96,48},{112,0},{1... | collective-permute-start | bytes 393224 | tf_op jit(solution)/shard_map/ppermute | solution.py:455
  (31 other events, 213.7 us)

commit v4 on v3

--- a/solution.py
+++ b/solution.py
@@ -10,9 +10,10 @@
 F32, BF16 = jnp.float32, jnp.bfloat16
 TILE = 256
 CHUNKS = (('b', 3), ('a', 4), ('a', 3), ('a', 3))
-ORDER = ((2, 'f'), (3, 'f'), (2, 'a1'), (0, 'f'), (3, 'a1'), (1, 'f'), (2, 'ac'), (0, 'b1'), (3, 'ac'), (2, 'a2'), (1, 'a1'), (3, 'a2'), (2, 'g'), (0, 'b2'), (2, 'b1'), (3, 'g'), (1, 'ac'), (2, 'b2'), (0, 'bc'), (1, 'a2'), (0, 'g'), (0, 'c1'), (1, 'g'), (3, 'b1'), (2, 'b3'), (0, 'c2'), (2, 'b4'), (3, 'b2'), (0, 'c3'), (1, 'b1'), (1, 'b2'), (2, 'd'), (2, 'K'), (3, 'b3'), (0, 'c4'), (1, 'b3'), (3, 'b4'), (0, 'd'), (0, 'K'), (3, 'd'), (1, 'b4'), (3, 'K'), (1, 'd'), (1, 'Ky'), (1, 'Kw'))
+ORDER = ((2, 'f'), (3, 'f'), (0, 'f'), (2, 'a1'), (3, 'a1'), (1, 'f'), (0, 'b1'), (2, 'ac'), (3, 'ac'), (2, 'a2'), (1, 'a1'), (3, 'a2'), (2, 'g'), (0, 'b2'), (2, 'b1'), (3, 'g'), (1, 'ac'), (2, 'b2'), (0, 'bc'), (1, 'a2'), (0, 'g'), (0, 'c1'), (1, 'g'), (3, 'b1'), (2, 'b3'), (0, 'c2'), (2, 'b4'), (3, 'b2'), (0, 'c3'), (1, 'b1'), (1, 'b2'), (2, 'd'), (2, 'K'), (3, 'b3'), (0, 'c4'), (1, 'b3'), (3, 'b4'), (0, 'd'), (0, 'K'), (3, 'd'), (1, 'b4'), (3, 'K'), (1, 'd'), (1, 'Ky'), (1, 'Kw'))
 MIB = 1 << 20
-COST = {'f': 0, 'g': 0.001, 'k': 0.3}
+APART = ()
+COST = {'f': 0, 'g': 0.001, 'k': 0.001}
 
 
 def column(x, y, core):
@@ -177,12 +178,16 @@
 
 
 def backward(first, tiles, pieces, table, xt, gate, lift, grads, with_y):
-    n = TILE
-    wide = pl.BlockSpec((512, n), lambda j: (0, first + j))
+    once = first % tiles == 0
+    n = tiles * TILE if once else TILE
+    mode = dict(pipeline_mode=pl.Buffered(1)) if once else {}
+    wide = pl.BlockSpec((512, n), lambda j: (0, first // tiles if once else first + j), **mode)
     args = [*pieces, xt, gate, lift]
-    specs = [pl.BlockSpec((v.shape[0], 2, 64, n), lambda j: (0, 0, 0, j)) for v in pieces]
+    specs = [pl.BlockSpec((v.shape[0], 2, 64, n), lambda j: (0, 0, 0, j), **mode) for v in pieces]
     specs += [whole(xt.shape), wide, wide]
-    alias, shapes, out_specs = {}, [jax.ShapeDtypeStruct(gate.shape, BF16)] * 2, [wide, wide]
+    alias, shapes = {}, [jax.ShapeDtypeStruct(gate.shape, BF16)] * 2
+    column = pl.BlockSpec((512, n), lambda j: (0, first // tiles if once else first + j))
+    out_specs = [column, column]
     if with_y:
         shapes.append(jax.ShapeDtypeStruct((1024, 512), F32))
         out_specs.append(pl.BlockSpec((1024, 512), lambda j: (0, 0)))
@@ -196,20 +201,20 @@
         out_shape=tuple(shapes),
         in_specs=specs,
         out_specs=tuple(out_specs),
-        grid=(tiles,),
+        grid=(1 if once else tiles,),
         input_output_aliases=alias,
-        compiler_params=params(16),
+        compiler_params=params(28 if once else 16),
         cost_estimate=cost("k", (1 + with_y) * 4 * 512 * 1024 * n * tiles, 8 * 1024 * n * tiles + 4 * MIB),
         name="backward",
     )(*args)
 
 
-def split_kernel(arrays, table, others, at_ref, *refs):
-    held, (gate_ref, lift_ref) = refs[:arrays], refs[arrays : arrays + 2]
-    y_refs, outs = refs[arrays + 2 : arrays + 2 + others], refs[arrays + 2 + others : -1]
+def split_kernel(arrays, table, tiles, others, at_ref, *refs):
+    held, w_refs = refs[:arrays], refs[arrays : arrays + 2 * tiles]
+    y_refs, outs = refs[arrays + 2 * tiles :][:others], refs[arrays + 2 * tiles + others : -1]
     total_ref = refs[-1]
     grad = jnp.concatenate([tokens(held, table, m) for m in range(2)], axis=1)
-    weight = jnp.concatenate([gate_ref[...], lift_ref[...]], axis=1)
+    weight = jnp.concatenate([ref[...] for ref in w_refs], axis=1)
     total = lax.dot_general(grad, weight, (((1,), (1,)), ((), ())), preferred_element_type=F32)
     for ref in y_refs:
         total = total + ref[...]
@@ -221,24 +226,24 @@
 
 
 def split(at, first, tiles, pieces, table, gate, lift, ys):
-    assert first % tiles == 0
     n = tiles * TILE
     kinds = [F32] + [BF16] * 7
-    w = pl.BlockSpec((256, n), lambda j: (j, first // tiles))
+    w = [pl.BlockSpec((256, TILE), lambda j, t=t: (j, first + t)) for t in range(tiles)]
     return pl.pallas_call(
-        functools.partial(split_kernel, len(pieces), table, len(ys)),
+        functools.partial(split_kernel, len(pieces), table, tiles, len(ys)),
         out_shape=tuple(jax.ShapeDtypeStruct((128, 512), t) for t in kinds),
         in_specs=[SMEM]
         + [whole(v.shape) for v in pieces]
-        + [w, w]
+        + w
+        + w
         + [pl.BlockSpec((1024, 256), lambda j: (0, j))] * len(ys),
         out_specs=tuple(pl.BlockSpec((128, 256), lambda j: (0, j)) for _ in kinds),
         scratch_shapes=[pltpu.VMEM((1024, 256), F32)],
         grid=(2,),
-        compiler_params=params(20),
+        compiler_params=params(24),
         cost_estimate=cost("k", 4 * 512 * 1024 * n, 8 * 1024 * n + 4 * MIB),
         name="split_rows",
-    )(at, *pieces, gate, lift, *ys)
+    )(at, *pieces, *[gate] * tiles, *[lift] * tiles, *ys)
 
 
 class Sequence:
@@ -254,7 +259,7 @@
         self.last = value
 
 
-def x_first(seq, first, tiles, use):
+def x_first(seq, first, tiles, use, apart):
     s = {}
     n = tiles * TILE
 
@@ -292,23 +297,34 @@
         own, other = seq(s["own"], s["other"])
         s["own"] = jnp.stack([own, other])
         seq.done(s["own"])
+        if apart:
+            s["near_k"] = over_x(s["own"])
         s["sib"] = over_core(s["own"])
 
     def spread_x():
         own, sib = seq(s["own"], s["sib"])
         s["full"] = jnp.stack([own, sib])
         seq.done(s["full"])
-        s["near"] = over_x(s["full"])
+        if apart:
+            s["near_o"] = over_x(sib)
+        else:
+            s["near"] = over_x(s["full"])
 
     def pass_on():
-        s["near"] = seq(s["near"])
-        far = s["near"][0]
+        if apart:
+            far = s["near_k"] = seq(s["near_k"])
+        else:
+            s["near"] = seq(s["near"])
+            far = s["near"][0]
         seq.done(far)
         s["far"] = over_x(far)
 
     def swap_near():
-        near, far = seq(s["near"], s["far"])
-        s["held"] = jnp.concatenate([near, far[None]])
+        if apart:
+            s["held"] = jnp.stack(seq(s["near_k"], s["near_o"], s["far"]))
+        else:
+            near, far = seq(s["near"], s["far"])
+            s["held"] = jnp.concatenate([near, far[None]])
         seq.done(s["held"])
         s["swapped"] = over_core(s["held"])
 
@@ -327,7 +343,7 @@
     )
 
 
-def y_first(seq, first, tiles, use):
+def y_first(seq, first, tiles, use, apart):
     s = {}
 
     def products():
@@ -359,23 +375,35 @@
         own, near, other = seq(s["own"], s["near"], s["other"])
         use["gated"][first], s["own"] = gating(first, tiles, [own, near[0], other], use["cot"])
         seq.done(s["own"])
+        if apart:
+            s["near_k"] = over_x(s["own"])
         s["sib"] = over_core(s["own"])
 
     def spread_x():
         own, s["sib"] = seq(s["own"], s["sib"])
-        full = jnp.stack([own, s["sib"]])
-        seq.done(full)
-        s["near"] = over_x(full)
+        if apart:
+            seq.done(s["sib"])
+            s["near_o"] = over_x(s["sib"])
+        else:
+            full = jnp.stack([own, s["sib"]])
+            seq.done(full)
+            s["near"] = over_x(full)
 
     def pass_on():
-        s["near"] = seq(s["near"])
-        far = s["near"][0]
+        if apart:
+            far = s["near_k"] = seq(s["near_k"])
+        else:
+            s["near"] = seq(s["near"])
+            far = s["near"][0]
         seq.done(far)
         s["far"] = over_x(far)
 
     def collect():
-        own, near, far = seq(s["own"], s["near"], s["far"])
-        s["here"] = jnp.concatenate([own[None], near, far[None]])
+        if apart:
+            s["here"] = jnp.stack(seq(s["own"], s["near_k"], s["near_o"], s["far"]))
+        else:
+            own, near, far = seq(s["own"], s["near"], s["far"])
+            s["here"] = jnp.concatenate([own[None], near, far[None]])
         seq.done(s["here"])
         s["there"] = over_y(s["here"])
 
@@ -433,10 +461,10 @@
     weights = (own_gate, sib_gate, own_lift, sib_lift)
     use = dict(lhs=lhs, weights=weights, cot=out_cotangent, gated={})
     seq = Sequence()
-    steps, spans, last = [], [], ORDER[-1][0]
+    steps, spans = [], []
     for i, (path, tiles) in enumerate(CHUNKS):
-        first = sum(t for j, (_, t) in enumerate(CHUNKS) if (j != last, t, j) < (i != last, tiles, i))
-        steps.append((x_first if path == "a" else y_first)(seq, first, tiles, use))
+        first = sum(t for j, (_, t) in enumerate(CHUNKS) if (t, j) < (tiles, i))
+        steps.append((x_first if path == "a" else y_first)(seq, first, tiles, use, i in APART))
         spans.append((first, tiles))
 
     grads, ys, xt = None, [], None
@@ -446,6 +474,9 @@
             seq.done(xt)
         if step[0] != "K":
             steps[i][step]()
+            if step == "g" and len(use["gated"]) == len(CHUNKS):
+                gated = jnp.concatenate([use["gated"][first] for first in sorted(use["gated"])], axis=1)
+                seq.done(gated)
             continue
         pieces = seq(*steps[i]["pieces"]())
         table = steps[i]["table"]
@@ -464,7 +495,6 @@
     total = parts[0]
     for i in range(1, 8):
         total = total + got[i].astype(F32)
-    gated = jnp.concatenate([use["gated"][first] for first in sorted(use["gated"])], axis=1)
     return (gated, total.astype(BF16), grads[0], grads[1])
 
 

time: 192 us -> 191 us (level)
  waiting for transfers between devices: 60.4 us -> 73.9 us
  starting transfers between devices: 46.6 us -> 35.7 us
  Pallas kernels: 49.6 us -> 46.9 us
    ppermute x16, waiting for transfers between devices: 18.9 us -> 30.7 us  [over_x(): return lax.ppermute(v, 'col', ALONG_X)]
    ppermute x16, starting transfers between devices: 16.8 us -> 9.42 us  [over_x(): return lax.ppermute(v, 'col', ALONG_X)]
    ppermute x8, starting transfers between devices: 16 us -> 13.1 us  [over_y(): return lax.ppermute(v, 'col', ALONG_Y)]
    pallas_call x4, Pallas kernels: 24.8 us -> 22 us  [backward(): pl.pallas_call(functools.partial(backward_kernel, len(pieces), table, wit...]
    unnamed x34 -> x27, local copies, waits for them, and re-layouts: 3.97 us -> 3.71 us
  transfers between devices with their start and end apart: 46 -> 46, of which waited for: 18 -> 22; matrix products, arithmetic and copies ran while one was open for 3% -> 3% of each run, Pallas kernels for 21% -> 20%
where the time goes in v4:
time: 191 us; the launch traced here: 190 us
  waiting for transfers between devices  73.9 us (39%)
  Pallas kernels  46.9 us (25%)
  starting transfers between devices  35.7 us (19%)
  blocking collectives  22.3 us (12%)
  local copies, waits for them, and re-layouts  6.39 us (3%)
  other arithmetic  3.78 us (2%)
    ppermute x8, waiting for transfers between devices, over_y(): return lax.ppermute(v, 'col', ALONG_Y)  35.9 us
    ppermute x16, waiting for transfers between devices, over_x(): return lax.ppermute(v, 'col', ALONG_X)  30.7 us
    all_to_all x1, blocking collectives, body(): lax.all_to_all(jnp.broadcast_to(inputs[None], (8, 128, 512)), 'row', 0, 0)  22.3 us
    pallas_call x4, Pallas kernels, backward(): pl.pallas_call(functools.partial(backward_kernel, len(pieces), table, wit...  22 us
    pallas_call x4, Pallas kernels, forward(): pl.pallas_call(functools.partial(forward_kernel, path), out_shape=tuple((...  16.2 us
    ppermute x8, starting transfers between devices, over_y(): return lax.ppermute(v, 'col', ALONG_Y)  13.1 us
    ppermute x7, starting transfers between devices, body(): lax.ppermute(parts[i], 'row', row_step(i))  10.1 us
    ppermute x16, starting transfers between devices, over_x(): return lax.ppermute(v, 'col', ALONG_X)  9.42 us
  transfers between devices with their start and end apart: 46, of which 22 were waited for; matrix products, arithmetic and copies ran while one was open for 3% of the time, Pallas kernels for 20%

profile of v4, /device:TPU:0, one launch (start us, length us, event | category | flops | bytes accessed | tf_op | source)
XLA Modules:
  0.0 190.3 jit_solution(7001891920676502000)
XLA Ops:
  2.2 22.3 %all_to_all.5.own_ref = bf16[8,128,512]{2,1,0:T(8,128)(2,1)} all-to-all(bf16[8,128,512]{2,1,0:T(8,128)(2,1)S(1)} %broadcast_in_dim.22), channel_id=1, replica_groups=mesh['row'=8,'col'=16] {'row'}, dimensions={0} | all-to-all | bytes 2097152 | tf_op jit(solution)/shard_map/all_to_all | solution.py:436
  29.2 3.9 %forward_a.3 = (bf16[2,2,64,768]{3,2,1,0:T(8,128)(2,1)S(1)}, bf16[2,2,64,768]{3,2,1,0:T(8,128)(2,1)S(1)}, f32[2,2,64,768]{3,2,1,0:T(8,128)S(1)}, f32[2,2,64,768]{3,2,1,0:T(8,128)S(1)}) custom-call(bf16[512,1024]{1,0:T(8,128)(2,1)S(1)} %arrange_tokens.2.lhs_ref, bf16[512,3328]{1,0:T(8,128)(2,1)} %refs_4_.7, ...), custom_call_target="tpu_custom_call" | custom-call | tf_op jit(solution)/shard_map/forward_a/pallas_call | solution.py:116
  34.6 3.8 %forward_a.4 = (bf16[2,2,64,768]{3,2,1,0:T(8,128)(2,1)S(1)}, bf16[2,2,64,768]{3,2,1,0:T(8,128)(2,1)S(1)}, f32[2,2,64,768]{3,2,1,0:T(8,128)S(1)}, f32[2,2,64,768]{3,2,1,0:T(8,128)S(1)}) custom-call(bf16[512,1024]{1,0:T(8,128)(2,1)S(1)} %arrange_tokens.2.lhs_ref, bf16[512,3328]{1,0:T(8,128)(2,1)} %refs_4_.7, ...), custom_call_target="tpu_custom_call" | custom-call | tf_op jit(solution)/shard_map/forward_a/pallas_call | solution.py:116
  40.0 3.8 %forward_b.1 = (f32[4,2,64,768]{3,2,1,0:T(8,128)S(1)}, bf16[4,2,64,768]{3,2,1,0:T(8,128)(2,1)S(1)}) custom-call(bf16[512,1024]{1,0:T(8,128)(2,1)S(1)} %arrange_tokens.2.lhs_ref, bf16[512,3328]{1,0:T(8,128)(2,1)} %refs_4_.7, bf16[512,3328]{1,0:T(8,128)(2,1)S(1)} %collective-permute-done.1.gs_ref, bf16[512,3328]{1,0:T(8,128)(2,1)} %refs_5_.9, ...), custom_call_target="tpu_custom_call" | custom-call | tf_op jit(solution)/shard_map/forward_b/pallas_call | solution.py:116
  43.8 3.0 %collective-permute-start.3 = (bf16[4,2,64,768]{3,2,1,0:T(8,128)(2,1)S(1)}, bf16[4,2,64,768]{3,2,1,0:T(8,128)(2,1)S(1)}, u32[]{:S(2)}, u32[]{:S(2)}) collective-permute-start(bf16[4,2,64,768]{3,2,1,0:T(8,128)(2,1)S(1)} %get-tuple-element.144), channel_id=1, source_target_pairs={{0,2},{1,3},{2,0},{3,1},{4,6},{5,7},{6,4},{7,5},{8,10},{9,11},{10,... | collective-permute-start | bytes 2359304 | tf_op jit(solution)/shard_map/ppermute | solution.py:38
  48.9 4.7 %forward_a.5 = (bf16[2,2,64,1024]{3,2,1,0:T(8,128)(2,1)S(1)}, bf16[2,2,64,1024]{3,2,1,0:T(8,128)(2,1)S(1)}, f32[2,2,64,1024]{3,2,1,0:T(8,128)S(1)}, f32[2,2,64,1024]{3,2,1,0:T(8,128)S(1)}) custom-call(bf16[512,1024]{1,0:T(8,128)(2,1)S(1)} %arrange_tokens.2.lhs_ref, bf16[512,3328]{1,0:T(8,128)(2,1)} %refs_4_.7, ...), custom_call_target="tpu_custom_call" | custom-call | tf_op jit(solution)/shard_map/forward_a/pallas_call | solution.py:116
  55.2 9.8 %collective-permute-done.3 = bf16[4,2,64,768]{3,2,1,0:T(8,128)(2,1)S(1)} collective-permute-done((bf16[4,2,64,768]{3,2,1,0:T(8,128)(2,1)S(1)}, bf16[4,2,64,768]{3,2,1,0:T(8,128)(2,1)S(1)}, u32[]{:S(2)}, u32[]{:S(2)}) %collective-permute-start.3) | collective-permute-done | bytes 786464 | tf_op jit(solution)/shard_map/ppermute | solution.py:38
  66.8 1.9 collective-permute-done.9
  72.2 2.1 %collective-permute-done.12 = bf16[2,2,64,1024]{3,2,1,0:T(8,128)(2,1)S(1)} collective-permute-done((bf16[2,2,64,1024]{3,2,1,0:T(8,128)(2,1)S(1)}, bf16[2,2,64,1024]{3,2,1,0:T(8,128)(2,1)S(1)}, u32[]{:S(2)}, u32[]{:S(2)}) %collective-permute-start.12) | collective-permute-done | bytes 524320 | tf_op jit(solution)/shard_map/ppermute | solution.py:34
  75.6 4.3 %collective-permute-done.10.refs_1_ = bf16[2,64,768]{2,1,0:T(8,128)(2,1)S(1)} collective-permute-done((bf16[2,64,768]{2,1,0:T(8,128)(2,1)S(1)}, bf16[2,64,768]{2,1,0:T(8,128)(2,1)S(1)}, u32[]{:S(2)}, u32[]{:S(2)}) %collective-permute-start.10) | collective-permute-done | bytes 196640 | tf_op jit(solution)/shard_map/ppermute | solution.py:38
  81.8 6.1 %collective-permute-done.14 = bf16[2,64,768]{2,1,0:T(8,128)(2,1)S(1)} collective-permute-done((bf16[2,64,768]{2,1,0:T(8,128)(2,1)S(1)}, bf16[2,64,768]{2,1,0:T(8,128)(2,1)S(1)}, u32[]{:S(2)}, u32[]{:S(2)}) %collective-permute-start.14) | collective-permute-done | bytes 196640 | tf_op jit(solution)/shard_map/ppermute | solution.py:38
  88.2 2.5 %collective-permute-done.16 = bf16[2,2,2,64,1024]{4,3,2,1,0:T(8,128)(2,1)S(1)} collective-permute-done((bf16[2,2,2,64,1024]{4,3,2,1,0:T(8,128)(2,1)S(1)}, bf16[2,2,2,64,1024]{4,3,2,1,0:T(8,128)(2,1)S(1)}, u32[]{:S(2)}, u32[]{:S(2)}) %collective-permute-start.16) | collective-permute-done | bytes 1048608 | tf_op jit(solution)/shard_map/ppermute | solution.py:34
  91.8 3.0 %collective-permute-done.13 = bf16[2,2,64,768]{3,2,1,0:T(8,128)(2,1)S(1)} collective-permute-done((bf16[2,2,64,768]{3,2,1,0:T(8,128)(2,1)S(1)}, bf16[2,2,64,768]{3,2,1,0:T(8,128)(2,1)S(1)}, u32[]{:S(2)}, u32[]{:S(2)}) %collective-permute-start.13) | collective-permute-done | bytes 393248 | tf_op jit(solution)/shard_map/ppermute | solution.py:34
  99.0 6.6 %collective-permute-done.20.refs_1_ = bf16[2,64,1024]{2,1,0:T(8,128)(2,1)S(1)} collective-permute-done((bf16[2,64,1024]{2,1,0:T(8,128)(2,1)S(1)}, bf16[2,64,1024]{2,1,0:T(8,128)(2,1)S(1)}, u32[]{:S(2)}, u32[]{:S(2)}) %collective-permute-start.20) | collective-permute-done | bytes 262176 | tf_op jit(solution)/shard_map/ppermute | solution.py:38
  106.0 2.4 %collective-permute-start.22 = (bf16[2,64,1024]{2,1,0:T(8,128)(2,1)S(1)}, bf16[2,64,1024]{2,1,0:T(8,128)(2,1)S(1)}, u32[]{:S(2)}, u32[]{:S(2)}) collective-permute-start(bf16[2,64,1024]{2,1,0:T(8,128)(2,1)S(1)} %get-tuple-element.219), channel_id=1, source_target_pairs={{0,2},{1,3},{2,0},{3,1},{4,6},{5,7},{6,4},{7,5},{8,10},{9,11},{10,... | collective-permute-start | bytes 786440 | tf_op jit(solution)/shard_map/ppermute | solution.py:38
  109.3 5.6 %collective-permute-done.28 = bf16[2,2,64,768]{3,2,1,0:T(8,128)(2,1)S(1)} collective-permute-done((bf16[2,2,64,768]{3,2,1,0:T(8,128)(2,1)S(1)}, bf16[2,2,64,768]{3,2,1,0:T(8,128)(2,1)S(1)}, u32[]{:S(2)}, u32[]{:S(2)}) %collective-permute-start.28) | collective-permute-done | bytes 393248 | tf_op jit(solution)/shard_map/ppermute | solution.py:34
  115.1 1.9 collective-permute-done.26
  119.4 2.2 %collective-permute-start.31 = (bf16[4,2,64,768]{3,2,1,0:T(8,128)(2,1)S(1)}, bf16[4,2,64,768]{3,2,1,0:T(8,128)(2,1)S(1)}, u32[]{:S(2)}, u32[]{:S(2)}) collective-permute-start(bf16[4,2,64,768]{3,2,1,0:T(8,128)(2,1)S(1)} %pad_maximum_fusion.10.refs_0_), channel_id=1, source_target_pairs={{0,2},{1,3},{2,0},{3,1},{4,6},{5,7},{6,4},{7,5},{8,10},{9,11},{10,... | collective-permute-start | bytes 2359304 | tf_op jit(solution)/shard_map/ppermute | solution.py:38
  121.5 5.5 %backward.4 = (bf16[512,3328]{1,0:T(8,128)(2,1)}, bf16[512,3328]{1,0:T(8,128)(2,1)}, f32[1024,512]{1,0:T(8,128)S(1)}) custom-call(bf16[4,2,64,768]{3,2,1,0:T(8,128)(2,1)S(1)} %bitcast.138, bf16[6,2,64,768]{3,2,1,0:T(8,128)(2,1)S(1)} %bitcast.136, bf16[6,2,64,768]{3,2,1,0:T(8,128)(2,1)S(1)} %bitcast.140, bf16[512,1024]{1,0:T(8,128)(2,1)S(1)} %arrange_tokens.3.refs_3_.refs_4_, ...), custom_call_target="tpu_custom_call" | custom-call | flops 9663676 | bytes 23068 | tf_op jit(solution)/shard_map/backward/pallas_call | solution.py:199
  127.0 4.0 %collective-permute-done.32 = bf16[2,2,2,64,768]{4,3,2,1,0:T(8,128)(2,1)S(1)} collective-permute-done((bf16[2,2,2,64,768]{4,3,2,1,0:T(8,128)(2,1)S(1)}, bf16[2,2,2,64,768]{4,3,2,1,0:T(8,128)(2,1)S(1)}, u32[]{:S(2)}, u32[]{:S(2)}) %collective-permute-start.32) | collective-permute-done | bytes 786464 | tf_op jit(solution)/shard_map/ppermute | solution.py:34
  131.1 9.2 %collective-permute-done.31.refs_1_ = bf16[4,2,64,768]{3,2,1,0:T(8,128)(2,1)S(1)} collective-permute-done((bf16[4,2,64,768]{3,2,1,0:T(8,128)(2,1)S(1)}, bf16[4,2,64,768]{3,2,1,0:T(8,128)(2,1)S(1)}, u32[]{:S(2)}, u32[]{:S(2)}) %collective-permute-start.31) | collective-permute-done | bytes 786464 | tf_op jit(solution)/shard_map/ppermute | solution.py:38
  142.3 4.2 %collective-permute-done.35 = bf16[2,2,64,768]{3,2,1,0:T(8,128)(2,1)S(1)} collective-permute-done((bf16[2,2,64,768]{3,2,1,0:T(8,128)(2,1)S(1)}, bf16[2,2,64,768]{3,2,1,0:T(8,128)(2,1)S(1)}, u32[]{:S(2)}, u32[]{:S(2)}) %collective-permute-start.35) | collective-permute-done | bytes 393248 | tf_op jit(solution)/shard_map/ppermute | solution.py:34
  147.0 5.2 %backward.5 = (bf16[512,3328]{1,0:T(8,128)(2,1)}, bf16[512,3328]{1,0:T(8,128)(2,1)}, f32[1024,512]{1,0:T(8,128)S(1)}) custom-call(bf16[4,2,64,768]{3,2,1,0:T(8,128)(2,1)S(1)} %pad_maximum_fusion.10.refs_0_, bf16[4,2,64,768]{3,2,1,0:T(8,128)(2,1)S(1)} %collective-permute-done.31.refs_1_, ...), custom_call_target="tpu_custom_call", output_to_operand_aliasing={{0}: (7, {}), {1}: (8, {})} | custom-call | flops 9663676 | bytes 23068 | tf_op jit(solution)/shard_map/backward/pallas_call | solution.py:199
  153.3 4.0 %collective-permute-done.34 = bf16[2,2,64,1024]{3,2,1,0:T(8,128)(2,1)S(1)} collective-permute-done((bf16[2,2,64,1024]{3,2,1,0:T(8,128)(2,1)S(1)}, bf16[2,2,64,1024]{3,2,1,0:T(8,128)(2,1)S(1)}, u32[]{:S(2)}, u32[]{:S(2)}) %collective-permute-start.34) | collective-permute-done | bytes 524320 | tf_op jit(solution)/shard_map/ppermute | solution.py:34
  160.2 5.6 %backward.6 = (bf16[512,3328]{1,0:T(8,128)(2,1)}, bf16[512,3328]{1,0:T(8,128)(2,1)}, f32[1024,512]{1,0:T(8,128)S(1)}) custom-call(bf16[4,2,64,768]{3,2,1,0:T(8,128)(2,1)S(1)} %bitcast.137, bf16[6,2,64,768]{3,2,1,0:T(8,128)(2,1)S(1)} %bitcast.135, bf16[6,2,64,768]{3,2,1,0:T(8,128)(2,1)S(1)} %bitcast.139, ...), custom_call_target="tpu_custom_call", output_to_operand_aliasing={{0}: (6, {}), {1}: (7, {})} | custom-call | flops 9663676 | bytes 23068 | tf_op jit(solution)/shard_map/backward/pallas_call | solution.py:199
  165.8 4.8 %split_rows.1 = (f32[128,512]{1,0:T(8,128)S(1)}, bf16[128,512]{1,0:T(8,128)(2,1)S(1)}, bf16[128,512]{1,0:T(8,128)(2,1)S(1)}, bf16[128,512]{1,0:T(8,128)(2,1)S(1)...) custom-call(s32[8,2]{1,0:T(8,128)S(1)} %copy.22.at_ref, ...), custom_call_target="tpu_custom_call" | custom-call | flops 2147483 | bytes 12582 | tf_op jit(solution)/shard_map/split_rows/pallas_call | solution.py:232
  171.2 2.5 %collective-permute-start.41 = (bf16[128,512]{1,0:T(8,128)(2,1)S(1)}, bf16[128,512]{1,0:T(8,128)(2,1)S(1)}, u32[]{:S(2)}, u32[]{:S(2)}) collective-permute-start(bf16[128,512]{1,0:T(8,128)(2,1)S(1)} %get-tuple-element.258), channel_id=1, source_target_pairs={{0,32},{16,48},{32,0},{48,16},{64,96},{80,112},{96,64},{112,80},{1... | collective-permute-start | bytes 393224 | tf_op jit(solution)/shard_map/ppermute | solution.py:486
  174.5 2.4 %collective-permute-start.42 = (bf16[128,512]{1,0:T(8,128)(2,1)S(1)}, bf16[128,512]{1,0:T(8,128)(2,1)S(1)}, u32[]{:S(2)}, u32[]{:S(2)}) collective-permute-start(bf16[128,512]{1,0:T(8,128)(2,1)S(1)} %get-tuple-element.260), channel_id=1, source_target_pairs={{0,48},{16,0},{32,16},{48,32},{64,112},{80,64},{96,80},{112,96},{1... | collective-permute-start | bytes 393224 | tf_op jit(solution)/shard_map/ppermute | solution.py:486
  176.9 2.1 %collective-permute-start.43 = (bf16[128,512]{1,0:T(8,128)(2,1)S(1)}, bf16[128,512]{1,0:T(8,128)(2,1)S(1)}, u32[]{:S(2)}, u32[]{:S(2)}) collective-permute-start(bf16[128,512]{1,0:T(8,128)(2,1)S(1)} %get-tuple-element.261), channel_id=1, source_target_pairs={{0,64},{16,80},{32,96},{48,112},{64,0},{80,16},{96,32},{112,48},{1... | collective-permute-start | bytes 393224 | tf_op jit(solution)/shard_map/ppermute | solution.py:486
  179.6 2.4 %collective-permute-done.41 = bf16[128,512]{1,0:T(8,128)(2,1)S(1)} collective-permute-done((bf16[128,512]{1,0:T(8,128)(2,1)S(1)}, bf16[128,512]{1,0:T(8,128)(2,1)S(1)}, u32[]{:S(2)}, u32[]{:S(2)}) %collective-permute-start.41) | collective-permute-done | bytes 131104 | tf_op jit(solution)/shard_map/ppermute | solution.py:486
  181.9 1.8 collective-permute-start.45
  183.7 5.7 %backward.7 = (bf16[512,3328]{1,0:T(8,128)(2,1)}, bf16[512,3328]{1,0:T(8,128)(2,1)}) custom-call(bf16[4,2,64,1024]{3,2,1,0:T(8,128)(2,1)S(1)} %bitcast.134, bf16[6,2,64,1024]{3,2,1,0:T(8,128)(2,1)S(1)} %bitcast.132, bf16[6,2,64,1024]{3,2,1,0:T(8,128)(2,1)} %bitcast.93.refs_2_, ...), custom_call_target="tpu_custom_call", output_to_operand_aliasing={{0}: (6, {}), {1}: (7, {})} | custom-call | flops 2147483 | bytes 12582 | tf_op jit(solution)/shard_map/backward/pallas_call | solution.py:199
  (171 shorter events, 39.9 us)
Async XLA Ops:
  0.6 28.5 %collective-permute-start.1 = (bf16[512,3328]{1,0:T(8,128)(2,1)}, bf16[512,3328]{1,0:T(8,128)(2,1)S(1)}, u32[]{:S(2)}, u32[]{:S(2)}) collective-permute-start(bf16[512,3328]{1,0:T(8,128)(2,1)} %refs_4_.7), channel_id=1, source_target_pairs={{0,1},{1,0},{2,3},{3,2},{4,5},{5,4},{6,7},{7,6},{8,9},{9,8},{10,11... | collective-permute-start | bytes 10223624 | tf_op jit(solution)/shard_map/ppermute | solution.py:42
  0.7 28.4 %collective-permute-start.2 = (bf16[512,3328]{1,0:T(8,128)(2,1)}, bf16[512,3328]{1,0:T(8,128)(2,1)}, u32[]{:S(2)}, u32[]{:S(2)}) collective-permute-start(bf16[512,3328]{1,0:T(8,128)(2,1)} %refs_5_.9), channel_id=1, source_target_pairs={{0,1},{1,0},{2,3},{3,2},{4,5},{5,4},{6,7},{7,6},{8,9},{9,8},{10,11... | collective-permute-start | bytes 10223624 | tf_op jit(solution)/shard_map/ppermute | solution.py:42
  33.1 13.7 %collective-permute-start.5 = (bf16[2,2,64,768]{3,2,1,0:T(8,128)(2,1)S(1)}, bf16[2,2,64,768]{3,2,1,0:T(8,128)(2,1)S(1)}, u32[]{:S(2)}, u32[]{:S(2)}) collective-permute-start(bf16[2,2,64,768]{3,2,1,0:T(8,128)(2,1)S(1)} %get-tuple-element.147), channel_id=1, source_target_pairs={{0,4},{1,13},{2,6},{3,15},{4,8},{5,1},{6,10},{7,3},{8,12},{9,5},{1... | collective-permute-start | bytes 1179656 | tf_op jit(solution)/shard_map/ppermute | solution.py:34
  38.5 9.8 %collective-permute-start.4 = (bf16[2,2,64,768]{3,2,1,0:T(8,128)(2,1)S(1)}, bf16[2,2,64,768]{3,2,1,0:T(8,128)(2,1)S(1)}, u32[]{:S(2)}, u32[]{:S(2)}) collective-permute-start(bf16[2,2,64,768]{3,2,1,0:T(8,128)(2,1)S(1)} %get-tuple-element.145), channel_id=1, source_target_pairs={{0,4},{1,13},{2,6},{3,15},{4,8},{5,1},{6,10},{7,3},{8,12},{9,5},{1... | collective-permute-start | bytes 1179656 | tf_op jit(solution)/shard_map/ppermute | solution.py:34
  43.8 21.2 %collective-permute-start.3 = (bf16[4,2,64,768]{3,2,1,0:T(8,128)(2,1)S(1)}, bf16[4,2,64,768]{3,2,1,0:T(8,128)(2,1)S(1)}, u32[]{:S(2)}, u32[]{:S(2)}) collective-permute-start(bf16[4,2,64,768]{3,2,1,0:T(8,128)(2,1)S(1)} %get-tuple-element.144), channel_id=1, source_target_pairs={{0,2},{1,3},{2,0},{3,1},{4,6},{5,7},{6,4},{7,5},{8,10},{9,11},{10,... | collective-permute-start | bytes 2359304 | tf_op jit(solution)/shard_map/ppermute | solution.py:38
  47.0 19.6 %collective-permute-start.7 = (bf16[2,2,2,64,768]{4,3,2,1,0:T(8,128)(2,1)S(1)}, bf16[2,2,2,64,768]{4,3,2,1,0:T(8,128)(2,1)S(1)}, u32[]{:S(2)}, u32[]{:S(2)}) collective-permute-start(bf16[2,2,2,64,768]{4,3,2,1,0:T(8,128)(2,1)S(1)} %pad_maximum_fusion.6), channel_id=1, source_target_pairs={{0,4},{1,13},{2,6},{3,15},{4,8},{5,1},{6,10},{7,3},{8,12},{9,5},{1... | collective-permute-start | bytes 2359304 | tf_op jit(solution)/shard_map/ppermute | solution.py:34
  48.4 20.3 %collective-permute-start.9 = (bf16[2,2,2,64,768]{4,3,2,1,0:T(8,128)(2,1)S(1)}, bf16[2,2,2,64,768]{4,3,2,1,0:T(8,128)(2,1)S(1)}, u32[]{:S(2)}, u32[]{:S(2)}) collective-permute-start(bf16[2,2,2,64,768]{4,3,2,1,0:T(8,128)(2,1)S(1)} %pad_maximum_fusion.7), channel_id=1, source_target_pairs={{0,4},{1,13},{2,6},{3,15},{4,8},{5,1},{6,10},{7,3},{8,12},{9,5},{1... | collective-permute-start | bytes 2359304 | tf_op jit(solution)/shard_map/ppermute | solution.py:34
  53.7 20.6 %collective-permute-start.12 = (bf16[2,2,64,1024]{3,2,1,0:T(8,128)(2,1)S(1)}, bf16[2,2,64,1024]{3,2,1,0:T(8,128)(2,1)S(1)}, u32[]{:S(2)}, u32[]{:S(2)}) collective-permute-start(bf16[2,2,64,1024]{3,2,1,0:T(8,128)(2,1)S(1)} %get-tuple-element.167), channel_id=1, source_target_pairs={{0,4},{1,13},{2,6},{3,15},{4,8},{5,1},{6,10},{7,3},{8,12},{9,5},{1... | collective-permute-start | bytes 1572872 | tf_op jit(solution)/shard_map/ppermute | solution.py:34
  65.3 16.3 %collective-permute-start.6 = (bf16[2,64,768]{2,1,0:T(8,128)(2,1)S(1)}, bf16[2,64,768]{2,1,0:T(8,128)(2,1)S(1)}, u32[]{:S(2)}, u32[]{:S(2)}) collective-permute-start(bf16[2,64,768]{2,1,0:T(8,128)(2,1)S(1)} %get-tuple-element.277), channel_id=1, source_target_pairs={{0,4},{1,13},{2,6},{3,15},{4,8},{5,1},{6,10},{7,3},{8,12},{9,5},{1... | collective-permute-start | bytes 589832 | tf_op jit(solution)/shard_map/ppermute | solution.py:34
  70.6 9.3 %collective-permute-start.10 = (bf16[2,64,768]{2,1,0:T(8,128)(2,1)S(1)}, bf16[2,64,768]{2,1,0:T(8,128)(2,1)S(1)}, u32[]{:S(2)}, u32[]{:S(2)}) collective-permute-start(bf16[2,64,768]{2,1,0:T(8,128)(2,1)S(1)} %fusion.8), channel_id=1, source_target_pairs={{0,2},{1,3},{2,0},{3,1},{4,6},{5,7},{6,4},{7,5},{8,10},{9,11},{10,... | collective-permute-start | bytes 589832 | tf_op jit(solution)/shard_map/ppermute | solution.py:38
  74.6 16.1 %collective-permute-start.16 = (bf16[2,2,2,64,1024]{4,3,2,1,0:T(8,128)(2,1)S(1)}, bf16[2,2,2,64,1024]{4,3,2,1,0:T(8,128)(2,1)S(1)}, u32[]{:S(2)}, u32[]{:S(2)}) collective-permute-start(bf16[2,2,2,64,1024]{4,3,2,1,0:T(8,128)(2,1)S(1)} %pad_maximum_fusion.4), channel_id=1, source_target_pairs={{0,4},{1,13},{2,6},{3,15},{4,8},{5,1},{6,10},{7,3},{8,12},{9,5},{1... | collective-permute-start | bytes 3145736 | tf_op jit(solution)/shard_map/ppermute | solution.py:34
  74.8 13.2 %collective-permute-start.17 = (bf16[2,64,768]{2,1,0:T(8,128)(2,1)S(1)}, bf16[2,64,768]{2,1,0:T(8,128)(2,1)S(1)}, u32[]{:S(2)}, u32[]{:S(2)}) collective-permute-start(bf16[2,64,768]{2,1,0:T(8,128)(2,1)S(1)} %fusion.9), channel_id=1, source_target_pairs={{0,2},{1,3},{2,0},{3,1},{4,6},{5,7},{6,4},{7,5},{8,10},{9,11},{10,... | collective-permute-start | bytes 589832 | tf_op jit(solution)/shard_map/ppermute | solution.py:38
  81.7 13.1 %collective-permute-start.13 = (bf16[2,2,64,768]{3,2,1,0:T(8,128)(2,1)S(1)}, bf16[2,2,64,768]{3,2,1,0:T(8,128)(2,1)S(1)}, u32[]{:S(2)}, u32[]{:S(2)}) collective-permute-start(bf16[2,2,64,768]{3,2,1,0:T(8,128)(2,1)S(1)} %pad_maximum_fusion.12), channel_id=1, source_target_pairs={{0,4},{1,13},{2,6},{3,15},{4,8},{5,1},{6,10},{7,3},{8,12},{9,5},{1... | collective-permute-start | bytes 1179656 | tf_op jit(solution)/shard_map/ppermute | solution.py:34
  90.8 15.0 %collective-permute-start.25 = (bf16[2,64,768]{2,1,0:T(8,128)(2,1)S(1)}, bf16[2,64,768]{2,1,0:T(8,128)(2,1)S(1)}, u32[]{:S(2)}, u32[]{:S(2)}) collective-permute-start(bf16[2,64,768]{2,1,0:T(8,128)(2,1)S(1)} %get-tuple-element.208), channel_id=1, source_target_pairs={{0,2},{1,3},{2,0},{3,1},{4,6},{5,7},{6,4},{7,5},{8,10},{9,11},{10,... | collective-permute-start | bytes 589832 | tf_op jit(solution)/shard_map/ppermute | solution.py:38
  91.8 14.1 %collective-permute-start.24 = (bf16[2,2,2,64,768]{4,3,2,1,0:T(8,128)(2,1)S(1)}, bf16[2,2,2,64,768]{4,3,2,1,0:T(8,128)(2,1)S(1)}, u32[]{:S(2)}, u32[]{:S(2)}) collective-permute-start(bf16[2,2,2,64,768]{4,3,2,1,0:T(8,128)(2,1)S(1)} %pad_maximum_fusion.8), channel_id=1, source_target_pairs={{0,4},{1,13},{2,6},{3,15},{4,8},{5,1},{6,10},{7,3},{8,12},{9,5},{1... | collective-permute-start | bytes 2359304 | tf_op jit(solution)/shard_map/ppermute | solution.py:34
  95.3 10.3 %collective-permute-start.20 = (bf16[2,64,1024]{2,1,0:T(8,128)(2,1)S(1)}, bf16[2,64,1024]{2,1,0:T(8,128)(2,1)S(1)}, u32[]{:S(2)}, u32[]{:S(2)}) collective-permute-start(bf16[2,64,1024]{2,1,0:T(8,128)(2,1)S(1)} %fusion.6), channel_id=1, source_target_pairs={{0,2},{1,3},{2,0},{3,1},{4,6},{5,7},{6,4},{7,5},{8,10},{9,11},{10,... | collective-permute-start | bytes 786440 | tf_op jit(solution)/shard_map/ppermute | solution.py:38
  98.1 11.1 %collective-permute-start.23 = (bf16[2,2,64,768]{3,2,1,0:T(8,128)(2,1)S(1)}, bf16[2,2,64,768]{3,2,1,0:T(8,128)(2,1)S(1)}, u32[]{:S(2)}, u32[]{:S(2)}) collective-permute-start(bf16[2,2,64,768]{3,2,1,0:T(8,128)(2,1)S(1)} %pad_maximum_fusion.14), channel_id=1, source_target_pairs={{0,4},{1,13},{2,6},{3,15},{4,8},{5,1},{6,10},{7,3},{8,12},{9,5},{1... | collective-permute-start | bytes 1179656 | tf_op jit(solution)/shard_map/ppermute | solution.py:34
  105.9 9.1 %collective-permute-start.28 = (bf16[2,2,64,768]{3,2,1,0:T(8,128)(2,1)S(1)}, bf16[2,2,64,768]{3,2,1,0:T(8,128)(2,1)S(1)}, u32[]{:S(2)}, u32[]{:S(2)}) collective-permute-start(bf16[2,2,64,768]{3,2,1,0:T(8,128)(2,1)S(1)} %slice_bitcast_fusion.8), channel_id=1, source_target_pairs={{0,4},{1,13},{2,6},{3,15},{4,8},{5,1},{6,10},{7,3},{8,12},{9,5},{1... | collective-permute-start | bytes 1179656 | tf_op jit(solution)/shard_map/ppermute | solution.py:34
  105.9 9.1 %collective-permute-start.27 = (bf16[2,2,64,768]{3,2,1,0:T(8,128)(2,1)S(1)}, bf16[2,2,64,768]{3,2,1,0:T(8,128)(2,1)S(1)}, u32[]{:S(2)}, u32[]{:S(2)}) collective-permute-start(bf16[2,2,64,768]{3,2,1,0:T(8,128)(2,1)S(1)} %pad_maximum_fusion.15), channel_id=1, source_target_pairs={{0,1},{1,0},{2,3},{3,2},{4,5},{5,4},{6,7},{7,6},{8,9},{9,8},{10,11... | collective-permute-start | bytes 1179656 | tf_op jit(solution)/shard_map/ppermute | solution.py:42
  106.0 11.1 %collective-permute-start.22 = (bf16[2,64,1024]{2,1,0:T(8,128)(2,1)S(1)}, bf16[2,64,1024]{2,1,0:T(8,128)(2,1)S(1)}, u32[]{:S(2)}, u32[]{:S(2)}) collective-permute-start(bf16[2,64,1024]{2,1,0:T(8,128)(2,1)S(1)} %get-tuple-element.219), channel_id=1, source_target_pairs={{0,2},{1,3},{2,0},{3,1},{4,6},{5,7},{6,4},{7,5},{8,10},{9,11},{10,... | collective-permute-start | bytes 786440 | tf_op jit(solution)/shard_map/ppermute | solution.py:38
  117.8 13.2 %collective-permute-start.32 = (bf16[2,2,2,64,768]{4,3,2,1,0:T(8,128)(2,1)S(1)}, bf16[2,2,2,64,768]{4,3,2,1,0:T(8,128)(2,1)S(1)}, u32[]{:S(2)}, u32[]{:S(2)}) collective-permute-start(bf16[2,2,2,64,768]{4,3,2,1,0:T(8,128)(2,1)S(1)} %pad_maximum_fusion.9), channel_id=1, source_target_pairs={{0,4},{1,13},{2,6},{3,15},{4,8},{5,1},{6,10},{7,3},{8,12},{9,5},{1... | collective-permute-start | bytes 2359304 | tf_op jit(solution)/shard_map/ppermute | solution.py:34
  119.3 22.9 %collective-permute-start.30 = (bf16[2,2,2,64,1024]{4,3,2,1,0:T(8,128)(2,1)S(1)}, bf16[2,2,2,64,1024]{4,3,2,1,0:T(8,128)(2,1)S(1)}, u32[]{:S(2)}, u32[]{:S(2)}) collective-permute-start(bf16[2,2,2,64,1024]{4,3,2,1,0:T(8,128)(2,1)S(1)} %pad_maximum_fusion.5), channel_id=1, source_target_pairs={{0,4},{1,13},{2,6},{3,15},{4,8},{5,1},{6,10},{7,3},{8,12},{9,5},{1... | collective-permute-start | bytes 3145736 | tf_op jit(solution)/shard_map/ppermute | solution.py:34
  119.4 20.9 %collective-permute-start.31 = (bf16[4,2,64,768]{3,2,1,0:T(8,128)(2,1)S(1)}, bf16[4,2,64,768]{3,2,1,0:T(8,128)(2,1)S(1)}, u32[]{:S(2)}, u32[]{:S(2)}) collective-permute-start(bf16[4,2,64,768]{3,2,1,0:T(8,128)(2,1)S(1)} %pad_maximum_fusion.10.refs_0_), channel_id=1, source_target_pairs={{0,2},{1,3},{2,0},{3,1},{4,6},{5,7},{6,4},{7,5},{8,10},{9,11},{10,... | collective-permute-start | bytes 2359304 | tf_op jit(solution)/shard_map/ppermute | solution.py:38
  131.0 15.4 %collective-permute-start.35 = (bf16[2,2,64,768]{3,2,1,0:T(8,128)(2,1)S(1)}, bf16[2,2,64,768]{3,2,1,0:T(8,128)(2,1)S(1)}, u32[]{:S(2)}, u32[]{:S(2)}) collective-permute-start(bf16[2,2,64,768]{3,2,1,0:T(8,128)(2,1)S(1)} %slice_bitcast_fusion.7), channel_id=1, source_target_pairs={{0,4},{1,13},{2,6},{3,15},{4,8},{5,1},{6,10},{7,3},{8,12},{9,5},{1... | collective-permute-start | bytes 1179656 | tf_op jit(solution)/shard_map/ppermute | solution.py:34
  146.6 10.7 %collective-permute-start.34 = (bf16[2,2,64,1024]{3,2,1,0:T(8,128)(2,1)S(1)}, bf16[2,2,64,1024]{3,2,1,0:T(8,128)(2,1)S(1)}, u32[]{:S(2)}, u32[]{:S(2)}) collective-permute-start(bf16[2,2,64,1024]{3,2,1,0:T(8,128)(2,1)S(1)} %slice_bitcast_fusion.1), channel_id=1, source_target_pairs={{0,4},{1,13},{2,6},{3,15},{4,8},{5,1},{6,10},{7,3},{8,12},{9,5},{1... | collective-permute-start | bytes 1572872 | tf_op jit(solution)/shard_map/ppermute | solution.py:34
  157.5 8.3 %collective-permute-start.38 = (bf16[3,2,2,64,1024]{4,3,2,1,0:T(8,128)(2,1)S(1)}, bf16[3,2,2,64,1024]{4,3,2,1,0:T(8,128)(2,1)}, u32[]{:S(2)}, u32[]{:S(2)}) collective-permute-start(bf16[3,2,2,64,1024]{4,3,2,1,0:T(8,128)(2,1)S(1)} %pad_maximum_fusion), channel_id=1, source_target_pairs={{0,1},{1,0},{2,3},{3,2},{4,5},{5,4},{6,7},{7,6},{8,9},{9,8},{10,11... | collective-permute-start | bytes 4718600 | tf_op jit(solution)/shard_map/ppermute | solution.py:42
  170.7 8.9 %collective-permute-start.40 = (bf16[128,512]{1,0:T(8,128)(2,1)S(1)}, bf16[128,512]{1,0:T(8,128)(2,1)S(1)}, u32[]{:S(2)}, u32[]{:S(2)}) collective-permute-start(bf16[128,512]{1,0:T(8,128)(2,1)S(1)} %get-tuple-element.257), channel_id=1, source_target_pairs={{0,96},{16,112},{32,64},{48,80},{64,32},{80,48},{96,0},{112,16},{1... | collective-permute-start | bytes 393224 | tf_op jit(solution)/shard_map/ppermute | solution.py:486
  171.2 10.7 %collective-permute-start.41 = (bf16[128,512]{1,0:T(8,128)(2,1)S(1)}, bf16[128,512]{1,0:T(8,128)(2,1)S(1)}, u32[]{:S(2)}, u32[]{:S(2)}) collective-permute-start(bf16[128,512]{1,0:T(8,128)(2,1)S(1)} %get-tuple-element.258), channel_id=1, source_target_pairs={{0,32},{16,48},{32,0},{48,16},{64,96},{80,112},{96,64},{112,80},{1... | collective-permute-start | bytes 393224 | tf_op jit(solution)/shard_map/ppermute | solution.py:486
  173.7 15.7 %collective-permute-start.39 = (bf16[128,512]{1,0:T(8,128)(2,1)S(1)}, bf16[128,512]{1,0:T(8,128)(2,1)S(1)}, u32[]{:S(2)}, u32[]{:S(2)}) collective-permute-start(bf16[128,512]{1,0:T(8,128)(2,1)S(1)} %get-tuple-element.256), channel_id=1, source_target_pairs={{0,16},{16,32},{32,48},{48,0},{64,80},{80,96},{96,112},{112,64},{1... | collective-permute-start | bytes 393224 | tf_op jit(solution)/shard_map/ppermute | solution.py:486
  174.5 14.9 %collective-permute-start.42 = (bf16[128,512]{1,0:T(8,128)(2,1)S(1)}, bf16[128,512]{1,0:T(8,128)(2,1)S(1)}, u32[]{:S(2)}, u32[]{:S(2)}) collective-permute-start(bf16[128,512]{1,0:T(8,128)(2,1)S(1)} %get-tuple-element.260), channel_id=1, source_target_pairs={{0,48},{16,0},{32,16},{48,32},{64,112},{80,64},{96,80},{112,96},{1... | collective-permute-start | bytes 393224 | tf_op jit(solution)/shard_map/ppermute | solution.py:486
  176.9 12.5 %collective-permute-start.43 = (bf16[128,512]{1,0:T(8,128)(2,1)S(1)}, bf16[128,512]{1,0:T(8,128)(2,1)S(1)}, u32[]{:S(2)}, u32[]{:S(2)}) collective-permute-start(bf16[128,512]{1,0:T(8,128)(2,1)S(1)} %get-tuple-element.261), channel_id=1, source_target_pairs={{0,64},{16,80},{32,96},{48,112},{64,0},{80,16},{96,32},{112,48},{1... | collective-permute-start | bytes 393224 | tf_op jit(solution)/shard_map/ppermute | solution.py:486
  179.6 9.9 %collective-permute-start.44 = (bf16[128,512]{1,0:T(8,128)(2,1)S(1)}, bf16[128,512]{1,0:T(8,128)(2,1)S(1)}, u32[]{:S(2)}, u32[]{:S(2)}) collective-permute-start(bf16[128,512]{1,0:T(8,128)(2,1)S(1)} %get-tuple-element.262), channel_id=1, source_target_pairs={{0,80},{16,96},{32,112},{48,64},{64,16},{80,32},{96,48},{112,0},{1... | collective-permute-start | bytes 393224 | tf_op jit(solution)/shard_map/ppermute | solution.py:486
  (26 other events, 132.6 us)

commit v5 on v4

--- a/solution.py
+++ b/solution.py
@@ -10,10 +10,10 @@
 F32, BF16 = jnp.float32, jnp.bfloat16
 TILE = 256
 CHUNKS = (('b', 3), ('a', 4), ('a', 3), ('a', 3))
-ORDER = ((2, 'f'), (3, 'f'), (0, 'f'), (2, 'a1'), (3, 'a1'), (1, 'f'), (0, 'b1'), (2, 'ac'), (3, 'ac'), (2, 'a2'), (1, 'a1'), (3, 'a2'), (2, 'g'), (0, 'b2'), (2, 'b1'), (3, 'g'), (1, 'ac'), (2, 'b2'), (0, 'bc'), (1, 'a2'), (0, 'g'), (0, 'c1'), (1, 'g'), (3, 'b1'), (2, 'b3'), (0, 'c2'), (2, 'b4'), (3, 'b2'), (0, 'c3'), (1, 'b1'), (1, 'b2'), (2, 'd'), (2, 'K'), (3, 'b3'), (0, 'c4'), (1, 'b3'), (3, 'b4'), (0, 'd'), (0, 'K'), (3, 'd'), (1, 'b4'), (3, 'K'), (1, 'd'), (1, 'Ky'), (1, 'Kw'))
+ORDER = ((2, 'f'), (3, 'f'), (2, 'a1'), (0, 'f'), (3, 'a1'), (1, 'f'), (2, 'ac'), (0, 'b1'), (3, 'ac'), (2, 'a2'), (1, 'a1'), (3, 'a2'), (2, 'g'), (0, 'b2'), (2, 'b1'), (3, 'g'), (1, 'ac'), (2, 'b2'), (0, 'bc'), (1, 'a2'), (0, 'g'), (0, 'c1'), (1, 'g'), (3, 'b1'), (2, 'b3'), (0, 'c2'), (2, 'b4'), (3, 'b2'), (0, 'c3'), (1, 'b1'), (1, 'b2'), (2, 'd'), (2, 'K'), (3, 'b3'), (0, 'c4'), (1, 'b3'), (3, 'b4'), (0, 'd'), (0, 'K'), (3, 'd'), (1, 'b4'), (3, 'K'), (1, 'd'), (1, 'Ky'), (1, 'Kw'))
 MIB = 1 << 20
 APART = ()
-COST = {'f': 0, 'g': 0.001, 'k': 0.001}
+COST = {'f': 0, 'g': 0.001, 'k': 0.3}
 
 
 def column(x, y, core):
@@ -333,7 +333,7 @@
         seq.done(s["swapped"])
 
     def pieces():
-        return [s[name].reshape(-1, 2, 64, n) for name in ("full", "held", "swapped")]
+        return [in_hbm(s[name].reshape(-1, 2, 64, n)) for name in ("full", "held", "swapped")]
 
     parts = [(0, 0), (1, 0), (1, 1), (1, 2), (0, 1), (2, 0), (2, 1), (2, 2)]
     table = [(i, 2 * j + dy) for dy in range(2) for i, j in parts]
@@ -418,7 +418,7 @@
         seq.done(s["swapped"])
 
     def pieces():
-        return [s["here"], s["there"], s["sib"][None], s["swapped"]]
+        return [in_hbm(v) for v in (s["here"], s["there"], s["sib"][None], s["swapped"])]
 
     table = [(0, q) for q in range(4)] + [(2, 0)] + [(3, q) for q in range(3)]
     table += [(1, q) for q in range(4)] + [(3, q) for q in range(3, 7)]
@@ -478,7 +478,7 @@
                 gated = jnp.concatenate([use["gated"][first] for first in sorted(use["gated"])], axis=1)
                 seq.done(gated)
             continue
-        pieces = seq(*steps[i]["pieces"]())
+        pieces = steps[i]["pieces"]()
         table = steps[i]["table"]
         if step == "Ky":
             assert len(ys) == len(CHUNKS) - 1

time: 191 us -> 190 us (level)
  waiting for transfers between devices: 73.9 us -> 60.5 us
  starting transfers between devices: 35.7 us -> 45.6 us
  Pallas kernels: 46.9 us -> 49 us
    ppermute x16, waiting for transfers between devices: 30.7 us -> 18.2 us  [over_x(): return lax.ppermute(v, 'col', ALONG_X)]
    ppermute x16, starting transfers between devices: 9.42 us -> 16.9 us  [over_x(): return lax.ppermute(v, 'col', ALONG_X)]
    ppermute x8, starting transfers between devices: 13.1 us -> 15.6 us  [over_y(): return lax.ppermute(v, 'col', ALONG_Y)]
  transfers between devices with their start and end apart: 46 -> 46, of which waited for: 22 -> 19; matrix products, arithmetic and copies ran while one was open for 3% -> 3% of each run, Pallas kernels for 20% -> 21%
where the time goes in v5:
time: 190 us; the launch traced here: 189 us
  waiting for transfers between devices  60.5 us (32%)
  Pallas kernels  49 us (26%)
  starting transfers between devices  45.6 us (24%)
  blocking collectives  22.3 us (12%)
  local copies, waits for them, and re-layouts  5.61 us (3%)
  other arithmetic  4.94 us (3%)
    ppermute x8, waiting for transfers between devices, over_y(): return lax.ppermute(v, 'col', ALONG_Y)  36.2 us
    pallas_call x4, Pallas kernels, backward(): pl.pallas_call(functools.partial(backward_kernel, len(pieces), table, wit...  23.4 us
    all_to_all x1, blocking collectives, body(): lax.all_to_all(jnp.broadcast_to(inputs[None], (8, 128, 512)), 'row', 0, 0)  22.3 us
    ppermute x16, waiting for transfers between devices, over_x(): return lax.ppermute(v, 'col', ALONG_X)  18.2 us
    ppermute x16, starting transfers between devices, over_x(): return lax.ppermute(v, 'col', ALONG_X)  16.9 us
    pallas_call x4, Pallas kernels, forward(): pl.pallas_call(functools.partial(forward_kernel, path), out_shape=tuple((...  16.1 us
    ppermute x8, starting transfers between devices, over_y(): return lax.ppermute(v, 'col', ALONG_Y)  15.6 us
    ppermute x7, starting transfers between devices, body(): lax.ppermute(parts[i], 'row', row_step(i))  10.1 us
  transfers between devices with their start and end apart: 46, of which 19 were waited for; matrix products, arithmetic and copies ran while one was open for 3% of the time, Pallas kernels for 21%

profile of v5, /device:TPU:0, one launch (start us, length us, event | category | flops | bytes accessed | tf_op | source)
XLA Modules:
  0.0 189.3 jit_solution(13951118158497767930)
XLA Ops:
  2.2 22.3 %all_to_all.5.own_ref = bf16[8,128,512]{2,1,0:T(8,128)(2,1)} all-to-all(bf16[8,128,512]{2,1,0:T(8,128)(2,1)S(1)} %broadcast_in_dim.22), channel_id=1, replica_groups=mesh['row'=8,'col'=16] {'row'}, dimensions={0} | all-to-all | bytes 2097152 | tf_op jit(solution)/shard_map/all_to_all | solution.py:436
  29.2 3.8 %forward_a.3 = (bf16[2,2,64,768]{3,2,1,0:T(8,128)(2,1)S(1)}, bf16[2,2,64,768]{3,2,1,0:T(8,128)(2,1)S(1)}, f32[2,2,64,768]{3,2,1,0:T(8,128)S(1)}, f32[2,2,64,768]{3,2,1,0:T(8,128)S(1)}) custom-call(bf16[512,1024]{1,0:T(8,128)(2,1)S(1)} %arrange_tokens.2.lhs_ref, bf16[512,3328]{1,0:T(8,128)(2,1)} %refs_4_.7, ...), custom_call_target="tpu_custom_call" | custom-call | tf_op jit(solution)/shard_map/forward_a/pallas_call | solution.py:116
  34.6 3.8 %forward_a.4 = (bf16[2,2,64,768]{3,2,1,0:T(8,128)(2,1)S(1)}, bf16[2,2,64,768]{3,2,1,0:T(8,128)(2,1)S(1)}, f32[2,2,64,768]{3,2,1,0:T(8,128)S(1)}, f32[2,2,64,768]{3,2,1,0:T(8,128)S(1)}) custom-call(bf16[512,1024]{1,0:T(8,128)(2,1)S(1)} %arrange_tokens.2.lhs_ref, bf16[512,3328]{1,0:T(8,128)(2,1)} %refs_4_.7, ...), custom_call_target="tpu_custom_call" | custom-call | tf_op jit(solution)/shard_map/forward_a/pallas_call | solution.py:116
  39.9 2.1 %collective-permute-done.3 = bf16[2,2,64,768]{3,2,1,0:T(8,128)(2,1)S(1)} collective-permute-done((bf16[2,2,64,768]{3,2,1,0:T(8,128)(2,1)S(1)}, bf16[2,2,64,768]{3,2,1,0:T(8,128)(2,1)S(1)}, u32[]{:S(2)}, u32[]{:S(2)}) %collective-permute-start.3) | collective-permute-done | bytes 393248 | tf_op jit(solution)/shard_map/ppermute | solution.py:34
  42.6 3.8 %forward_b.1 = (f32[4,2,64,768]{3,2,1,0:T(8,128)S(1)}, bf16[4,2,64,768]{3,2,1,0:T(8,128)(2,1)S(1)}) custom-call(bf16[512,1024]{1,0:T(8,128)(2,1)S(1)} %arrange_tokens.2.lhs_ref, bf16[512,3328]{1,0:T(8,128)(2,1)} %refs_4_.7, bf16[512,3328]{1,0:T(8,128)(2,1)S(1)} %collective-permute-done.1.gs_ref, bf16[512,3328]{1,0:T(8,128)(2,1)} %refs_5_.9, ...), custom_call_target="tpu_custom_call" | custom-call | tf_op jit(solution)/shard_map/forward_b/pallas_call | solution.py:116
  46.4 3.0 %collective-permute-start.4 = (bf16[4,2,64,768]{3,2,1,0:T(8,128)(2,1)S(1)}, bf16[4,2,64,768]{3,2,1,0:T(8,128)(2,1)S(1)}, u32[]{:S(2)}, u32[]{:S(2)}) collective-permute-start(bf16[4,2,64,768]{3,2,1,0:T(8,128)(2,1)S(1)} %get-tuple-element.133), channel_id=1, source_target_pairs={{0,2},{1,3},{2,0},{3,1},{4,6},{5,7},{6,4},{7,5},{8,10},{9,11},{10,... | collective-permute-start | bytes 2359304 | tf_op jit(solution)/shard_map/ppermute | solution.py:38
  51.1 4.7 %forward_a.5 = (bf16[2,2,64,1024]{3,2,1,0:T(8,128)(2,1)S(1)}, bf16[2,2,64,1024]{3,2,1,0:T(8,128)(2,1)S(1)}, f32[2,2,64,1024]{3,2,1,0:T(8,128)S(1)}, f32[2,2,64,1024]{3,2,1,0:T(8,128)S(1)}) custom-call(bf16[512,1024]{1,0:T(8,128)(2,1)S(1)} %arrange_tokens.2.lhs_ref, bf16[512,3328]{1,0:T(8,128)(2,1)} %refs_4_.7, ...), custom_call_target="tpu_custom_call" | custom-call | tf_op jit(solution)/shard_map/forward_a/pallas_call | solution.py:116
  57.2 10.9 %collective-permute-done.4 = bf16[4,2,64,768]{3,2,1,0:T(8,128)(2,1)S(1)} collective-permute-done((bf16[4,2,64,768]{3,2,1,0:T(8,128)(2,1)S(1)}, bf16[4,2,64,768]{3,2,1,0:T(8,128)(2,1)S(1)}, u32[]{:S(2)}, u32[]{:S(2)}) %collective-permute-start.4) | collective-permute-done | bytes 786464 | tf_op jit(solution)/shard_map/ppermute | solution.py:38
  70.6 3.2 %collective-permute-start.10 = (bf16[2,64,768]{2,1,0:T(8,128)(2,1)S(1)}, bf16[2,64,768]{2,1,0:T(8,128)(2,1)S(1)}, u32[]{:S(2)}, u32[]{:S(2)}) collective-permute-start(bf16[2,64,768]{2,1,0:T(8,128)(2,1)S(1)} %fusion.8), channel_id=1, source_target_pairs={{0,2},{1,3},{2,0},{3,1},{4,6},{5,7},{6,4},{7,5},{8,10},{9,11},{10,... | collective-permute-start | bytes 589832 | tf_op jit(solution)/shard_map/ppermute | solution.py:38
  74.1 1.8 collective-permute-start.16
  76.6 2.8 %collective-permute-done.10.refs_1_ = bf16[2,64,768]{2,1,0:T(8,128)(2,1)S(1)} collective-permute-done((bf16[2,64,768]{2,1,0:T(8,128)(2,1)S(1)}, bf16[2,64,768]{2,1,0:T(8,128)(2,1)S(1)}, u32[]{:S(2)}, u32[]{:S(2)}) %collective-permute-start.10) | collective-permute-done | bytes 196640 | tf_op jit(solution)/shard_map/ppermute | solution.py:38
  79.5 3.3 %collective-permute-start.14 = (bf16[2,64,768]{2,1,0:T(8,128)(2,1)S(1)}, bf16[2,64,768]{2,1,0:T(8,128)(2,1)S(1)}, u32[]{:S(2)}, u32[]{:S(2)}) collective-permute-start(bf16[2,64,768]{2,1,0:T(8,128)(2,1)S(1)} %get-tuple-element.165), channel_id=1, source_target_pairs={{0,2},{1,3},{2,0},{3,1},{4,6},{5,7},{6,4},{7,5},{8,10},{9,11},{10,... | collective-permute-start | bytes 589832 | tf_op jit(solution)/shard_map/ppermute | solution.py:38
  82.9 2.3 %collective-permute-start.13 = (bf16[2,2,64,768]{3,2,1,0:T(8,128)(2,1)S(1)}, bf16[2,2,64,768]{3,2,1,0:T(8,128)(2,1)S(1)}, u32[]{:S(2)}, u32[]{:S(2)}) collective-permute-start(bf16[2,2,64,768]{3,2,1,0:T(8,128)(2,1)S(1)} %pad_maximum_fusion.12), channel_id=1, source_target_pairs={{0,4},{1,13},{2,6},{3,15},{4,8},{5,1},{6,10},{7,3},{8,12},{9,5},{1... | collective-permute-start | bytes 1179656 | tf_op jit(solution)/shard_map/ppermute | solution.py:34
  85.2 4.3 %collective-permute-done.14 = bf16[2,64,768]{2,1,0:T(8,128)(2,1)S(1)} collective-permute-done((bf16[2,64,768]{2,1,0:T(8,128)(2,1)S(1)}, bf16[2,64,768]{2,1,0:T(8,128)(2,1)S(1)}, u32[]{:S(2)}, u32[]{:S(2)}) %collective-permute-start.14) | collective-permute-done | bytes 196640 | tf_op jit(solution)/shard_map/ppermute | solution.py:38
  98.5 6.6 %collective-permute-done.20.refs_1_ = bf16[2,64,1024]{2,1,0:T(8,128)(2,1)S(1)} collective-permute-done((bf16[2,64,1024]{2,1,0:T(8,128)(2,1)S(1)}, bf16[2,64,1024]{2,1,0:T(8,128)(2,1)S(1)}, u32[]{:S(2)}, u32[]{:S(2)}) %collective-permute-start.20) | collective-permute-done | bytes 262176 | tf_op jit(solution)/shard_map/ppermute | solution.py:38
  106.9 1.7 collective-permute-start.22
  109.9 4.5 %collective-permute-done.28 = bf16[2,2,64,768]{3,2,1,0:T(8,128)(2,1)S(1)} collective-permute-done((bf16[2,2,64,768]{3,2,1,0:T(8,128)(2,1)S(1)}, bf16[2,2,64,768]{3,2,1,0:T(8,128)(2,1)S(1)}, u32[]{:S(2)}, u32[]{:S(2)}) %collective-permute-start.28) | collective-permute-done | bytes 393248 | tf_op jit(solution)/shard_map/ppermute | solution.py:34
  114.8 1.8 collective-permute-done.26
  122.6 5.7 %backward.4 = (bf16[512,3328]{1,0:T(8,128)(2,1)}, bf16[512,3328]{1,0:T(8,128)(2,1)}, f32[1024,512]{1,0:T(8,128)S(1)}) custom-call(bf16[4,2,64,768]{3,2,1,0:T(8,128)(2,1)} %bitcast.144, bf16[6,2,64,768]{3,2,1,0:T(8,128)(2,1)} %bitcast.142, bf16[6,2,64,768]{3,2,1,0:T(8,128)(2,1)} %bitcast.149, bf16[512,1024]{1,0:T(8,128)(2,1)S(1)} %arrange_tokens.3.refs_3_.refs_4_, ...), custom_call_target="tpu_custom_call" | custom-call | flops 2899102976 | bytes 6920601 | tf_op jit(solution)/shard_map/backward/pallas_call | solution.py:199
  128.3 1.8 collective-permute-done.32
  130.4 11.6 %collective-permute-done.31.refs_1_ = bf16[4,2,64,768]{3,2,1,0:T(8,128)(2,1)S(1)} collective-permute-done((bf16[4,2,64,768]{3,2,1,0:T(8,128)(2,1)S(1)}, bf16[4,2,64,768]{3,2,1,0:T(8,128)(2,1)S(1)}, u32[]{:S(2)}, u32[]{:S(2)}) %collective-permute-start.31) | collective-permute-done | bytes 786464 | tf_op jit(solution)/shard_map/ppermute | solution.py:38
  142.9 2.7 %collective-permute-done.35 = bf16[2,2,64,768]{3,2,1,0:T(8,128)(2,1)S(1)} collective-permute-done((bf16[2,2,64,768]{3,2,1,0:T(8,128)(2,1)S(1)}, bf16[2,2,64,768]{3,2,1,0:T(8,128)(2,1)S(1)}, u32[]{:S(2)}, u32[]{:S(2)}) %collective-permute-start.35) | collective-permute-done | bytes 393248 | tf_op jit(solution)/shard_map/ppermute | solution.py:34
  147.3 5.7 %backward.5 = (bf16[512,3328]{1,0:T(8,128)(2,1)}, bf16[512,3328]{1,0:T(8,128)(2,1)}, f32[1024,512]{1,0:T(8,128)S(1)}) custom-call(bf16[4,2,64,768]{3,2,1,0:T(8,128)(2,1)} %copy-done.3, bf16[4,2,64,768]{3,2,1,0:T(8,128)(2,1)} %copy-done.7, bf16[1,2,64,768]{3,2,1,0:T(8,128)(2,1)} %bitcast.151, ...), custom_call_target="tpu_custom_call", output_to_operand_aliasing={{0}: (7, {}), {1}: (8, {})} | custom-call | flops 2899102976 | bytes 6920601 | tf_op jit(solution)/shard_map/backward/pallas_call | solution.py:199
  153.1 3.4 %collective-permute-done.34 = bf16[2,2,64,1024]{3,2,1,0:T(8,128)(2,1)S(1)} collective-permute-done((bf16[2,2,64,1024]{3,2,1,0:T(8,128)(2,1)S(1)}, bf16[2,2,64,1024]{3,2,1,0:T(8,128)(2,1)S(1)}, u32[]{:S(2)}, u32[]{:S(2)}) %collective-permute-start.34) | collective-permute-done | bytes 524320 | tf_op jit(solution)/shard_map/ppermute | solution.py:34
  157.9 5.9 %backward.6 = (bf16[512,3328]{1,0:T(8,128)(2,1)}, bf16[512,3328]{1,0:T(8,128)(2,1)}, f32[1024,512]{1,0:T(8,128)S(1)}) custom-call(bf16[4,2,64,768]{3,2,1,0:T(8,128)(2,1)} %bitcast.143, bf16[6,2,64,768]{3,2,1,0:T(8,128)(2,1)} %bitcast.141, bf16[6,2,64,768]{3,2,1,0:T(8,128)(2,1)} %bitcast.148, ...), custom_call_target="tpu_custom_call", output_to_operand_aliasing={{0}: (6, {}), {1}: (7, {})} | custom-call | flops 2899102976 | bytes 6920601 | tf_op jit(solution)/shard_map/backward/pallas_call | solution.py:199
  163.8 5.6 %split_rows.1 = (f32[128,512]{1,0:T(8,128)S(1)}, bf16[128,512]{1,0:T(8,128)(2,1)S(1)}, bf16[128,512]{1,0:T(8,128)(2,1)S(1)}, bf16[128,512]{1,0:T(8,128)(2,1)S(1)...) custom-call(s32[8,2]{1,0:T(8,128)S(1)} %copy.22.at_ref, ...), custom_call_target="tpu_custom_call" | custom-call | flops 644245120 | bytes 3774873 | tf_op jit(solution)/shard_map/split_rows/pallas_call | solution.py:232
  170.0 2.5 %collective-permute-start.41 = (bf16[128,512]{1,0:T(8,128)(2,1)S(1)}, bf16[128,512]{1,0:T(8,128)(2,1)S(1)}, u32[]{:S(2)}, u32[]{:S(2)}) collective-permute-start(bf16[128,512]{1,0:T(8,128)(2,1)S(1)} %get-tuple-element.229), channel_id=1, source_target_pairs={{0,32},{16,48},{32,0},{48,16},{64,96},{80,112},{96,64},{112,80},{1... | collective-permute-start | bytes 393224 | tf_op jit(solution)/shard_map/ppermute | solution.py:486
  173.3 2.4 %collective-permute-start.42 = (bf16[128,512]{1,0:T(8,128)(2,1)S(1)}, bf16[128,512]{1,0:T(8,128)(2,1)S(1)}, u32[]{:S(2)}, u32[]{:S(2)}) collective-permute-start(bf16[128,512]{1,0:T(8,128)(2,1)S(1)} %get-tuple-element.231), channel_id=1, source_target_pairs={{0,48},{16,0},{32,16},{48,32},{64,112},{80,64},{96,80},{112,96},{1... | collective-permute-start | bytes 393224 | tf_op jit(solution)/shard_map/ppermute | solution.py:486
  175.7 2.0 %collective-permute-start.43 = (bf16[128,512]{1,0:T(8,128)(2,1)S(1)}, bf16[128,512]{1,0:T(8,128)(2,1)S(1)}, u32[]{:S(2)}, u32[]{:S(2)}) collective-permute-start(bf16[128,512]{1,0:T(8,128)(2,1)S(1)} %get-tuple-element.232), channel_id=1, source_target_pairs={{0,64},{16,80},{32,96},{48,112},{64,0},{80,16},{96,32},{112,48},{1... | collective-permute-start | bytes 393224 | tf_op jit(solution)/shard_map/ppermute | solution.py:486
  178.3 2.4 %collective-permute-done.41 = bf16[128,512]{1,0:T(8,128)(2,1)S(1)} collective-permute-done((bf16[128,512]{1,0:T(8,128)(2,1)S(1)}, bf16[128,512]{1,0:T(8,128)(2,1)S(1)}, u32[]{:S(2)}, u32[]{:S(2)}) %collective-permute-start.41) | collective-permute-done | bytes 131104 | tf_op jit(solution)/shard_map/ppermute | solution.py:486
  180.7 1.7 collective-permute-start.45
  182.4 6.0 %backward.7 = (bf16[512,3328]{1,0:T(8,128)(2,1)}, bf16[512,3328]{1,0:T(8,128)(2,1)}) custom-call(bf16[4,2,64,1024]{3,2,1,0:T(8,128)(2,1)} %bitcast.140, bf16[6,2,64,1024]{3,2,1,0:T(8,128)(2,1)} %bitcast.89.refs_1_, bf16[6,2,64,1024]{3,2,1,0:T(8,128)(2,1)} %bitcast.93.refs_2_, ...), custom_call_target="tpu_custom_call", output_to_operand_aliasing={{0}: (6, {}), {1}: (7, {})} | custom-call | flops 644245120 | bytes 3774873 | tf_op jit(solution)/shard_map/backward/pallas_call | solution.py:199
  (177 shorter events, 41.7 us)
Async XLA Ops:
  0.6 28.5 %collective-permute-start.1 = (bf16[512,3328]{1,0:T(8,128)(2,1)}, bf16[512,3328]{1,0:T(8,128)(2,1)S(1)}, u32[]{:S(2)}, u32[]{:S(2)}) collective-permute-start(bf16[512,3328]{1,0:T(8,128)(2,1)} %refs_4_.7), channel_id=1, source_target_pairs={{0,1},{1,0},{2,3},{3,2},{4,5},{5,4},{6,7},{7,6},{8,9},{9,8},{10,11... | collective-permute-start | bytes 10223624 | tf_op jit(solution)/shard_map/ppermute | solution.py:42
  0.7 28.4 %collective-permute-start.2 = (bf16[512,3328]{1,0:T(8,128)(2,1)}, bf16[512,3328]{1,0:T(8,128)(2,1)}, u32[]{:S(2)}, u32[]{:S(2)}) collective-permute-start(bf16[512,3328]{1,0:T(8,128)(2,1)} %refs_5_.9), channel_id=1, source_target_pairs={{0,1},{1,0},{2,3},{3,2},{4,5},{5,4},{6,7},{7,6},{8,9},{9,8},{10,11... | collective-permute-start | bytes 10223624 | tf_op jit(solution)/shard_map/ppermute | solution.py:42
  33.0 9.1 %collective-permute-start.3 = (bf16[2,2,64,768]{3,2,1,0:T(8,128)(2,1)S(1)}, bf16[2,2,64,768]{3,2,1,0:T(8,128)(2,1)S(1)}, u32[]{:S(2)}, u32[]{:S(2)}) collective-permute-start(bf16[2,2,64,768]{3,2,1,0:T(8,128)(2,1)S(1)} %get-tuple-element.123), channel_id=1, source_target_pairs={{0,4},{1,13},{2,6},{3,15},{4,8},{5,1},{6,10},{7,3},{8,12},{9,5},{1... | collective-permute-start | bytes 1179656 | tf_op jit(solution)/shard_map/ppermute | solution.py:34
  38.4 11.0 %collective-permute-start.6 = (bf16[2,2,64,768]{3,2,1,0:T(8,128)(2,1)S(1)}, bf16[2,2,64,768]{3,2,1,0:T(8,128)(2,1)S(1)}, u32[]{:S(2)}, u32[]{:S(2)}) collective-permute-start(bf16[2,2,64,768]{3,2,1,0:T(8,128)(2,1)S(1)} %get-tuple-element.134), channel_id=1, source_target_pairs={{0,4},{1,13},{2,6},{3,15},{4,8},{5,1},{6,10},{7,3},{8,12},{9,5},{1... | collective-permute-start | bytes 1179656 | tf_op jit(solution)/shard_map/ppermute | solution.py:34
  42.2 14.8 %collective-permute-start.5 = (bf16[2,2,2,64,768]{4,3,2,1,0:T(8,128)(2,1)S(1)}, bf16[2,2,2,64,768]{4,3,2,1,0:T(8,128)(2,1)S(1)}, u32[]{:S(2)}, u32[]{:S(2)}) collective-permute-start(bf16[2,2,2,64,768]{4,3,2,1,0:T(8,128)(2,1)S(1)} %pad_maximum_fusion.6), channel_id=1, source_target_pairs={{0,4},{1,13},{2,6},{3,15},{4,8},{5,1},{6,10},{7,3},{8,12},{9,5},{1... | collective-permute-start | bytes 2359304 | tf_op jit(solution)/shard_map/ppermute | solution.py:34
  46.4 21.8 %collective-permute-start.4 = (bf16[4,2,64,768]{3,2,1,0:T(8,128)(2,1)S(1)}, bf16[4,2,64,768]{3,2,1,0:T(8,128)(2,1)S(1)}, u32[]{:S(2)}, u32[]{:S(2)}) collective-permute-start(bf16[4,2,64,768]{3,2,1,0:T(8,128)(2,1)S(1)} %get-tuple-element.133), channel_id=1, source_target_pairs={{0,2},{1,3},{2,0},{3,1},{4,6},{5,7},{6,4},{7,5},{8,10},{9,11},{10,... | collective-permute-start | bytes 2359304 | tf_op jit(solution)/shard_map/ppermute | solution.py:38
  49.6 19.0 %collective-permute-start.9 = (bf16[2,2,2,64,768]{4,3,2,1,0:T(8,128)(2,1)S(1)}, bf16[2,2,2,64,768]{4,3,2,1,0:T(8,128)(2,1)S(1)}, u32[]{:S(2)}, u32[]{:S(2)}) collective-permute-start(bf16[2,2,2,64,768]{4,3,2,1,0:T(8,128)(2,1)S(1)} %pad_maximum_fusion.7), channel_id=1, source_target_pairs={{0,4},{1,13},{2,6},{3,15},{4,8},{5,1},{6,10},{7,3},{8,12},{9,5},{1... | collective-permute-start | bytes 2359304 | tf_op jit(solution)/shard_map/ppermute | solution.py:34
  55.8 18.0 %collective-permute-start.12 = (bf16[2,2,64,1024]{3,2,1,0:T(8,128)(2,1)S(1)}, bf16[2,2,64,1024]{3,2,1,0:T(8,128)(2,1)S(1)}, u32[]{:S(2)}, u32[]{:S(2)}) collective-permute-start(bf16[2,2,64,1024]{3,2,1,0:T(8,128)(2,1)S(1)} %get-tuple-element.151), channel_id=1, source_target_pairs={{0,4},{1,13},{2,6},{3,15},{4,8},{5,1},{6,10},{7,3},{8,12},{9,5},{1... | collective-permute-start | bytes 1572872 | tf_op jit(solution)/shard_map/ppermute | solution.py:34
  57.1 13.3 %collective-permute-start.8 = (bf16[2,2,64,768]{3,2,1,0:T(8,128)(2,1)S(1)}, bf16[2,2,64,768]{3,2,1,0:T(8,128)(2,1)S(1)}, u32[]{:S(2)}, u32[]{:S(2)}) collective-permute-start(bf16[2,2,64,768]{3,2,1,0:T(8,128)(2,1)S(1)} %slice_bitcast_fusion.10), channel_id=1, source_target_pairs={{0,1},{1,0},{2,3},{3,2},{4,5},{5,4},{6,7},{7,6},{8,9},{9,8},{10,11... | collective-permute-start | bytes 1179656 | tf_op jit(solution)/shard_map/ppermute | solution.py:42
  68.4 14.4 %collective-permute-start.7 = (bf16[2,64,768]{2,1,0:T(8,128)(2,1)S(1)}, bf16[2,64,768]{2,1,0:T(8,128)(2,1)S(1)}, u32[]{:S(2)}, u32[]{:S(2)}) collective-permute-start(bf16[2,64,768]{2,1,0:T(8,128)(2,1)S(1)} %get-tuple-element.245), channel_id=1, source_target_pairs={{0,4},{1,13},{2,6},{3,15},{4,8},{5,1},{6,10},{7,3},{8,12},{9,5},{1... | collective-permute-start | bytes 589832 | tf_op jit(solution)/shard_map/ppermute | solution.py:34
  70.6 8.8 %collective-permute-start.10 = (bf16[2,64,768]{2,1,0:T(8,128)(2,1)S(1)}, bf16[2,64,768]{2,1,0:T(8,128)(2,1)S(1)}, u32[]{:S(2)}, u32[]{:S(2)}) collective-permute-start(bf16[2,64,768]{2,1,0:T(8,128)(2,1)S(1)} %fusion.8), channel_id=1, source_target_pairs={{0,2},{1,3},{2,0},{3,1},{4,6},{5,7},{6,4},{7,5},{8,10},{9,11},{10,... | collective-permute-start | bytes 589832 | tf_op jit(solution)/shard_map/ppermute | solution.py:38
  74.1 16.1 %collective-permute-start.16 = (bf16[2,2,2,64,1024]{4,3,2,1,0:T(8,128)(2,1)S(1)}, bf16[2,2,2,64,1024]{4,3,2,1,0:T(8,128)(2,1)S(1)}, u32[]{:S(2)}, u32[]{:S(2)}) collective-permute-start(bf16[2,2,2,64,1024]{4,3,2,1,0:T(8,128)(2,1)S(1)} %pad_maximum_fusion.4), channel_id=1, source_target_pairs={{0,4},{1,13},{2,6},{3,15},{4,8},{5,1},{6,10},{7,3},{8,12},{9,5},{1... | collective-permute-start | bytes 3145736 | tf_op jit(solution)/shard_map/ppermute | solution.py:34
  76.0 13.7 %collective-permute-start.17 = (bf16[2,64,768]{2,1,0:T(8,128)(2,1)S(1)}, bf16[2,64,768]{2,1,0:T(8,128)(2,1)S(1)}, u32[]{:S(2)}, u32[]{:S(2)}) collective-permute-start(bf16[2,64,768]{2,1,0:T(8,128)(2,1)S(1)} %fusion.9), channel_id=1, source_target_pairs={{0,2},{1,3},{2,0},{3,1},{4,6},{5,7},{6,4},{7,5},{8,10},{9,11},{10,... | collective-permute-start | bytes 589832 | tf_op jit(solution)/shard_map/ppermute | solution.py:38
  79.5 9.9 %collective-permute-start.14 = (bf16[2,64,768]{2,1,0:T(8,128)(2,1)S(1)}, bf16[2,64,768]{2,1,0:T(8,128)(2,1)S(1)}, u32[]{:S(2)}, u32[]{:S(2)}) collective-permute-start(bf16[2,64,768]{2,1,0:T(8,128)(2,1)S(1)} %get-tuple-element.165), channel_id=1, source_target_pairs={{0,2},{1,3},{2,0},{3,1},{4,6},{5,7},{6,4},{7,5},{8,10},{9,11},{10,... | collective-permute-start | bytes 589832 | tf_op jit(solution)/shard_map/ppermute | solution.py:38
  82.9 11.5 %collective-permute-start.13 = (bf16[2,2,64,768]{3,2,1,0:T(8,128)(2,1)S(1)}, bf16[2,2,64,768]{3,2,1,0:T(8,128)(2,1)S(1)}, u32[]{:S(2)}, u32[]{:S(2)}) collective-permute-start(bf16[2,2,64,768]{3,2,1,0:T(8,128)(2,1)S(1)} %pad_maximum_fusion.12), channel_id=1, source_target_pairs={{0,4},{1,13},{2,6},{3,15},{4,8},{5,1},{6,10},{7,3},{8,12},{9,5},{1... | collective-permute-start | bytes 1179656 | tf_op jit(solution)/shard_map/ppermute | solution.py:34
  90.4 14.9 %collective-permute-start.25 = (bf16[2,64,768]{2,1,0:T(8,128)(2,1)S(1)}, bf16[2,64,768]{2,1,0:T(8,128)(2,1)S(1)}, u32[]{:S(2)}, u32[]{:S(2)}) collective-permute-start(bf16[2,64,768]{2,1,0:T(8,128)(2,1)S(1)} %get-tuple-element.192), channel_id=1, source_target_pairs={{0,2},{1,3},{2,0},{3,1},{4,6},{5,7},{6,4},{7,5},{8,10},{9,11},{10,... | collective-permute-start | bytes 589832 | tf_op jit(solution)/shard_map/ppermute | solution.py:38
  92.0 13.4 %collective-permute-start.24 = (bf16[2,2,2,64,768]{4,3,2,1,0:T(8,128)(2,1)S(1)}, bf16[2,2,2,64,768]{4,3,2,1,0:T(8,128)(2,1)S(1)}, u32[]{:S(2)}, u32[]{:S(2)}) collective-permute-start(bf16[2,2,2,64,768]{4,3,2,1,0:T(8,128)(2,1)S(1)} %pad_maximum_fusion.8), channel_id=1, source_target_pairs={{0,4},{1,13},{2,6},{3,15},{4,8},{5,1},{6,10},{7,3},{8,12},{9,5},{1... | collective-permute-start | bytes 2359304 | tf_op jit(solution)/shard_map/ppermute | solution.py:34
  95.1 9.9 %collective-permute-start.20 = (bf16[2,64,1024]{2,1,0:T(8,128)(2,1)S(1)}, bf16[2,64,1024]{2,1,0:T(8,128)(2,1)S(1)}, u32[]{:S(2)}, u32[]{:S(2)}) collective-permute-start(bf16[2,64,1024]{2,1,0:T(8,128)(2,1)S(1)} %fusion.6), channel_id=1, source_target_pairs={{0,2},{1,3},{2,0},{3,1},{4,6},{5,7},{6,4},{7,5},{8,10},{9,11},{10,... | collective-permute-start | bytes 786440 | tf_op jit(solution)/shard_map/ppermute | solution.py:38
  98.1 11.4 %collective-permute-start.23 = (bf16[2,2,64,768]{3,2,1,0:T(8,128)(2,1)S(1)}, bf16[2,2,64,768]{3,2,1,0:T(8,128)(2,1)S(1)}, u32[]{:S(2)}, u32[]{:S(2)}) collective-permute-start(bf16[2,2,64,768]{3,2,1,0:T(8,128)(2,1)S(1)} %pad_maximum_fusion.14), channel_id=1, source_target_pairs={{0,4},{1,13},{2,6},{3,15},{4,8},{5,1},{6,10},{7,3},{8,12},{9,5},{1... | collective-permute-start | bytes 1179656 | tf_op jit(solution)/shard_map/ppermute | solution.py:34
  105.4 9.1 %collective-permute-start.28 = (bf16[2,2,64,768]{3,2,1,0:T(8,128)(2,1)S(1)}, bf16[2,2,64,768]{3,2,1,0:T(8,128)(2,1)S(1)}, u32[]{:S(2)}, u32[]{:S(2)}) collective-permute-start(bf16[2,2,64,768]{3,2,1,0:T(8,128)(2,1)S(1)} %slice_bitcast_fusion.8), channel_id=1, source_target_pairs={{0,4},{1,13},{2,6},{3,15},{4,8},{5,1},{6,10},{7,3},{8,12},{9,5},{1... | collective-permute-start | bytes 1179656 | tf_op jit(solution)/shard_map/ppermute | solution.py:34
  106.9 9.8 %collective-permute-start.22 = (bf16[2,64,1024]{2,1,0:T(8,128)(2,1)S(1)}, bf16[2,64,1024]{2,1,0:T(8,128)(2,1)S(1)}, u32[]{:S(2)}, u32[]{:S(2)}) collective-permute-start(bf16[2,64,1024]{2,1,0:T(8,128)(2,1)S(1)} %get-tuple-element.203), channel_id=1, source_target_pairs={{0,2},{1,3},{2,0},{3,1},{4,6},{5,7},{6,4},{7,5},{8,10},{9,11},{10,... | collective-permute-start | bytes 786440 | tf_op jit(solution)/shard_map/ppermute | solution.py:38
  116.9 13.3 %collective-permute-start.32 = (bf16[2,2,2,64,768]{4,3,2,1,0:T(8,128)(2,1)S(1)}, bf16[2,2,2,64,768]{4,3,2,1,0:T(8,128)(2,1)S(1)}, u32[]{:S(2)}, u32[]{:S(2)}) collective-permute-start(bf16[2,2,2,64,768]{4,3,2,1,0:T(8,128)(2,1)S(1)} %pad_maximum_fusion.9), channel_id=1, source_target_pairs={{0,4},{1,13},{2,6},{3,15},{4,8},{5,1},{6,10},{7,3},{8,12},{9,5},{1... | collective-permute-start | bytes 2359304 | tf_op jit(solution)/shard_map/ppermute | solution.py:34
  118.9 24.0 %collective-permute-start.30 = (bf16[2,2,2,64,1024]{4,3,2,1,0:T(8,128)(2,1)S(1)}, bf16[2,2,2,64,1024]{4,3,2,1,0:T(8,128)(2,1)S(1)}, u32[]{:S(2)}, u32[]{:S(2)}) collective-permute-start(bf16[2,2,2,64,1024]{4,3,2,1,0:T(8,128)(2,1)S(1)} %pad_maximum_fusion.5), channel_id=1, source_target_pairs={{0,4},{1,13},{2,6},{3,15},{4,8},{5,1},{6,10},{7,3},{8,12},{9,5},{1... | collective-permute-start | bytes 3145736 | tf_op jit(solution)/shard_map/ppermute | solution.py:34
  120.3 21.7 %collective-permute-start.31 = (bf16[4,2,64,768]{3,2,1,0:T(8,128)(2,1)S(1)}, bf16[4,2,64,768]{3,2,1,0:T(8,128)(2,1)S(1)}, u32[]{:S(2)}, u32[]{:S(2)}) collective-permute-start(bf16[4,2,64,768]{3,2,1,0:T(8,128)(2,1)S(1)} %pad_maximum_fusion.10.refs_0_), channel_id=1, source_target_pairs={{0,2},{1,3},{2,0},{3,1},{4,6},{5,7},{6,4},{7,5},{8,10},{9,11},{10,... | collective-permute-start | bytes 2359304 | tf_op jit(solution)/shard_map/ppermute | solution.py:38
  130.2 15.4 %collective-permute-start.35 = (bf16[2,2,64,768]{3,2,1,0:T(8,128)(2,1)S(1)}, bf16[2,2,64,768]{3,2,1,0:T(8,128)(2,1)S(1)}, u32[]{:S(2)}, u32[]{:S(2)}) collective-permute-start(bf16[2,2,64,768]{3,2,1,0:T(8,128)(2,1)S(1)} %slice_bitcast_fusion.7), channel_id=1, source_target_pairs={{0,4},{1,13},{2,6},{3,15},{4,8},{5,1},{6,10},{7,3},{8,12},{9,5},{1... | collective-permute-start | bytes 1179656 | tf_op jit(solution)/shard_map/ppermute | solution.py:34
  145.8 10.7 %collective-permute-start.34 = (bf16[2,2,64,1024]{3,2,1,0:T(8,128)(2,1)S(1)}, bf16[2,2,64,1024]{3,2,1,0:T(8,128)(2,1)S(1)}, u32[]{:S(2)}, u32[]{:S(2)}) collective-permute-start(bf16[2,2,64,1024]{3,2,1,0:T(8,128)(2,1)S(1)} %slice_bitcast_fusion.1), channel_id=1, source_target_pairs={{0,4},{1,13},{2,6},{3,15},{4,8},{5,1},{6,10},{7,3},{8,12},{9,5},{1... | collective-permute-start | bytes 1572872 | tf_op jit(solution)/shard_map/ppermute | solution.py:34
  169.4 8.9 %collective-permute-start.40 = (bf16[128,512]{1,0:T(8,128)(2,1)S(1)}, bf16[128,512]{1,0:T(8,128)(2,1)S(1)}, u32[]{:S(2)}, u32[]{:S(2)}) collective-permute-start(bf16[128,512]{1,0:T(8,128)(2,1)S(1)} %get-tuple-element.228), channel_id=1, source_target_pairs={{0,96},{16,112},{32,64},{48,80},{64,32},{80,48},{96,0},{112,16},{1... | collective-permute-start | bytes 393224 | tf_op jit(solution)/shard_map/ppermute | solution.py:486
  170.0 10.7 %collective-permute-start.41 = (bf16[128,512]{1,0:T(8,128)(2,1)S(1)}, bf16[128,512]{1,0:T(8,128)(2,1)S(1)}, u32[]{:S(2)}, u32[]{:S(2)}) collective-permute-start(bf16[128,512]{1,0:T(8,128)(2,1)S(1)} %get-tuple-element.229), channel_id=1, source_target_pairs={{0,32},{16,48},{32,0},{48,16},{64,96},{80,112},{96,64},{112,80},{1... | collective-permute-start | bytes 393224 | tf_op jit(solution)/shard_map/ppermute | solution.py:486
  172.5 16.0 %collective-permute-start.39 = (bf16[128,512]{1,0:T(8,128)(2,1)S(1)}, bf16[128,512]{1,0:T(8,128)(2,1)S(1)}, u32[]{:S(2)}, u32[]{:S(2)}) collective-permute-start(bf16[128,512]{1,0:T(8,128)(2,1)S(1)} %get-tuple-element.227), channel_id=1, source_target_pairs={{0,16},{16,32},{32,48},{48,0},{64,80},{80,96},{96,112},{112,64},{1... | collective-permute-start | bytes 393224 | tf_op jit(solution)/shard_map/ppermute | solution.py:486
  173.3 15.2 %collective-permute-start.42 = (bf16[128,512]{1,0:T(8,128)(2,1)S(1)}, bf16[128,512]{1,0:T(8,128)(2,1)S(1)}, u32[]{:S(2)}, u32[]{:S(2)}) collective-permute-start(bf16[128,512]{1,0:T(8,128)(2,1)S(1)} %get-tuple-element.231), channel_id=1, source_target_pairs={{0,48},{16,0},{32,16},{48,32},{64,112},{80,64},{96,80},{112,96},{1... | collective-permute-start | bytes 393224 | tf_op jit(solution)/shard_map/ppermute | solution.py:486
  175.7 12.8 %collective-permute-start.43 = (bf16[128,512]{1,0:T(8,128)(2,1)S(1)}, bf16[128,512]{1,0:T(8,128)(2,1)S(1)}, u32[]{:S(2)}, u32[]{:S(2)}) collective-permute-start(bf16[128,512]{1,0:T(8,128)(2,1)S(1)} %get-tuple-element.232), channel_id=1, source_target_pairs={{0,64},{16,80},{32,96},{48,112},{64,0},{80,16},{96,32},{112,48},{1... | collective-permute-start | bytes 393224 | tf_op jit(solution)/shard_map/ppermute | solution.py:486
  178.3 10.2 %collective-permute-start.44 = (bf16[128,512]{1,0:T(8,128)(2,1)S(1)}, bf16[128,512]{1,0:T(8,128)(2,1)S(1)}, u32[]{:S(2)}, u32[]{:S(2)}) collective-permute-start(bf16[128,512]{1,0:T(8,128)(2,1)S(1)} %get-tuple-element.233), channel_id=1, source_target_pairs={{0,80},{16,96},{32,112},{48,64},{64,16},{80,32},{96,48},{112,0},{1... | collective-permute-start | bytes 393224 | tf_op jit(solution)/shard_map/ppermute | solution.py:486
  (29 other events, 163.5 us)

commit v6 on v5

--- a/solution.py
+++ b/solution.py
@@ -158,12 +158,13 @@
 
 
 def backward_kernel(arrays, table, with_y, *refs):
-    held, (xt_ref, gate_ref, lift_ref) = refs[:arrays], refs[arrays : arrays + 3]
+    held, xt_ref = refs[:arrays], refs[arrays]
     outs = refs[-3:] if with_y else refs[-2:]
     both = [tokens(held, table, m) for m in range(2)]
     for m in range(2):
         outs[m][...] = jnp.dot(xt_ref[...], both[m], preferred_element_type=F32).astype(BF16)
     if with_y:
+        gate_ref, lift_ref = refs[arrays + 1 : arrays + 3]
         grad = jnp.concatenate(both, axis=1)
         weight = jnp.concatenate([gate_ref[...], lift_ref[...]], axis=1)
         part = lax.dot_general(grad, weight, (((1,), (1,)), ((), ())), preferred_element_type=F32)
@@ -182,9 +183,9 @@
     n = tiles * TILE if once else TILE
     mode = dict(pipeline_mode=pl.Buffered(1)) if once else {}
     wide = pl.BlockSpec((512, n), lambda j: (0, first // tiles if once else first + j), **mode)
-    args = [*pieces, xt, gate, lift]
+    args = [*pieces, xt, gate, lift] if with_y else [*pieces, xt]
     specs = [pl.BlockSpec((v.shape[0], 2, 64, n), lambda j: (0, 0, 0, j), **mode) for v in pieces]
-    specs += [whole(xt.shape), wide, wide]
+    specs += [whole(xt.shape), wide, wide] if with_y else [whole(xt.shape)]
     alias, shapes = {}, [jax.ShapeDtypeStruct(gate.shape, BF16)] * 2
     column = pl.BlockSpec((512, n), lambda j: (0, first // tiles if once else first + j))
     out_specs = [column, column]

time: 190 us -> 189 us (level)
  no operation moved by 1% of the time
where the time goes in v6:
time: 189 us
  waiting for transfers between devices  60.5 us (32%)
  Pallas kernels  48.6 us (26%)
  starting transfers between devices  45.6 us (24%)
  blocking collectives  22.3 us (12%)
  local copies, waits for them, and re-layouts  5.61 us (3%)
  other arithmetic  4.94 us (3%)
    ppermute x8, waiting for transfers between devices, over_y(): return lax.ppermute(v, 'col', ALONG_Y)  36.2 us
    pallas_call x4, Pallas kernels, backward(): pl.pallas_call(functools.partial(backward_kernel, len(pieces), table, wit...  23 us
    all_to_all x1, blocking collectives, body(): lax.all_to_all(jnp.broadcast_to(inputs[None], (8, 128, 512)), 'row', 0, 0)  22.3 us
    ppermute x16, waiting for transfers between devices, over_x(): return lax.ppermute(v, 'col', ALONG_X)  18.2 us
    ppermute x16, starting transfers between devices, over_x(): return lax.ppermute(v, 'col', ALONG_X)  16.9 us
    pallas_call x4, Pallas kernels, forward(): pl.pallas_call(functools.partial(forward_kernel, path), out_shape=tuple((...  16.1 us
    ppermute x8, starting transfers between devices, over_y(): return lax.ppermute(v, 'col', ALONG_Y)  15.6 us
    ppermute x7, starting transfers between devices, body(): lax.ppermute(parts[i], 'row', row_step(i))  10.1 us
  transfers between devices with their start and end apart: 46, of which 19 were waited for; matrix products, arithmetic and copies ran while one was open for 3% of the time, Pallas kernels for 21%

profile of v6, /device:TPU:0, one launch (start us, length us, event | category | flops | bytes accessed | tf_op | source)
XLA Modules:
  0.0 188.9 jit_solution(8088469170259189842)
XLA Ops:
  2.2 22.3 %all_to_all.5.own_ref = bf16[8,128,512]{2,1,0:T(8,128)(2,1)} all-to-all(bf16[8,128,512]{2,1,0:T(8,128)(2,1)S(1)} %broadcast_in_dim.22), channel_id=1, replica_groups=mesh['row'=8,'col'=16] {'row'}, dimensions={0} | all-to-all | bytes 2097152 | tf_op jit(solution)/shard_map/all_to_all | solution.py:437
  29.2 3.8 %forward_a.3 = (bf16[2,2,64,768]{3,2,1,0:T(8,128)(2,1)S(1)}, bf16[2,2,64,768]{3,2,1,0:T(8,128)(2,1)S(1)}, f32[2,2,64,768]{3,2,1,0:T(8,128)S(1)}, f32[2,2,64,768]{3,2,1,0:T(8,128)S(1)}) custom-call(bf16[512,1024]{1,0:T(8,128)(2,1)S(1)} %arrange_tokens.2.lhs_ref, bf16[512,3328]{1,0:T(8,128)(2,1)} %refs_6_.3, ...), custom_call_target="tpu_custom_call" | custom-call | tf_op jit(solution)/shard_map/forward_a/pallas_call | solution.py:116
  34.6 3.8 %forward_a.4 = (bf16[2,2,64,768]{3,2,1,0:T(8,128)(2,1)S(1)}, bf16[2,2,64,768]{3,2,1,0:T(8,128)(2,1)S(1)}, f32[2,2,64,768]{3,2,1,0:T(8,128)S(1)}, f32[2,2,64,768]{3,2,1,0:T(8,128)S(1)}) custom-call(bf16[512,1024]{1,0:T(8,128)(2,1)S(1)} %arrange_tokens.2.lhs_ref, bf16[512,3328]{1,0:T(8,128)(2,1)} %refs_6_.3, ...), custom_call_target="tpu_custom_call" | custom-call | tf_op jit(solution)/shard_map/forward_a/pallas_call | solution.py:116
  39.9 2.1 %collective-permute-done.3 = bf16[2,2,64,768]{3,2,1,0:T(8,128)(2,1)S(1)} collective-permute-done((bf16[2,2,64,768]{3,2,1,0:T(8,128)(2,1)S(1)}, bf16[2,2,64,768]{3,2,1,0:T(8,128)(2,1)S(1)}, u32[]{:S(2)}, u32[]{:S(2)}) %collective-permute-start.3) | collective-permute-done | bytes 393248 | tf_op jit(solution)/shard_map/ppermute | solution.py:34
  42.6 3.8 %forward_b.1 = (f32[4,2,64,768]{3,2,1,0:T(8,128)S(1)}, bf16[4,2,64,768]{3,2,1,0:T(8,128)(2,1)S(1)}) custom-call(bf16[512,1024]{1,0:T(8,128)(2,1)S(1)} %arrange_tokens.2.lhs_ref, bf16[512,3328]{1,0:T(8,128)(2,1)} %refs_6_.3, bf16[512,3328]{1,0:T(8,128)(2,1)S(1)} %collective-permute-done.1.gs_ref, bf16[512,3328]{1,0:T(8,128)(2,1)} %refs_10_.1, ...), custom_call_target="tpu_custom_call" | custom-call | tf_op jit(solution)/shard_map/forward_b/pallas_call | solution.py:116
  46.4 3.0 %collective-permute-start.4 = (bf16[4,2,64,768]{3,2,1,0:T(8,128)(2,1)S(1)}, bf16[4,2,64,768]{3,2,1,0:T(8,128)(2,1)S(1)}, u32[]{:S(2)}, u32[]{:S(2)}) collective-permute-start(bf16[4,2,64,768]{3,2,1,0:T(8,128)(2,1)S(1)} %get-tuple-element.133), channel_id=1, source_target_pairs={{0,2},{1,3},{2,0},{3,1},{4,6},{5,7},{6,4},{7,5},{8,10},{9,11},{10,... | collective-permute-start | bytes 2359304 | tf_op jit(solution)/shard_map/ppermute | solution.py:38
  51.1 4.7 %forward_a.5 = (bf16[2,2,64,1024]{3,2,1,0:T(8,128)(2,1)S(1)}, bf16[2,2,64,1024]{3,2,1,0:T(8,128)(2,1)S(1)}, f32[2,2,64,1024]{3,2,1,0:T(8,128)S(1)}, f32[2,2,64,1024]{3,2,1,0:T(8,128)S(1)}) custom-call(bf16[512,1024]{1,0:T(8,128)(2,1)S(1)} %arrange_tokens.2.lhs_ref, bf16[512,3328]{1,0:T(8,128)(2,1)} %refs_6_.3, ...), custom_call_target="tpu_custom_call" | custom-call | tf_op jit(solution)/shard_map/forward_a/pallas_call | solution.py:116
  57.2 10.9 %collective-permute-done.4 = bf16[4,2,64,768]{3,2,1,0:T(8,128)(2,1)S(1)} collective-permute-done((bf16[4,2,64,768]{3,2,1,0:T(8,128)(2,1)S(1)}, bf16[4,2,64,768]{3,2,1,0:T(8,128)(2,1)S(1)}, u32[]{:S(2)}, u32[]{:S(2)}) %collective-permute-start.4) | collective-permute-done | bytes 786464 | tf_op jit(solution)/shard_map/ppermute | solution.py:38
  70.6 3.2 %collective-permute-start.10 = (bf16[2,64,768]{2,1,0:T(8,128)(2,1)S(1)}, bf16[2,64,768]{2,1,0:T(8,128)(2,1)S(1)}, u32[]{:S(2)}, u32[]{:S(2)}) collective-permute-start(bf16[2,64,768]{2,1,0:T(8,128)(2,1)S(1)} %fusion.8), channel_id=1, source_target_pairs={{0,2},{1,3},{2,0},{3,1},{4,6},{5,7},{6,4},{7,5},{8,10},{9,11},{10,... | collective-permute-start | bytes 589832 | tf_op jit(solution)/shard_map/ppermute | solution.py:38
  74.1 1.8 collective-permute-start.16
  76.6 2.8 %collective-permute-done.10.refs_1_ = bf16[2,64,768]{2,1,0:T(8,128)(2,1)S(1)} collective-permute-done((bf16[2,64,768]{2,1,0:T(8,128)(2,1)S(1)}, bf16[2,64,768]{2,1,0:T(8,128)(2,1)S(1)}, u32[]{:S(2)}, u32[]{:S(2)}) %collective-permute-start.10) | collective-permute-done | bytes 196640 | tf_op jit(solution)/shard_map/ppermute | solution.py:38
  79.5 3.3 %collective-permute-start.14 = (bf16[2,64,768]{2,1,0:T(8,128)(2,1)S(1)}, bf16[2,64,768]{2,1,0:T(8,128)(2,1)S(1)}, u32[]{:S(2)}, u32[]{:S(2)}) collective-permute-start(bf16[2,64,768]{2,1,0:T(8,128)(2,1)S(1)} %get-tuple-element.165), channel_id=1, source_target_pairs={{0,2},{1,3},{2,0},{3,1},{4,6},{5,7},{6,4},{7,5},{8,10},{9,11},{10,... | collective-permute-start | bytes 589832 | tf_op jit(solution)/shard_map/ppermute | solution.py:38
  82.9 2.3 %collective-permute-start.13 = (bf16[2,2,64,768]{3,2,1,0:T(8,128)(2,1)S(1)}, bf16[2,2,64,768]{3,2,1,0:T(8,128)(2,1)S(1)}, u32[]{:S(2)}, u32[]{:S(2)}) collective-permute-start(bf16[2,2,64,768]{3,2,1,0:T(8,128)(2,1)S(1)} %pad_maximum_fusion.12), channel_id=1, source_target_pairs={{0,4},{1,13},{2,6},{3,15},{4,8},{5,1},{6,10},{7,3},{8,12},{9,5},{1... | collective-permute-start | bytes 1179656 | tf_op jit(solution)/shard_map/ppermute | solution.py:34
  85.2 4.3 %collective-permute-done.14 = bf16[2,64,768]{2,1,0:T(8,128)(2,1)S(1)} collective-permute-done((bf16[2,64,768]{2,1,0:T(8,128)(2,1)S(1)}, bf16[2,64,768]{2,1,0:T(8,128)(2,1)S(1)}, u32[]{:S(2)}, u32[]{:S(2)}) %collective-permute-start.14) | collective-permute-done | bytes 196640 | tf_op jit(solution)/shard_map/ppermute | solution.py:38
  98.5 6.6 %collective-permute-done.20.refs_1_ = bf16[2,64,1024]{2,1,0:T(8,128)(2,1)S(1)} collective-permute-done((bf16[2,64,1024]{2,1,0:T(8,128)(2,1)S(1)}, bf16[2,64,1024]{2,1,0:T(8,128)(2,1)S(1)}, u32[]{:S(2)}, u32[]{:S(2)}) %collective-permute-start.20) | collective-permute-done | bytes 262176 | tf_op jit(solution)/shard_map/ppermute | solution.py:38
  106.9 1.7 collective-permute-start.22
  109.9 4.5 %collective-permute-done.28 = bf16[2,2,64,768]{3,2,1,0:T(8,128)(2,1)S(1)} collective-permute-done((bf16[2,2,64,768]{3,2,1,0:T(8,128)(2,1)S(1)}, bf16[2,2,64,768]{3,2,1,0:T(8,128)(2,1)S(1)}, u32[]{:S(2)}, u32[]{:S(2)}) %collective-permute-start.28) | collective-permute-done | bytes 393248 | tf_op jit(solution)/shard_map/ppermute | solution.py:34
  114.8 1.8 collective-permute-done.26
  122.6 5.7 %backward.4 = (bf16[512,3328]{1,0:T(8,128)(2,1)}, bf16[512,3328]{1,0:T(8,128)(2,1)}, f32[1024,512]{1,0:T(8,128)S(1)}) custom-call(bf16[4,2,64,768]{3,2,1,0:T(8,128)(2,1)} %bitcast.144, bf16[6,2,64,768]{3,2,1,0:T(8,128)(2,1)} %bitcast.142, bf16[6,2,64,768]{3,2,1,0:T(8,128)(2,1)} %bitcast.149, bf16[512,1024]{1,0:T(8,128)(2,1)S(1)} %arrange_tokens.3.refs_3_.refs_4_, ...), custom_call_target="tpu_custom_call" | custom-call | flops 2899102976 | bytes 6920601 | tf_op jit(solution)/shard_map/backward/pallas_call | solution.py:200
  128.3 1.8 collective-permute-done.32
  130.4 11.6 %collective-permute-done.31.refs_1_ = bf16[4,2,64,768]{3,2,1,0:T(8,128)(2,1)S(1)} collective-permute-done((bf16[4,2,64,768]{3,2,1,0:T(8,128)(2,1)S(1)}, bf16[4,2,64,768]{3,2,1,0:T(8,128)(2,1)S(1)}, u32[]{:S(2)}, u32[]{:S(2)}) %collective-permute-start.31) | collective-permute-done | bytes 786464 | tf_op jit(solution)/shard_map/ppermute | solution.py:38
  142.9 2.7 %collective-permute-done.35 = bf16[2,2,64,768]{3,2,1,0:T(8,128)(2,1)S(1)} collective-permute-done((bf16[2,2,64,768]{3,2,1,0:T(8,128)(2,1)S(1)}, bf16[2,2,64,768]{3,2,1,0:T(8,128)(2,1)S(1)}, u32[]{:S(2)}, u32[]{:S(2)}) %collective-permute-start.35) | collective-permute-done | bytes 393248 | tf_op jit(solution)/shard_map/ppermute | solution.py:34
  147.3 5.7 %backward.5 = (bf16[512,3328]{1,0:T(8,128)(2,1)}, bf16[512,3328]{1,0:T(8,128)(2,1)}, f32[1024,512]{1,0:T(8,128)S(1)}) custom-call(bf16[4,2,64,768]{3,2,1,0:T(8,128)(2,1)} %copy-done.3, bf16[4,2,64,768]{3,2,1,0:T(8,128)(2,1)} %copy-done.7, bf16[1,2,64,768]{3,2,1,0:T(8,128)(2,1)} %bitcast.151, ...), custom_call_target="tpu_custom_call", output_to_operand_aliasing={{0}: (7, {}), {1}: (8, {})} | custom-call | flops 2899102976 | bytes 6920601 | tf_op jit(solution)/shard_map/backward/pallas_call | solution.py:200
  153.1 3.4 %collective-permute-done.34 = bf16[2,2,64,1024]{3,2,1,0:T(8,128)(2,1)S(1)} collective-permute-done((bf16[2,2,64,1024]{3,2,1,0:T(8,128)(2,1)S(1)}, bf16[2,2,64,1024]{3,2,1,0:T(8,128)(2,1)S(1)}, u32[]{:S(2)}, u32[]{:S(2)}) %collective-permute-start.34) | collective-permute-done | bytes 524320 | tf_op jit(solution)/shard_map/ppermute | solution.py:34
  157.9 5.9 %backward.6 = (bf16[512,3328]{1,0:T(8,128)(2,1)}, bf16[512,3328]{1,0:T(8,128)(2,1)}, f32[1024,512]{1,0:T(8,128)S(1)}) custom-call(bf16[4,2,64,768]{3,2,1,0:T(8,128)(2,1)} %bitcast.143, bf16[6,2,64,768]{3,2,1,0:T(8,128)(2,1)} %bitcast.141, bf16[6,2,64,768]{3,2,1,0:T(8,128)(2,1)} %bitcast.148, ...), custom_call_target="tpu_custom_call", output_to_operand_aliasing={{0}: (6, {}), {1}: (7, {})} | custom-call | flops 2899102976 | bytes 6920601 | tf_op jit(solution)/shard_map/backward/pallas_call | solution.py:200
  163.8 5.6 %split_rows.1 = (f32[128,512]{1,0:T(8,128)S(1)}, bf16[128,512]{1,0:T(8,128)(2,1)S(1)}, bf16[128,512]{1,0:T(8,128)(2,1)S(1)}, bf16[128,512]{1,0:T(8,128)(2,1)S(1)...) custom-call(s32[8,2]{1,0:T(8,128)S(1)} %copy.22.at_ref, ...), custom_call_target="tpu_custom_call" | custom-call | flops 644245120 | bytes 3774873 | tf_op jit(solution)/shard_map/split_rows/pallas_call | solution.py:233
  170.0 2.5 %collective-permute-start.41 = (bf16[128,512]{1,0:T(8,128)(2,1)S(1)}, bf16[128,512]{1,0:T(8,128)(2,1)S(1)}, u32[]{:S(2)}, u32[]{:S(2)}) collective-permute-start(bf16[128,512]{1,0:T(8,128)(2,1)S(1)} %get-tuple-element.229), channel_id=1, source_target_pairs={{0,32},{16,48},{32,0},{48,16},{64,96},{80,112},{96,64},{112,80},{1... | collective-permute-start | bytes 393224 | tf_op jit(solution)/shard_map/ppermute | solution.py:487
  173.3 2.4 %collective-permute-start.42 = (bf16[128,512]{1,0:T(8,128)(2,1)S(1)}, bf16[128,512]{1,0:T(8,128)(2,1)S(1)}, u32[]{:S(2)}, u32[]{:S(2)}) collective-permute-start(bf16[128,512]{1,0:T(8,128)(2,1)S(1)} %get-tuple-element.231), channel_id=1, source_target_pairs={{0,48},{16,0},{32,16},{48,32},{64,112},{80,64},{96,80},{112,96},{1... | collective-permute-start | bytes 393224 | tf_op jit(solution)/shard_map/ppermute | solution.py:487
  175.7 2.0 %collective-permute-start.43 = (bf16[128,512]{1,0:T(8,128)(2,1)S(1)}, bf16[128,512]{1,0:T(8,128)(2,1)S(1)}, u32[]{:S(2)}, u32[]{:S(2)}) collective-permute-start(bf16[128,512]{1,0:T(8,128)(2,1)S(1)} %get-tuple-element.232), channel_id=1, source_target_pairs={{0,64},{16,80},{32,96},{48,112},{64,0},{80,16},{96,32},{112,48},{1... | collective-permute-start | bytes 393224 | tf_op jit(solution)/shard_map/ppermute | solution.py:487
  178.3 2.4 %collective-permute-done.41 = bf16[128,512]{1,0:T(8,128)(2,1)S(1)} collective-permute-done((bf16[128,512]{1,0:T(8,128)(2,1)S(1)}, bf16[128,512]{1,0:T(8,128)(2,1)S(1)}, u32[]{:S(2)}, u32[]{:S(2)}) %collective-permute-start.41) | collective-permute-done | bytes 131104 | tf_op jit(solution)/shard_map/ppermute | solution.py:487
  180.7 1.7 collective-permute-start.45
  182.4 5.6 %backward.7 = (bf16[512,3328]{1,0:T(8,128)(2,1)}, bf16[512,3328]{1,0:T(8,128)(2,1)}) custom-call(bf16[4,2,64,1024]{3,2,1,0:T(8,128)(2,1)} %bitcast.140, bf16[6,2,64,1024]{3,2,1,0:T(8,128)(2,1)} %bitcast.89.refs_1_, bf16[6,2,64,1024]{3,2,1,0:T(8,128)(2,1)} %bitcast.93.refs_2_, ...), custom_call_target="tpu_custom_call", output_to_operand_aliasing={{0}: (4, {}), {1}: (5, {})} | custom-call | flops 644245120 | bytes 3774873 | tf_op jit(solution)/shard_map/backward/pallas_call | solution.py:200
  (177 shorter events, 41.7 us)
Async XLA Ops:
  0.6 28.5 %collective-permute-start.1 = (bf16[512,3328]{1,0:T(8,128)(2,1)}, bf16[512,3328]{1,0:T(8,128)(2,1)S(1)}, u32[]{:S(2)}, u32[]{:S(2)}) collective-permute-start(bf16[512,3328]{1,0:T(8,128)(2,1)} %refs_6_.3), channel_id=1, source_target_pairs={{0,1},{1,0},{2,3},{3,2},{4,5},{5,4},{6,7},{7,6},{8,9},{9,8},{10,11... | collective-permute-start | bytes 10223624 | tf_op jit(solution)/shard_map/ppermute | solution.py:42
  0.7 28.4 %collective-permute-start.2 = (bf16[512,3328]{1,0:T(8,128)(2,1)}, bf16[512,3328]{1,0:T(8,128)(2,1)}, u32[]{:S(2)}, u32[]{:S(2)}) collective-permute-start(bf16[512,3328]{1,0:T(8,128)(2,1)} %refs_10_.1), channel_id=1, source_target_pairs={{0,1},{1,0},{2,3},{3,2},{4,5},{5,4},{6,7},{7,6},{8,9},{9,8},{10,11... | collective-permute-start | bytes 10223624 | tf_op jit(solution)/shard_map/ppermute | solution.py:42
  33.0 9.1 %collective-permute-start.3 = (bf16[2,2,64,768]{3,2,1,0:T(8,128)(2,1)S(1)}, bf16[2,2,64,768]{3,2,1,0:T(8,128)(2,1)S(1)}, u32[]{:S(2)}, u32[]{:S(2)}) collective-permute-start(bf16[2,2,64,768]{3,2,1,0:T(8,128)(2,1)S(1)} %get-tuple-element.123), channel_id=1, source_target_pairs={{0,4},{1,13},{2,6},{3,15},{4,8},{5,1},{6,10},{7,3},{8,12},{9,5},{1... | collective-permute-start | bytes 1179656 | tf_op jit(solution)/shard_map/ppermute | solution.py:34
  38.4 11.0 %collective-permute-start.6 = (bf16[2,2,64,768]{3,2,1,0:T(8,128)(2,1)S(1)}, bf16[2,2,64,768]{3,2,1,0:T(8,128)(2,1)S(1)}, u32[]{:S(2)}, u32[]{:S(2)}) collective-permute-start(bf16[2,2,64,768]{3,2,1,0:T(8,128)(2,1)S(1)} %get-tuple-element.134), channel_id=1, source_target_pairs={{0,4},{1,13},{2,6},{3,15},{4,8},{5,1},{6,10},{7,3},{8,12},{9,5},{1... | collective-permute-start | bytes 1179656 | tf_op jit(solution)/shard_map/ppermute | solution.py:34
  42.2 14.8 %collective-permute-start.5 = (bf16[2,2,2,64,768]{4,3,2,1,0:T(8,128)(2,1)S(1)}, bf16[2,2,2,64,768]{4,3,2,1,0:T(8,128)(2,1)S(1)}, u32[]{:S(2)}, u32[]{:S(2)}) collective-permute-start(bf16[2,2,2,64,768]{4,3,2,1,0:T(8,128)(2,1)S(1)} %pad_maximum_fusion.6), channel_id=1, source_target_pairs={{0,4},{1,13},{2,6},{3,15},{4,8},{5,1},{6,10},{7,3},{8,12},{9,5},{1... | collective-permute-start | bytes 2359304 | tf_op jit(solution)/shard_map/ppermute | solution.py:34
  46.4 21.8 %collective-permute-start.4 = (bf16[4,2,64,768]{3,2,1,0:T(8,128)(2,1)S(1)}, bf16[4,2,64,768]{3,2,1,0:T(8,128)(2,1)S(1)}, u32[]{:S(2)}, u32[]{:S(2)}) collective-permute-start(bf16[4,2,64,768]{3,2,1,0:T(8,128)(2,1)S(1)} %get-tuple-element.133), channel_id=1, source_target_pairs={{0,2},{1,3},{2,0},{3,1},{4,6},{5,7},{6,4},{7,5},{8,10},{9,11},{10,... | collective-permute-start | bytes 2359304 | tf_op jit(solution)/shard_map/ppermute | solution.py:38
  49.6 19.0 %collective-permute-start.9 = (bf16[2,2,2,64,768]{4,3,2,1,0:T(8,128)(2,1)S(1)}, bf16[2,2,2,64,768]{4,3,2,1,0:T(8,128)(2,1)S(1)}, u32[]{:S(2)}, u32[]{:S(2)}) collective-permute-start(bf16[2,2,2,64,768]{4,3,2,1,0:T(8,128)(2,1)S(1)} %pad_maximum_fusion.7), channel_id=1, source_target_pairs={{0,4},{1,13},{2,6},{3,15},{4,8},{5,1},{6,10},{7,3},{8,12},{9,5},{1... | collective-permute-start | bytes 2359304 | tf_op jit(solution)/shard_map/ppermute | solution.py:34
  55.8 18.0 %collective-permute-start.12 = (bf16[2,2,64,1024]{3,2,1,0:T(8,128)(2,1)S(1)}, bf16[2,2,64,1024]{3,2,1,0:T(8,128)(2,1)S(1)}, u32[]{:S(2)}, u32[]{:S(2)}) collective-permute-start(bf16[2,2,64,1024]{3,2,1,0:T(8,128)(2,1)S(1)} %get-tuple-element.151), channel_id=1, source_target_pairs={{0,4},{1,13},{2,6},{3,15},{4,8},{5,1},{6,10},{7,3},{8,12},{9,5},{1... | collective-permute-start | bytes 1572872 | tf_op jit(solution)/shard_map/ppermute | solution.py:34
  57.1 13.3 %collective-permute-start.8 = (bf16[2,2,64,768]{3,2,1,0:T(8,128)(2,1)S(1)}, bf16[2,2,64,768]{3,2,1,0:T(8,128)(2,1)S(1)}, u32[]{:S(2)}, u32[]{:S(2)}) collective-permute-start(bf16[2,2,64,768]{3,2,1,0:T(8,128)(2,1)S(1)} %slice_bitcast_fusion.10), channel_id=1, source_target_pairs={{0,1},{1,0},{2,3},{3,2},{4,5},{5,4},{6,7},{7,6},{8,9},{9,8},{10,11... | collective-permute-start | bytes 1179656 | tf_op jit(solution)/shard_map/ppermute | solution.py:42
  68.4 14.4 %collective-permute-start.7 = (bf16[2,64,768]{2,1,0:T(8,128)(2,1)S(1)}, bf16[2,64,768]{2,1,0:T(8,128)(2,1)S(1)}, u32[]{:S(2)}, u32[]{:S(2)}) collective-permute-start(bf16[2,64,768]{2,1,0:T(8,128)(2,1)S(1)} %get-tuple-element.245), channel_id=1, source_target_pairs={{0,4},{1,13},{2,6},{3,15},{4,8},{5,1},{6,10},{7,3},{8,12},{9,5},{1... | collective-permute-start | bytes 589832 | tf_op jit(solution)/shard_map/ppermute | solution.py:34
  70.6 8.8 %collective-permute-start.10 = (bf16[2,64,768]{2,1,0:T(8,128)(2,1)S(1)}, bf16[2,64,768]{2,1,0:T(8,128)(2,1)S(1)}, u32[]{:S(2)}, u32[]{:S(2)}) collective-permute-start(bf16[2,64,768]{2,1,0:T(8,128)(2,1)S(1)} %fusion.8), channel_id=1, source_target_pairs={{0,2},{1,3},{2,0},{3,1},{4,6},{5,7},{6,4},{7,5},{8,10},{9,11},{10,... | collective-permute-start | bytes 589832 | tf_op jit(solution)/shard_map/ppermute | solution.py:38
  74.1 16.1 %collective-permute-start.16 = (bf16[2,2,2,64,1024]{4,3,2,1,0:T(8,128)(2,1)S(1)}, bf16[2,2,2,64,1024]{4,3,2,1,0:T(8,128)(2,1)S(1)}, u32[]{:S(2)}, u32[]{:S(2)}) collective-permute-start(bf16[2,2,2,64,1024]{4,3,2,1,0:T(8,128)(2,1)S(1)} %pad_maximum_fusion.4), channel_id=1, source_target_pairs={{0,4},{1,13},{2,6},{3,15},{4,8},{5,1},{6,10},{7,3},{8,12},{9,5},{1... | collective-permute-start | bytes 3145736 | tf_op jit(solution)/shard_map/ppermute | solution.py:34
  76.0 13.7 %collective-permute-start.17 = (bf16[2,64,768]{2,1,0:T(8,128)(2,1)S(1)}, bf16[2,64,768]{2,1,0:T(8,128)(2,1)S(1)}, u32[]{:S(2)}, u32[]{:S(2)}) collective-permute-start(bf16[2,64,768]{2,1,0:T(8,128)(2,1)S(1)} %fusion.9), channel_id=1, source_target_pairs={{0,2},{1,3},{2,0},{3,1},{4,6},{5,7},{6,4},{7,5},{8,10},{9,11},{10,... | collective-permute-start | bytes 589832 | tf_op jit(solution)/shard_map/ppermute | solution.py:38
  79.5 9.9 %collective-permute-start.14 = (bf16[2,64,768]{2,1,0:T(8,128)(2,1)S(1)}, bf16[2,64,768]{2,1,0:T(8,128)(2,1)S(1)}, u32[]{:S(2)}, u32[]{:S(2)}) collective-permute-start(bf16[2,64,768]{2,1,0:T(8,128)(2,1)S(1)} %get-tuple-element.165), channel_id=1, source_target_pairs={{0,2},{1,3},{2,0},{3,1},{4,6},{5,7},{6,4},{7,5},{8,10},{9,11},{10,... | collective-permute-start | bytes 589832 | tf_op jit(solution)/shard_map/ppermute | solution.py:38
  82.9 11.5 %collective-permute-start.13 = (bf16[2,2,64,768]{3,2,1,0:T(8,128)(2,1)S(1)}, bf16[2,2,64,768]{3,2,1,0:T(8,128)(2,1)S(1)}, u32[]{:S(2)}, u32[]{:S(2)}) collective-permute-start(bf16[2,2,64,768]{3,2,1,0:T(8,128)(2,1)S(1)} %pad_maximum_fusion.12), channel_id=1, source_target_pairs={{0,4},{1,13},{2,6},{3,15},{4,8},{5,1},{6,10},{7,3},{8,12},{9,5},{1... | collective-permute-start | bytes 1179656 | tf_op jit(solution)/shard_map/ppermute | solution.py:34
  90.4 14.9 %collective-permute-start.25 = (bf16[2,64,768]{2,1,0:T(8,128)(2,1)S(1)}, bf16[2,64,768]{2,1,0:T(8,128)(2,1)S(1)}, u32[]{:S(2)}, u32[]{:S(2)}) collective-permute-start(bf16[2,64,768]{2,1,0:T(8,128)(2,1)S(1)} %get-tuple-element.192), channel_id=1, source_target_pairs={{0,2},{1,3},{2,0},{3,1},{4,6},{5,7},{6,4},{7,5},{8,10},{9,11},{10,... | collective-permute-start | bytes 589832 | tf_op jit(solution)/shard_map/ppermute | solution.py:38
  92.0 13.4 %collective-permute-start.24 = (bf16[2,2,2,64,768]{4,3,2,1,0:T(8,128)(2,1)S(1)}, bf16[2,2,2,64,768]{4,3,2,1,0:T(8,128)(2,1)S(1)}, u32[]{:S(2)}, u32[]{:S(2)}) collective-permute-start(bf16[2,2,2,64,768]{4,3,2,1,0:T(8,128)(2,1)S(1)} %pad_maximum_fusion.8), channel_id=1, source_target_pairs={{0,4},{1,13},{2,6},{3,15},{4,8},{5,1},{6,10},{7,3},{8,12},{9,5},{1... | collective-permute-start | bytes 2359304 | tf_op jit(solution)/shard_map/ppermute | solution.py:34
  95.1 9.9 %collective-permute-start.20 = (bf16[2,64,1024]{2,1,0:T(8,128)(2,1)S(1)}, bf16[2,64,1024]{2,1,0:T(8,128)(2,1)S(1)}, u32[]{:S(2)}, u32[]{:S(2)}) collective-permute-start(bf16[2,64,1024]{2,1,0:T(8,128)(2,1)S(1)} %fusion.6), channel_id=1, source_target_pairs={{0,2},{1,3},{2,0},{3,1},{4,6},{5,7},{6,4},{7,5},{8,10},{9,11},{10,... | collective-permute-start | bytes 786440 | tf_op jit(solution)/shard_map/ppermute | solution.py:38
  98.1 11.4 %collective-permute-start.23 = (bf16[2,2,64,768]{3,2,1,0:T(8,128)(2,1)S(1)}, bf16[2,2,64,768]{3,2,1,0:T(8,128)(2,1)S(1)}, u32[]{:S(2)}, u32[]{:S(2)}) collective-permute-start(bf16[2,2,64,768]{3,2,1,0:T(8,128)(2,1)S(1)} %pad_maximum_fusion.14), channel_id=1, source_target_pairs={{0,4},{1,13},{2,6},{3,15},{4,8},{5,1},{6,10},{7,3},{8,12},{9,5},{1... | collective-permute-start | bytes 1179656 | tf_op jit(solution)/shard_map/ppermute | solution.py:34
  105.4 9.1 %collective-permute-start.28 = (bf16[2,2,64,768]{3,2,1,0:T(8,128)(2,1)S(1)}, bf16[2,2,64,768]{3,2,1,0:T(8,128)(2,1)S(1)}, u32[]{:S(2)}, u32[]{:S(2)}) collective-permute-start(bf16[2,2,64,768]{3,2,1,0:T(8,128)(2,1)S(1)} %slice_bitcast_fusion.8), channel_id=1, source_target_pairs={{0,4},{1,13},{2,6},{3,15},{4,8},{5,1},{6,10},{7,3},{8,12},{9,5},{1... | collective-permute-start | bytes 1179656 | tf_op jit(solution)/shard_map/ppermute | solution.py:34
  106.9 9.8 %collective-permute-start.22 = (bf16[2,64,1024]{2,1,0:T(8,128)(2,1)S(1)}, bf16[2,64,1024]{2,1,0:T(8,128)(2,1)S(1)}, u32[]{:S(2)}, u32[]{:S(2)}) collective-permute-start(bf16[2,64,1024]{2,1,0:T(8,128)(2,1)S(1)} %get-tuple-element.203), channel_id=1, source_target_pairs={{0,2},{1,3},{2,0},{3,1},{4,6},{5,7},{6,4},{7,5},{8,10},{9,11},{10,... | collective-permute-start | bytes 786440 | tf_op jit(solution)/shard_map/ppermute | solution.py:38
  116.9 13.3 %collective-permute-start.32 = (bf16[2,2,2,64,768]{4,3,2,1,0:T(8,128)(2,1)S(1)}, bf16[2,2,2,64,768]{4,3,2,1,0:T(8,128)(2,1)S(1)}, u32[]{:S(2)}, u32[]{:S(2)}) collective-permute-start(bf16[2,2,2,64,768]{4,3,2,1,0:T(8,128)(2,1)S(1)} %pad_maximum_fusion.9), channel_id=1, source_target_pairs={{0,4},{1,13},{2,6},{3,15},{4,8},{5,1},{6,10},{7,3},{8,12},{9,5},{1... | collective-permute-start | bytes 2359304 | tf_op jit(solution)/shard_map/ppermute | solution.py:34
  118.9 24.0 %collective-permute-start.30 = (bf16[2,2,2,64,1024]{4,3,2,1,0:T(8,128)(2,1)S(1)}, bf16[2,2,2,64,1024]{4,3,2,1,0:T(8,128)(2,1)S(1)}, u32[]{:S(2)}, u32[]{:S(2)}) collective-permute-start(bf16[2,2,2,64,1024]{4,3,2,1,0:T(8,128)(2,1)S(1)} %pad_maximum_fusion.5), channel_id=1, source_target_pairs={{0,4},{1,13},{2,6},{3,15},{4,8},{5,1},{6,10},{7,3},{8,12},{9,5},{1... | collective-permute-start | bytes 3145736 | tf_op jit(solution)/shard_map/ppermute | solution.py:34
  120.3 21.7 %collective-permute-start.31 = (bf16[4,2,64,768]{3,2,1,0:T(8,128)(2,1)S(1)}, bf16[4,2,64,768]{3,2,1,0:T(8,128)(2,1)S(1)}, u32[]{:S(2)}, u32[]{:S(2)}) collective-permute-start(bf16[4,2,64,768]{3,2,1,0:T(8,128)(2,1)S(1)} %pad_maximum_fusion.10.refs_0_), channel_id=1, source_target_pairs={{0,2},{1,3},{2,0},{3,1},{4,6},{5,7},{6,4},{7,5},{8,10},{9,11},{10,... | collective-permute-start | bytes 2359304 | tf_op jit(solution)/shard_map/ppermute | solution.py:38
  130.2 15.4 %collective-permute-start.35 = (bf16[2,2,64,768]{3,2,1,0:T(8,128)(2,1)S(1)}, bf16[2,2,64,768]{3,2,1,0:T(8,128)(2,1)S(1)}, u32[]{:S(2)}, u32[]{:S(2)}) collective-permute-start(bf16[2,2,64,768]{3,2,1,0:T(8,128)(2,1)S(1)} %slice_bitcast_fusion.7), channel_id=1, source_target_pairs={{0,4},{1,13},{2,6},{3,15},{4,8},{5,1},{6,10},{7,3},{8,12},{9,5},{1... | collective-permute-start | bytes 1179656 | tf_op jit(solution)/shard_map/ppermute | solution.py:34
  145.8 10.7 %collective-permute-start.34 = (bf16[2,2,64,1024]{3,2,1,0:T(8,128)(2,1)S(1)}, bf16[2,2,64,1024]{3,2,1,0:T(8,128)(2,1)S(1)}, u32[]{:S(2)}, u32[]{:S(2)}) collective-permute-start(bf16[2,2,64,1024]{3,2,1,0:T(8,128)(2,1)S(1)} %slice_bitcast_fusion.1), channel_id=1, source_target_pairs={{0,4},{1,13},{2,6},{3,15},{4,8},{5,1},{6,10},{7,3},{8,12},{9,5},{1... | collective-permute-start | bytes 1572872 | tf_op jit(solution)/shard_map/ppermute | solution.py:34
  169.4 8.9 %collective-permute-start.40 = (bf16[128,512]{1,0:T(8,128)(2,1)S(1)}, bf16[128,512]{1,0:T(8,128)(2,1)S(1)}, u32[]{:S(2)}, u32[]{:S(2)}) collective-permute-start(bf16[128,512]{1,0:T(8,128)(2,1)S(1)} %get-tuple-element.228), channel_id=1, source_target_pairs={{0,96},{16,112},{32,64},{48,80},{64,32},{80,48},{96,0},{112,16},{1... | collective-permute-start | bytes 393224 | tf_op jit(solution)/shard_map/ppermute | solution.py:487
  170.0 10.7 %collective-permute-start.41 = (bf16[128,512]{1,0:T(8,128)(2,1)S(1)}, bf16[128,512]{1,0:T(8,128)(2,1)S(1)}, u32[]{:S(2)}, u32[]{:S(2)}) collective-permute-start(bf16[128,512]{1,0:T(8,128)(2,1)S(1)} %get-tuple-element.229), channel_id=1, source_target_pairs={{0,32},{16,48},{32,0},{48,16},{64,96},{80,112},{96,64},{112,80},{1... | collective-permute-start | bytes 393224 | tf_op jit(solution)/shard_map/ppermute | solution.py:487
  172.5 15.6 %collective-permute-start.39 = (bf16[128,512]{1,0:T(8,128)(2,1)S(1)}, bf16[128,512]{1,0:T(8,128)(2,1)S(1)}, u32[]{:S(2)}, u32[]{:S(2)}) collective-permute-start(bf16[128,512]{1,0:T(8,128)(2,1)S(1)} %get-tuple-element.227), channel_id=1, source_target_pairs={{0,16},{16,32},{32,48},{48,0},{64,80},{80,96},{96,112},{112,64},{1... | collective-permute-start | bytes 393224 | tf_op jit(solution)/shard_map/ppermute | solution.py:487
  173.3 14.8 %collective-permute-start.42 = (bf16[128,512]{1,0:T(8,128)(2,1)S(1)}, bf16[128,512]{1,0:T(8,128)(2,1)S(1)}, u32[]{:S(2)}, u32[]{:S(2)}) collective-permute-start(bf16[128,512]{1,0:T(8,128)(2,1)S(1)} %get-tuple-element.231), channel_id=1, source_target_pairs={{0,48},{16,0},{32,16},{48,32},{64,112},{80,64},{96,80},{112,96},{1... | collective-permute-start | bytes 393224 | tf_op jit(solution)/shard_map/ppermute | solution.py:487
  175.7 12.4 %collective-permute-start.43 = (bf16[128,512]{1,0:T(8,128)(2,1)S(1)}, bf16[128,512]{1,0:T(8,128)(2,1)S(1)}, u32[]{:S(2)}, u32[]{:S(2)}) collective-permute-start(bf16[128,512]{1,0:T(8,128)(2,1)S(1)} %get-tuple-element.232), channel_id=1, source_target_pairs={{0,64},{16,80},{32,96},{48,112},{64,0},{80,16},{96,32},{112,48},{1... | collective-permute-start | bytes 393224 | tf_op jit(solution)/shard_map/ppermute | solution.py:487
  178.3 9.8 %collective-permute-start.44 = (bf16[128,512]{1,0:T(8,128)(2,1)S(1)}, bf16[128,512]{1,0:T(8,128)(2,1)S(1)}, u32[]{:S(2)}, u32[]{:S(2)}) collective-permute-start(bf16[128,512]{1,0:T(8,128)(2,1)S(1)} %get-tuple-element.233), channel_id=1, source_target_pairs={{0,80},{16,96},{32,112},{48,64},{64,16},{80,32},{96,48},{112,0},{1... | collective-permute-start | bytes 393224 | tf_op jit(solution)/shard_map/ppermute | solution.py:487
  (29 other events, 163.1 us)
